TPU v7x, 1024 devices: a whole 8x8x8 slice. The times are simulated.
1024 devices in a mesh: owner: 64 (over z, x), red: 8 (over y), rep: 2 (over core).
Axes of the slice: x: 8, y: 8, z: 8, core: 2. Of those that a mesh axis runs over, the one named last changes fastest.
Arguments:
- amps: bfloat16 [1024, 16384], P('owner', ('red', 'rep')), may hold values from -6 to 6
- integrals: bfloat16 [16384, 65536], P(('red', 'rep'), 'owner'), may hold values from -0.15625 to 0.15625
- shape: int32 [128, 512], P(('red', 'rep'), 'owner'), may hold values from 0 to 1, as said below
Outputs:
- residual: bfloat16 [1024, 65536], P(('red', 'rep'), 'owner')
Inputs may be any that keep to these rules, and one draw needn't show every extreme that they name: shape[q, p] is 1 where amplitude tile q and residual tile p are coupled, else 0; the integral blocks are given dense and the bitmap selects which enter.
All inputs are finite; a program needn't handle non-finite values.
Results may differ from a plain program's by a relative error of at most 0.018.
Values may be sent and summed in bfloat16 or wider, within the bound.
No kernel may reach another device: no remote copies, remote signals or barrier semaphores. Data moves between devices by JAX's collectives and lax.ppermute only.
A program may use at most 32 MiB of HBM per device.

v0:
```python
import jax
import jax.numpy as jnp
from jax import lax
from jax.sharding import PartitionSpec as P


def per_device(amps, integrals, shape):
    row_count, col_count = integrals.shape
    amp_tiles = shape.shape[0]
    res_tiles = shape.shape[1]
    tile_cols = row_count // amp_tiles
    block_bits = shape.astype(jnp.bfloat16)
    masked = (
        integrals.reshape(amp_tiles, tile_cols, res_tiles, tile_cols) * block_bits[:, None, :, None]
    ).reshape(row_count, col_count)
    gathered = lax.all_gather(amps, "owner", axis=0, tiled=True)
    partial_sums = jnp.dot(gathered, masked, preferred_element_type=jnp.float32)
    summed = lax.psum_scatter(
        partial_sums.astype(jnp.bfloat16), ("red", "rep"), scatter_dimension=0, tiled=True
    )
    return summed


def solution(mesh):
    return jax.shard_map(
        per_device,
        mesh=mesh,
        in_specs=(
            P("owner", ("red", "rep")),
            P(("red", "rep"), "owner"),
            P(("red", "rep"), "owner"),
        ),
        out_specs=P(("red", "rep"), "owner"),
        check_vma=False,
    )
```

profile of v0, /device:TPU:1, one launch (start us, length us, event | category | flops | bytes accessed | tf_op | source)
XLA Modules:
  0.0 190.3 jit_solution(2971946308636403214)
XLA Ops:
  6.5 0.0 all-gather.2.cloned.1.call-start
  6.5 0.7 all-gather.2.cloned.1.call-update
  7.3 0.0 reduce-scatter.4.cloned.1.call-start
  7.3 0.7 convert_element_type.9
  8.0 102.7 %all-gather.2.cloned.1.call-done = bf16[1024,1024]{1,0:T(8,128)(2,1)} async-done(((bf16[16,1024]{1,0:T(8,128)(2,1)}), bf16[1024,1024]{1,0:T(8,128)(2,1)}) %all-gather.2.cloned.1.call-update) | async-done | bytes 2097168 | tf_op jit(solution)/shard_map/all_gather | solution.py:16
  110.7 0.0 copy-start
  110.7 0.3 mul.11
  111.0 1.2 copy-done
  112.3 4.0 %convert_bitcast_fusion = bf16[1024,1024]{0,1:T(8,128)(2,1)S(1)} fusion(bf16[1024,1024]{1,0:T(8,128)(2,1)} %all-gather.2.cloned.1.call-done, bf16[1024,1024]{1,0:T(8,128)(2,1)S(1)} %copy-done, bf16[128,8,8,128]{3,2,1,0:T(8,128)(2,1)S(1)} %bitcast.11), kind=kOutput, calls=%fused_computation.3 | convolution fusion | flops 2149580800 | bytes 8388608 | tf_op jit(solution)/shard_map/dot_general | solution.py:17
  116.3 2.6 %copy.6 = bf16[1024,1024]{1,0:T(8,128)(2,1)} copy(bf16[1024,1024]{0,1:T(8,128)(2,1)S(1)} %convert_bitcast_fusion) | data formatting | bytes 4194304
  118.8 0.0 reduce-scatter.4.cloned.1.call-update
  118.9 64.6 %reduce-scatter.4.cloned.1.call-done = bf16[64,1024]{1,0:T(8,128)(2,1)} async-done(((bf16[1024,1024]{1,0:T(8,128)(2,1)}), bf16[64,1024]{1,0:T(8,128)(2,1)}) %reduce-scatter.4.cloned.1.call-update) | async-done | bytes 131088 | tf_op jit(solution)/shard_map/reduce_scatter | solution.py:18
Async XLA Ops:
  6.5 104.1 %all-gather.2.cloned.1.call-start = ((), (), s32[]{:S(2)}) async-start(), calls=%async_computation.1 | async-start | bytes 2129920 | tf_op jit(solution)/shard_map/all_gather | solution.py:16
  7.3 176.2 %reduce-scatter.4.cloned.1.call-start = ((), (), s32[]{:S(2)}) async-start(), calls=%async_computation.2 | async-start | bytes 2228224 | tf_op jit(solution)/shard_map/reduce_scatter | solution.py:18
  110.7 1.6 copy-start
Sparse Core Ops, SparseCore 0:
  11.6 99.0 all-gather.1
  119.0 64.4 reduce-scatter.3
where the time goes:
time: 191 us; the launch traced here: 190 us
  waiting for transfers between devices  168 us (88%)
  between operations  13.4 us (7%)
  local copies, waits for them, and re-layouts  4.15 us (2%)
  matrix products  3.99 us (2%)
    all_gather x1, waiting for transfers between devices, per_device(): gathered = lax.all_gather(amps, 'owner', axis=0, tiled=True)  103 us
    reduce_scatter x1, waiting for transfers between devices, per_device(): lax.psum_scatter(partial_sums.astype(jnp.bfloat16), ('red', 'rep'), scatt...  64.6 us
    dot_general x1, matrix products, per_device(): partial_sums = jnp.dot(gathered, masked, preferred_element_type=jnp.float32)  3.99 us
  transfers between devices with their start and end apart: 2, of which 2 were waited for; matrix products, arithmetic and copies ran while one was open for 0% of the time, Pallas kernels for 0%

commit v1 on v0

v1 whole, which is shorter than its diff:
```python
import functools

import jax
import jax.numpy as jnp
from jax import lax
from jax.experimental import pallas as pl
from jax.experimental.pallas import tpu as pltpu
from jax.sharding import PartitionSpec as P

TILE = 128
SIDE = 8
ROWS = 16


def line_groups(first_phase):
    along_x, along_z = (0, 1) if first_phase else (1, 0)
    groups = [[(z * SIDE + x) * 2 + along_x for x in range(SIDE)] for z in range(SIDE)]
    groups += [[(z * SIDE + x) * 2 + along_z for z in range(SIDE)] for x in range(SIDE)]
    return groups


def spread(block, groups):
    copies = jnp.broadcast_to(block[None], (SIDE,) + block.shape)
    return lax.all_to_all(copies, ("owner", "rep"), 0, 0, axis_index_groups=groups, tiled=True)


def masked_dot_kernel(other, rep_ref, bits_ref, amps_ref, ints_ref, out_ref, masked_ref):
    step = pl.program_id(0)
    col_tiles = ints_ref.shape[1] // TILE
    for q in range(ints_ref.shape[0] // TILE):
        for p in range(col_tiles):
            here = (slice(q * TILE, (q + 1) * TILE), slice(p * TILE, (p + 1) * TILE))
            bit = bits_ref[q, step * col_tiles + p].astype(jnp.float32)
            masked_ref[here] = ints_ref[here] * bit.astype(ints_ref.dtype)
    rep = rep_ref[0]
    half = SIDE // 2
    depth = amps_ref.shape[-1]

    @pl.when(rep == 0)
    def _():
        low = half if other else 0
        rows = amps_ref[:, low : low + half].reshape(SIDE * half * ROWS, depth)
        total = jnp.dot(rows, masked_ref[...], preferred_element_type=jnp.float32)
        out_ref[...] = total.astype(out_ref.dtype).reshape(out_ref.shape)

    @pl.when(rep == 1)
    def _():
        low = 0 if other else half
        rows = amps_ref[low : low + half].reshape(half * SIDE * ROWS, depth)
        total = jnp.dot(rows, masked_ref[...], preferred_element_type=jnp.float32)
        total = total.astype(out_ref.dtype).reshape((half, SIDE, ROWS, total.shape[-1]))
        for x in range(half):
            out_ref[:, x] = total[x]


def masked_dot(other, rep, bits, gathered, ints):
    depth, cols = ints.shape
    width = 256
    half = SIDE // 2
    return pl.pallas_call(
        functools.partial(masked_dot_kernel, other),
        grid=(cols // width,),
        in_specs=[
            pl.BlockSpec(memory_space=pltpu.SMEM),
            pl.BlockSpec(memory_space=pltpu.SMEM),
            pl.BlockSpec(gathered.shape, lambda i: (0, 0, 0, 0)),
            pl.BlockSpec((depth, width), lambda i: (0, i)),
        ],
        out_specs=pl.BlockSpec((SIDE, half, ROWS, width), lambda i: (0, 0, 0, i)),
        out_shape=jax.ShapeDtypeStruct((SIDE, half, ROWS, cols), jnp.bfloat16),
        scratch_shapes=[pltpu.VMEM((depth, width), jnp.bfloat16)],
        compiler_params=pltpu.CompilerParams(vmem_limit_bytes=32 * 1024 * 1024),
        cost_estimate=pl.CostEstimate(
            flops=SIDE * half * ROWS * depth * cols * 2, bytes_accessed=5 * 1024 * 1024, transcendentals=0
        ),
    )(rep, bits, gathered, ints)


def per_device(amps, ints, bits):
    rep = lax.axis_index("rep").astype(jnp.int32).reshape(1)
    line = spread(amps, line_groups(True))
    plane = spread(line, line_groups(False))
    plane = plane.reshape(SIDE, SIDE, ROWS, amps.shape[1])
    away = masked_dot(True, rep, bits, plane, ints)
    arrived = lax.ppermute(away, "rep", [(0, 1), (1, 0)])
    kept = masked_dot(False, rep, bits, plane, ints)
    both = (kept.astype(jnp.float32) + arrived.astype(jnp.float32)).astype(jnp.bfloat16)
    shares = lax.all_to_all(both.reshape(SIDE, -1, ints.shape[1]), "red", 0, 0, tiled=True)
    return jnp.sum(shares.astype(jnp.float32), axis=0).astype(jnp.bfloat16)


def solution(mesh):
    return jax.shard_map(
        per_device,
        mesh=mesh,
        in_specs=(
            P("owner", ("red", "rep")),
            P(("red", "rep"), "owner"),
            P(("red", "rep"), "owner"),
        ),
        out_specs=P(("red", "rep"), "owner"),
        check_vma=False,
    )
```

time: 191 us -> 116 us (0.61)
  waiting for transfers between devices: 168 us -> 29.4 us
  blocking collectives: 0 us -> 62.9 us
  between operations: 13.4 us -> 0.05 us
  starting transfers between devices: 0.04 us -> 11.5 us
  Pallas kernels: 0 us -> 6.38 us
  matrix products: 3.99 us -> 0 us
    all_gather x1 -> x0, waiting for transfers between devices: 103 us -> none  [per_device(): gathered = lax.all_gather(amps, 'owner', axis=0, tiled=True)]
    reduce_scatter x1 -> x0, waiting for transfers between devices: 64.6 us -> none  [per_device(): lax.psum_scatter(partial_sums.astype(jnp.bfloat16), ('red', 'rep'), scatt...]
    all_to_all x0 -> x2, blocking collectives: none -> 62.9 us  [the longest x1 36.3 us: per_device(): lax.all_to_all(both.reshape(SIDE, -1, ints.shape[1]), 'red', 0, 0, tiled=...]
    all_to_all x0 -> x1, waiting for transfers between devices: none -> 29.4 us  [spread(): lax.all_to_all(copies, ('owner', 'rep'), 0, 0, axis_index_groups=groups,...]
    pallas_call x0 -> x2, Pallas kernels: none -> 6.38 us  [masked_dot(): pl.pallas_call(functools.partial(masked_dot_kernel, other), grid=(cols //...]
    all_to_all x0 -> x1, starting transfers between devices: none -> 6.33 us  [spread(): lax.all_to_all(copies, ('owner', 'rep'), 0, 0, axis_index_groups=groups,...]
    ppermute x0 -> x1, starting transfers between devices: none -> 5.18 us  [per_device(): arrived = lax.ppermute(away, 'rep', [(0, 1), (1, 0)])]
    dot_general x1 -> x0, matrix products: 3.99 us -> none  [per_device(): partial_sums = jnp.dot(gathered, masked, preferred_element_type=jnp.float32)]
  transfers between devices with their start and end apart: 2 -> 2, of which waited for: 2 -> 1; matrix products, arithmetic and copies ran while one was open for 0% -> 0% of each run, Pallas kernels for 0% -> 3%
where the time goes in v1:
time: 116 us; the launch traced here: 115 us
  blocking collectives  62.9 us (54%)
  waiting for transfers between devices  29.4 us (25%)
  starting transfers between devices  11.5 us (10%)
  Pallas kernels  6.38 us (6%)
  local copies, waits for them, and re-layouts  3.97 us (3%)
  other arithmetic  1.24 us (1%)
    all_to_all x1, blocking collectives, per_device(): lax.all_to_all(both.reshape(SIDE, -1, ints.shape[1]), 'red', 0, 0, tiled=...  36.3 us
    all_to_all x1, waiting for transfers between devices, spread(): lax.all_to_all(copies, ('owner', 'rep'), 0, 0, axis_index_groups=groups,...  29.4 us
    all_to_all x1, blocking collectives, spread(): lax.all_to_all(copies, ('owner', 'rep'), 0, 0, axis_index_groups=groups,...  26.6 us
    pallas_call x2, Pallas kernels, masked_dot(): pl.pallas_call(functools.partial(masked_dot_kernel, other), grid=(cols //...  6.38 us
    all_to_all x1, starting transfers between devices, spread(): lax.all_to_all(copies, ('owner', 'rep'), 0, 0, axis_index_groups=groups,...  6.33 us
    ppermute x1, starting transfers between devices, per_device(): arrived = lax.ppermute(away, 'rep', [(0, 1), (1, 0)])  5.18 us
    broadcast_in_dim x2, local copies, waits for them, and re-layouts, spread(): copies = jnp.broadcast_to(block[None], (SIDE,) + block.shape)  2.38 us
  transfers between devices with their start and end apart: 2, of which 1 were waited for; matrix products, arithmetic and copies ran while one was open for 0% of the time, Pallas kernels for 3%

profile of v1, /device:TPU:1, one launch (start us, length us, event | category | flops | bytes accessed | tf_op | source)
XLA Modules:
  0.0 115.5 jit_solution(14380121780817037574)
XLA Ops:
  0.0 0.8 broadcast_in_dim.4
  0.8 26.6 %all_to_all.15 = bf16[8,16,1024]{2,1,0:T(8,128)(2,1)S(1)} all-to-all(bf16[8,16,1024]{2,1,0:T(8,128)(2,1)S(1)} %broadcast_in_dim.4), channel_id=1, replica_groups={{0,16,32,48,64,80,96,112},{128,144,160,176,192,208,224,240},{256,272,28..., dimensions={0} | all-to-all | bytes 524288 | tf_op jit(solution)/shard_map/all_to_all | solution.py:24
  27.4 1.6 %broadcast_in_dim.5 = bf16[8,8,16,1024]{3,2,1,0:T(8,128)(2,1)} broadcast(bf16[8,16,1024]{2,1,0:T(8,128)(2,1)S(1)} %all_to_all.15), dimensions={1,2,3} | broadcast | bytes 2359296 | tf_op jit(solution)/shard_map/broadcast_in_dim | solution.py:23
  29.0 0.0 copy-start.1
  29.0 6.3 %all-to-all-start.1 = ((bf16[8,8,16,1024]{3,2,1,0:T(8,128)(2,1)}), bf16[8,8,16,1024]{3,2,1,0:T(8,128)(2,1)S(1)}, u32[]{:S(2)}, u32[]{:S(2)}) async-start(bf16[8,8,16,1024]{3,2,1,0:T(8,128)(2,1)} %broadcast_in_dim.5), calls=%async_computation.1 | async-start | bytes 4194304 | tf_op jit(solution)/shard_map/all_to_all | solution.py:24
  35.4 29.4 %all-to-all-done.1.amps_ref = bf16[8,8,16,1024]{3,2,1,0:T(8,128)(2,1)S(1)} async-done(((bf16[8,8,16,1024]{3,2,1,0:T(8,128)(2,1)}), bf16[8,8,16,1024]{3,2,1,0:T(8,128)(2,1)S(1)}, u32[]{:S(2)}, u32[]{:S(2)}) %all-to-all-start.1) | async-done | bytes 2097184 | tf_op jit(solution)/shard_map/all_to_all | solution.py:24
  64.7 0.0 copy-done.1
  64.7 0.0 copy-start
  64.7 1.6 %copy-done = bf16[1024,1024]{1,0:T(8,128)(2,1)S(1)} copy-done((bf16[1024,1024]{1,0:T(8,128)(2,1)S(1)}, bf16[1024,1024]{1,0:T(8,128)(2,1)}, u32[]{:S(2)}) %copy-start) | copy-done | bytes 2097176
  66.3 3.2 %shard_map.38 = bf16[8,4,16,1024]{3,2,1,0:T(8,128)(2,1)S(1)} custom-call(s32[1]{0:T(128)} %bitcast.rep_ref, s32[8,8]{1,0:T(8,128)S(1)} %copy-done.1, bf16[8,8,16,1024]{3,2,1,0:T(8,128)(2,1)S(1)} %all-to-all-done.1.amps_ref, bf16[1024,1024]{1,0:T(8,128)(2,1)S(1)} %copy-done), custom_call_target="tpu_custom_call" | custom-call | flops 1073741824 | bytes 5242880 | tf_op jit(solution)/shard_map/pallas_call | solution.py:60
  69.5 5.2 %collective-permute-start = (bf16[8,4,16,1024]{3,2,1,0:T(8,128)(2,1)S(1)}, bf16[8,4,16,1024]{3,2,1,0:T(8,128)(2,1)S(1)}, u32[]{:S(2)}, u32[]{:S(2)}) collective-permute-start(bf16[8,4,16,1024]{3,2,1,0:T(8,128)(2,1)S(1)} %shard_map.38), channel_id=1, source_target_pairs={{0,1},{1,0},{2,3},{3,2},{4,5},{5,4},{6,7},{7,6},{8,9},{9,8},{10,11... | collective-permute-start | bytes 3145736 | tf_op jit(solution)/shard_map/ppermute | solution.py:85
  74.7 3.2 %shard_map.37 = bf16[8,4,16,1024]{3,2,1,0:T(8,128)(2,1)S(1)} custom-call(s32[1]{0:T(128)} %bitcast.rep_ref, s32[8,8]{1,0:T(8,128)S(1)} %copy-done.1, bf16[8,8,16,1024]{3,2,1,0:T(8,128)(2,1)S(1)} %all-to-all-done.1.amps_ref, bf16[1024,1024]{1,0:T(8,128)(2,1)S(1)} %copy-done), custom_call_target="tpu_custom_call" | custom-call | flops 1073741824 | bytes 5242880 | tf_op jit(solution)/shard_map/pallas_call | solution.py:60
  77.9 0.0 collective-permute-done
  77.9 0.4 add_convert_fusion
  78.3 36.3 %all_to_all.16 = bf16[8,64,1024]{2,1,0:T(8,128)(2,1)S(1)} all-to-all(bf16[8,64,1024]{2,1,0:T(8,128)(2,1)S(1)} %bitcast.2), channel_id=1, replica_groups=mesh['owner'=64,'red'=8,'rep'=2] {'red'}, dimensions={0} | all-to-all | bytes 2097152 | tf_op jit(solution)/shard_map/all_to_all | solution.py:88
  114.6 0.8 reduce_sum.12
Async XLA Ops:
  29.0 35.7 %copy-start.1 = (s32[8,8]{1,0:T(8,128)S(1)}, s32[8,8]{1,0:T(8,128)}, u32[]{:S(2)}) copy-start(s32[8,8]{1,0:T(8,128)} %bits_ref.3) | copy-start | bytes 772
  29.0 35.7 %all-to-all-start.1 = ((bf16[8,8,16,1024]{3,2,1,0:T(8,128)(2,1)}), bf16[8,8,16,1024]{3,2,1,0:T(8,128)(2,1)S(1)}, u32[]{:S(2)}, u32[]{:S(2)}) async-start(bf16[8,8,16,1024]{3,2,1,0:T(8,128)(2,1)} %broadcast_in_dim.5), calls=%async_computation.1 | async-start | bytes 4194304 | tf_op jit(solution)/shard_map/all_to_all | solution.py:24
  64.7 1.6 %copy-start = (bf16[1024,1024]{1,0:T(8,128)(2,1)S(1)}, bf16[1024,1024]{1,0:T(8,128)(2,1)}, u32[]{:S(2)}) copy-start(bf16[1024,1024]{1,0:T(8,128)(2,1)} %ints_ref.3) | copy-start | bytes 6291460
  69.5 8.4 %collective-permute-start = (bf16[8,4,16,1024]{3,2,1,0:T(8,128)(2,1)S(1)}, bf16[8,4,16,1024]{3,2,1,0:T(8,128)(2,1)S(1)}, u32[]{:S(2)}, u32[]{:S(2)}) collective-permute-start(bf16[8,4,16,1024]{3,2,1,0:T(8,128)(2,1)S(1)} %shard_map.38), channel_id=1, source_target_pairs={{0,1},{1,0},{2,3},{3,2},{4,5},{5,4},{6,7},{7,6},{8,9},{9,8},{10,11... | collective-permute-start | bytes 3145736 | tf_op jit(solution)/shard_map/ppermute | solution.py:85

commit v2 on v0

v2 whole, which is shorter than its diff:
```python
import functools

import jax
import jax.numpy as jnp
from jax import lax
from jax.experimental import pallas as pl
from jax.experimental.pallas import tpu as pltpu
from jax.sharding import PartitionSpec as P

TILE = 128
SIDE = 8
HALF = SIDE // 2
ROWS = 16
VMEM = pl.BlockSpec(memory_space=pltpu.VMEM)
SMEM = pl.BlockSpec(memory_space=pltpu.SMEM)


def line_groups():
    groups = [[(z * SIDE + x) * 2 for x in range(SIDE)] for z in range(SIDE)]
    groups += [[(z * SIDE + x) * 2 + 1 for z in range(SIDE)] for x in range(SIDE)]
    return groups


def ring_step(step):
    pairs = []
    for z in range(SIDE):
        for x in range(SIDE):
            here = (z * SIDE + x) * 2
            pairs.append((here, ((z + step) % SIDE * SIDE + x) * 2))
            pairs.append((here + 1, (z * SIDE + (x + step) % SIDE) * 2 + 1))
    return pairs


def red_step(step):
    return [(y * 2 + c, (y + (step if c == 0 else -step)) % SIDE * 2 + c) for y in range(SIDE) for c in range(2)]


def mask_kernel(bits_ref, ints_ref, out_ref):
    for q in range(ints_ref.shape[0] // TILE):
        for p in range(ints_ref.shape[1] // TILE):
            here = (slice(q * TILE, (q + 1) * TILE), slice(p * TILE, (p + 1) * TILE))
            bit = bits_ref[q, p].astype(jnp.float32).astype(ints_ref.dtype)
            out_ref[here] = ints_ref[here] * bit


def mask(bits, ints):
    return pl.pallas_call(
        mask_kernel,
        in_specs=[SMEM, VMEM],
        out_specs=VMEM,
        out_shape=jax.ShapeDtypeStruct(ints.shape, ints.dtype),
        compiler_params=pltpu.CompilerParams(vmem_limit_bytes=16 * 1024 * 1024),
        cost_estimate=pl.CostEstimate(flops=ints.size, bytes_accessed=4 * ints.size, transcendentals=0),
    )(bits, ints)


def planes_kernel(steps, place_ref, *refs):
    count = len(steps)
    planes, masked_ref = refs[:count], refs[count]
    kept_ref, away_ref = refs[-2:]
    depth, cols = masked_ref.shape
    rep = place_ref[0]
    width = 256
    rows = jnp.concatenate([plane[...].reshape(SIDE * ROWS, depth) for plane in planes], axis=0)
    for start in range(0, cols, width):
        here = slice(start, start + width)
        total = jnp.dot(rows, masked_ref[:, here], preferred_element_type=jnp.float32)
        total = total.astype(kept_ref.dtype).reshape(count, SIDE, ROWS, width)
        for i in range(count):
            index = (place_ref[1] + (steps[i] + SIDE)) & (SIDE - 1)

            @pl.when(rep == 0)
            def _(i=i, index=index):
                kept_ref[index, :, :, here] = total[i, :HALF]
                away_ref[index, :, :, here] = total[i, HALF:]

            @pl.when((rep == 1) & (index < HALF))
            def _(i=i, index=index):
                away_ref[:, index, :, here] = total[i]

            @pl.when((rep == 1) & (index >= HALF))
            def _(i=i, index=index):
                kept_ref[:, index - HALF, :, here] = total[i]


def planes_dot(place, steps, planes, masked, sums):
    count = len(planes)
    depth, cols = masked.shape
    shape = jax.ShapeDtypeStruct((SIDE, HALF, ROWS, cols), jnp.bfloat16)
    operands = [place, *planes, masked, *sums]
    aliases = {2 + count + i: i for i in range(len(sums))}
    return pl.pallas_call(
        functools.partial(planes_kernel, steps),
        in_specs=[SMEM] + [VMEM] * (len(operands) - 1),
        out_specs=[VMEM, VMEM],
        out_shape=[shape, shape],
        input_output_aliases=aliases,
        compiler_params=pltpu.CompilerParams(vmem_limit_bytes=16 * 1024 * 1024),
        cost_estimate=pl.CostEstimate(
            flops=count * SIDE * ROWS * depth * cols * 2, bytes_accessed=1024 * 1024, transcendentals=0
        ),
    )(*operands)


def share_kernel(place_ref, kept_ref, arrived_ref, near_a_ref, near_b_ref, own_ref):
    y, way = place_ref[2], 1 - 2 * place_ref[0]

    def block(index):
        index = (index + SIDE) & (SIDE - 1)
        both = kept_ref[index].astype(jnp.float32) + arrived_ref[index].astype(jnp.float32)
        return both.astype(own_ref.dtype).reshape(HALF * ROWS, both.shape[-1])

    there = y + way
    near_a_ref[0] = block(there + 4)
    near_a_ref[1] = block(there - 2 * way)
    near_b_ref[0] = block(there + 2 * way)
    near_b_ref[1] = block(there)
    own_ref[0] = block(y + 4)
    own_ref[1] = block(y - 2 * way)
    own_ref[2] = block(y + 2 * way)
    own_ref[3] = block(y)


def share(place, kept, arrived):
    cols = kept.shape[-1]
    pair = jax.ShapeDtypeStruct((2, HALF * ROWS, cols), kept.dtype)
    four = jax.ShapeDtypeStruct((4, HALF * ROWS, cols), kept.dtype)
    return pl.pallas_call(
        share_kernel,
        in_specs=[SMEM, VMEM, VMEM],
        out_specs=[VMEM, VMEM, VMEM],
        out_shape=[pair, pair, four],
        compiler_params=pltpu.CompilerParams(vmem_limit_bytes=16 * 1024 * 1024),
        cost_estimate=pl.CostEstimate(flops=kept.size, bytes_accessed=6 * kept.size, transcendentals=0),
    )(place, kept, arrived)


def added(*terms):
    return sum(t.astype(jnp.float32) for t in terms).astype(jnp.bfloat16)


def per_device(amps, ints, bits):
    owner, y, rep = (lax.axis_index(name).astype(jnp.int32) for name in ("owner", "red", "rep"))
    z, x = owner >> 3, owner & (SIDE - 1)
    place = jnp.stack([rep, jnp.where(rep == 0, z, x), y])

    copies = jnp.broadcast_to(amps[None], (SIDE,) + amps.shape)
    line = lax.all_to_all(copies, ("owner", "rep"), 0, 0, axis_index_groups=line_groups(), tiled=True)
    masked = mask(bits, ints)

    sums = ()
    from_low, from_high = line, line
    sums = planes_dot(place, (0,), [line], masked, sums)
    for step in range(1, HALF):
        from_low = lax.ppermute(from_low, ("owner", "rep"), ring_step(1))
        from_high = lax.ppermute(from_high, ("owner", "rep"), ring_step(-1))
        sums = planes_dot(place, (-step, step), [from_low, from_high], masked, sums)
    from_low = lax.ppermute(from_low, ("owner", "rep"), ring_step(1))
    kept, away = planes_dot(place, (HALF,), [from_low], masked, sums)

    arrived = lax.ppermute(away, "rep", [(0, 1), (1, 0)])
    near_a, near_b, own = share(place, kept, arrived)
    axes = ("red", "rep")
    near_a = lax.ppermute(near_a, axes, red_step(1))
    near_b = lax.ppermute(near_b, axes, red_step(1))
    relay = lax.ppermute(added(own[0], near_a[0]), axes, red_step(2))
    back = lax.ppermute(added(own[1], near_a[1]), axes, red_step(-2))
    ahead = lax.ppermute(added(own[2], near_b[0], relay), axes, red_step(2))
    return added(own[3], near_b[1], back, ahead)


def solution(mesh):
    return jax.shard_map(
        per_device,
        mesh=mesh,
        in_specs=(
            P("owner", ("red", "rep")),
            P(("red", "rep"), "owner"),
            P(("red", "rep"), "owner"),
        ),
        out_specs=P(("red", "rep"), "owner"),
        check_vma=False,
    )
```

time: 191 us -> 109 us (0.57)
  the two profiles are of different devices: /device:TPU:1 before, /device:TPU:64 now
where the time goes in v2:
time: 109 us; the launch traced here: 108 us
  starting transfers between devices  52.6 us (48%)
  waiting for transfers between devices  22 us (20%)
  blocking collectives  17 us (16%)
  Pallas kernels  12.4 us (11%)
  local copies, waits for them, and re-layouts  3.05 us (3%)
    ppermute x3, starting transfers between devices, per_device(): from_high = lax.ppermute(from_high, ('owner', 'rep'), ring_step(-1))  24.4 us
    all_to_all x1, blocking collectives, per_device(): lax.all_to_all(copies, ('owner', 'rep'), 0, 0, axis_index_groups=line_gro...  17 us
    ppermute x4, starting transfers between devices, per_device(): from_low = lax.ppermute(from_low, ('owner', 'rep'), ring_step(1))  10.9 us
    pallas_call x5, Pallas kernels, planes_dot(): pl.pallas_call(functools.partial(planes_kernel, steps), in_specs=[SMEM] +...  10.5 us
    ppermute x1, waiting for transfers between devices, per_device(): ahead = lax.ppermute(added(own[2], near_b[0], relay), axes, red_step(2))  6.96 us
    ppermute x1, starting transfers between devices, per_device(): back = lax.ppermute(added(own[1], near_a[1]), axes, red_step(-2))  6.03 us
    ppermute x4, waiting for transfers between devices, per_device(): from_low = lax.ppermute(from_low, ('owner', 'rep'), ring_step(1))  4.81 us
    ppermute x1, waiting for transfers between devices, per_device(): near_a = lax.ppermute(near_a, axes, red_step(1))  4.06 us
  transfers between devices with their start and end apart: 13, of which 7 were waited for; matrix products, arithmetic and copies ran while one was open for 0% of the time, Pallas kernels for 9%

profile of v2, /device:TPU:64, one launch (start us, length us, event | category | flops | bytes accessed | tf_op | source)
XLA Modules:
  0.0 108.2 jit_solution(15894302568498328177)
XLA Ops:
  0.0 0.8 broadcast_in_dim.2
  0.8 17.0 %all_to_all.5.refs_0_ = bf16[8,16,1024]{2,1,0:T(8,128)(2,1)S(1)} all-to-all(bf16[8,16,1024]{2,1,0:T(8,128)(2,1)S(1)} %broadcast_in_dim.2), channel_id=1, replica_groups={{0,16,32,48,64,80,96,112},{128,144,160,176,192,208,224,240},{256,272,28..., dimensions={0} | all-to-all | bytes 524288 | tf_op jit(solution)/shard_map/all_to_all | solution.py:148
  17.8 5.2 %collective-permute-start = (bf16[8,16,1024]{2,1,0:T(8,128)(2,1)S(1)}, bf16[8,16,1024]{2,1,0:T(8,128)(2,1)S(1)}, u32[]{:S(2)}, u32[]{:S(2)}) collective-permute-start(bf16[8,16,1024]{2,1,0:T(8,128)(2,1)S(1)} %all_to_all.5.refs_0_), channel_id=1, source_target_pairs={{0,128},{1,17},{16,144},{17,33},{32,160},{33,49},{48,176},{49,65},... | collective-permute-start | bytes 786440 | tf_op jit(solution)/shard_map/ppermute | solution.py:155
  23.0 14.2 %collective-permute-start.4 = (bf16[8,16,1024]{2,1,0:T(8,128)(2,1)S(1)}, bf16[8,16,1024]{2,1,0:T(8,128)(2,1)S(1)}, u32[]{:S(2)}, u32[]{:S(2)}) collective-permute-start(bf16[8,16,1024]{2,1,0:T(8,128)(2,1)S(1)} %all_to_all.5.refs_0_), channel_id=1, source_target_pairs={{0,896},{1,113},{16,912},{17,1},{32,928},{33,17},{48,944},{49,33},... | collective-permute-start | bytes 786440 | tf_op jit(solution)/shard_map/ppermute | solution.py:156
  37.2 2.4 %collective-permute-done.refs_0_ = bf16[8,16,1024]{2,1,0:T(8,128)(2,1)S(1)} collective-permute-done((bf16[8,16,1024]{2,1,0:T(8,128)(2,1)S(1)}, bf16[8,16,1024]{2,1,0:T(8,128)(2,1)S(1)}, u32[]{:S(2)}, u32[]{:S(2)}) %collective-permute-start) | collective-permute-done | bytes 262176 | tf_op jit(solution)/shard_map/ppermute | solution.py:155
  39.6 1.9 %collective-permute-start.1 = (bf16[8,16,1024]{2,1,0:T(8,128)(2,1)S(1)}, bf16[8,16,1024]{2,1,0:T(8,128)(2,1)S(1)}, u32[]{:S(2)}, u32[]{:S(2)}) collective-permute-start(bf16[8,16,1024]{2,1,0:T(8,128)(2,1)S(1)} %collective-permute-done.refs_0_), channel_id=1, source_target_pairs={{0,128},{1,17},{16,144},{17,33},{32,160},{33,49},{48,176},{49,65},... | collective-permute-start | bytes 786440 | tf_op jit(solution)/shard_map/ppermute | solution.py:155
  41.5 0.0 collective-permute-done.4.refs_1_
  41.5 5.1 %collective-permute-start.5 = (bf16[8,16,1024]{2,1,0:T(8,128)(2,1)S(1)}, bf16[8,16,1024]{2,1,0:T(8,128)(2,1)S(1)}, u32[]{:S(2)}, u32[]{:S(2)}) collective-permute-start(bf16[8,16,1024]{2,1,0:T(8,128)(2,1)S(1)} %collective-permute-done.4.refs_1_), channel_id=1, source_target_pairs={{0,896},{1,113},{16,912},{17,1},{32,928},{33,17},{48,944},{49,33},... | collective-permute-start | bytes 786440 | tf_op jit(solution)/shard_map/ppermute | solution.py:156
  46.7 2.4 %collective-permute-done.1.refs_0_ = bf16[8,16,1024]{2,1,0:T(8,128)(2,1)S(1)} collective-permute-done((bf16[8,16,1024]{2,1,0:T(8,128)(2,1)S(1)}, bf16[8,16,1024]{2,1,0:T(8,128)(2,1)S(1)}, u32[]{:S(2)}, u32[]{:S(2)}) %collective-permute-start.1) | collective-permute-done | bytes 262176 | tf_op jit(solution)/shard_map/ppermute | solution.py:155
  49.1 1.9 %collective-permute-start.2 = (bf16[8,16,1024]{2,1,0:T(8,128)(2,1)S(1)}, bf16[8,16,1024]{2,1,0:T(8,128)(2,1)S(1)}, u32[]{:S(2)}, u32[]{:S(2)}) collective-permute-start(bf16[8,16,1024]{2,1,0:T(8,128)(2,1)S(1)} %collective-permute-done.1.refs_0_), channel_id=1, source_target_pairs={{0,128},{1,17},{16,144},{17,33},{32,160},{33,49},{48,176},{49,65},... | collective-permute-start | bytes 786440 | tf_op jit(solution)/shard_map/ppermute | solution.py:155
  51.0 0.0 collective-permute-done.5.refs_1_
  51.0 5.1 %collective-permute-start.6 = (bf16[8,16,1024]{2,1,0:T(8,128)(2,1)S(1)}, bf16[8,16,1024]{2,1,0:T(8,128)(2,1)S(1)}, u32[]{:S(2)}, u32[]{:S(2)}) collective-permute-start(bf16[8,16,1024]{2,1,0:T(8,128)(2,1)S(1)} %collective-permute-done.5.refs_1_), channel_id=1, source_target_pairs={{0,896},{1,113},{16,912},{17,1},{32,928},{33,17},{48,944},{49,33},... | collective-permute-start | bytes 786440 | tf_op jit(solution)/shard_map/ppermute | solution.py:156
  56.2 0.0 copy-start
  56.2 1.6 %copy-done = bf16[1024,1024]{1,0:T(8,128)(2,1)S(1)} copy-done((bf16[1024,1024]{1,0:T(8,128)(2,1)S(1)}, bf16[1024,1024]{1,0:T(8,128)(2,1)}, u32[]{:S(2)}) %copy-start) | copy-done | bytes 2097176
  57.7 0.0 copy-start.1
  57.8 0.7 copy-done.1
  58.4 1.2 %shard_map.37.refs_1_.refs_2_ = bf16[1024,1024]{1,0:T(8,128)(2,1)S(1)} custom-call(s32[8,8]{1,0:T(8,128)S(1)} %copy-done.1, bf16[1024,1024]{1,0:T(8,128)(2,1)S(1)} %copy-done), custom_call_target="tpu_custom_call" | custom-call | flops 1048576 | bytes 4194304 | tf_op jit(solution)/shard_map/pallas_call | solution.py:47
  59.6 0.0 collective-permute-done.2.refs_0_
  59.6 1.9 %collective-permute-start.3 = (bf16[8,16,1024]{2,1,0:T(8,128)(2,1)S(1)}, bf16[8,16,1024]{2,1,0:T(8,128)(2,1)S(1)}, u32[]{:S(2)}, u32[]{:S(2)}) collective-permute-start(bf16[8,16,1024]{2,1,0:T(8,128)(2,1)S(1)} %collective-permute-done.2.refs_0_), channel_id=1, source_target_pairs={{0,128},{1,17},{16,144},{17,33},{32,160},{33,49},{48,176},{49,65},... | collective-permute-start | bytes 786440 | tf_op jit(solution)/shard_map/ppermute | solution.py:158
  61.5 0.1 pad_add_fusion.place_ref
  61.6 1.7 %shard_map.38 = (bf16[8,4,16,1024]{3,2,1,0:T(8,128)(2,1)S(1)}, bf16[8,4,16,1024]{3,2,1,0:T(8,128)(2,1)S(1)}) custom-call(s32[3]{0:T(128)S(1)} %pad_add_fusion.place_ref, bf16[8,16,1024]{2,1,0:T(8,128)(2,1)S(1)} %all_to_all.5.refs_0_, bf16[1024,1024]{1,0:T(8,128)(2,1)S(1)} %shard_map.37.refs_1_.refs_2_), custom_call_target="tpu_custom_call" | custom-call | flops 268435456 | bytes 1048576 | tf_op jit(solution)/shard_map/pallas_call | solution.py:92
  63.3 2.3 %shard_map.39 = (bf16[8,4,16,1024]{3,2,1,0:T(8,128)(2,1)S(1)}, bf16[8,4,16,1024]{3,2,1,0:T(8,128)(2,1)S(1)}) custom-call(s32[3]{0:T(128)S(1)} %pad_add_fusion.place_ref, bf16[8,16,1024]{2,1,0:T(8,128)(2,1)S(1)} %collective-permute-done.refs_0_, ...), custom_call_target="tpu_custom_call", output_to_operand_aliasing={{0}: (4, {}), {1}: (5, {})} | custom-call | flops 536870912 | bytes 1048576 | tf_op jit(solution)/shard_map/pallas_call | solution.py:92
  65.7 2.3 %shard_map.40 = (bf16[8,4,16,1024]{3,2,1,0:T(8,128)(2,1)S(1)}, bf16[8,4,16,1024]{3,2,1,0:T(8,128)(2,1)S(1)}) custom-call(s32[3]{0:T(128)S(1)} %pad_add_fusion.place_ref, bf16[8,16,1024]{2,1,0:T(8,128)(2,1)S(1)} %collective-permute-done.1.refs_0_, ...), custom_call_target="tpu_custom_call", output_to_operand_aliasing={{0}: (4, {}), {1}: (5, {})} | custom-call | flops 536870912 | bytes 1048576 | tf_op jit(solution)/shard_map/pallas_call | solution.py:92
  68.1 0.0 collective-permute-done.6.refs_1_
  68.1 2.3 %shard_map.41 = (bf16[8,4,16,1024]{3,2,1,0:T(8,128)(2,1)S(1)}, bf16[8,4,16,1024]{3,2,1,0:T(8,128)(2,1)S(1)}) custom-call(s32[3]{0:T(128)S(1)} %pad_add_fusion.place_ref, bf16[8,16,1024]{2,1,0:T(8,128)(2,1)S(1)} %collective-permute-done.2.refs_0_, ...), custom_call_target="tpu_custom_call", output_to_operand_aliasing={{0}: (4, {}), {1}: (5, {})} | custom-call | flops 536870912 | bytes 1048576 | tf_op jit(solution)/shard_map/pallas_call | solution.py:92
  70.4 0.0 collective-permute-done.3.refs_0_
  70.4 1.7 %shard_map.42 = (bf16[8,4,16,1024]{3,2,1,0:T(8,128)(2,1)S(1)}, bf16[8,4,16,1024]{3,2,1,0:T(8,128)(2,1)S(1)}) custom-call(s32[3]{0:T(128)S(1)} %pad_add_fusion.place_ref, bf16[8,16,1024]{2,1,0:T(8,128)(2,1)S(1)} %collective-permute-done.3.refs_0_, bf16[1024,1024]{1,0:T(8,128)(2,1)S(1)} %shard_map.37.refs_1_.refs_2_, ...), custom_call_target="tpu_custom_call", output_to_operand_aliasing={{0}: (3, {}), {1}: (4, {})} | custom-call | flops 268435456 | bytes 1048576 | tf_op jit(solution)/shard_map/pallas_call | solution.py:92
  72.1 1.9 %collective-permute-start.7 = (bf16[8,4,16,1024]{3,2,1,0:T(8,128)(2,1)S(1)}, bf16[8,4,16,1024]{3,2,1,0:T(8,128)(2,1)S(1)}, u32[]{:S(2)}, u32[]{:S(2)}) collective-permute-start(bf16[8,4,16,1024]{3,2,1,0:T(8,128)(2,1)S(1)} %get-tuple-element.27), channel_id=1, source_target_pairs={{0,1},{1,0},{2,3},{3,2},{4,5},{5,4},{6,7},{7,6},{8,9},{9,8},{10,11... | collective-permute-start | bytes 3145736 | tf_op jit(solution)/shard_map/ppermute | solution.py:161
  74.1 2.6 %collective-permute-done.7.arrived_ref = bf16[8,4,16,1024]{3,2,1,0:T(8,128)(2,1)S(1)} collective-permute-done((bf16[8,4,16,1024]{3,2,1,0:T(8,128)(2,1)S(1)}, bf16[8,4,16,1024]{3,2,1,0:T(8,128)(2,1)S(1)}, u32[]{:S(2)}, u32[]{:S(2)}) %collective-permute-start.7) | collective-permute-done | bytes 1048608 | tf_op jit(solution)/shard_map/ppermute | solution.py:161
  76.7 0.8 shard_map.43
  77.5 2.7 %collective-permute-start.9 = (bf16[2,64,1024]{2,1,0:T(8,128)(2,1)S(1)}, bf16[2,64,1024]{2,1,0:T(8,128)(2,1)S(1)}, u32[]{:S(2)}, u32[]{:S(2)}) collective-permute-start(bf16[2,64,1024]{2,1,0:T(8,128)(2,1)S(1)} %get-tuple-element.30), channel_id=1, source_target_pairs={{0,2},{1,15},{2,4},{3,1},{4,6},{5,3},{6,8},{7,5},{8,10},{9,7},{10,... | collective-permute-start | bytes 786440 | tf_op jit(solution)/shard_map/ppermute | solution.py:164
  80.2 2.7 %collective-permute-start.8 = (bf16[2,64,1024]{2,1,0:T(8,128)(2,1)S(1)}, bf16[2,64,1024]{2,1,0:T(8,128)(2,1)S(1)}, u32[]{:S(2)}, u32[]{:S(2)}) collective-permute-start(bf16[2,64,1024]{2,1,0:T(8,128)(2,1)S(1)} %get-tuple-element.29), channel_id=1, source_target_pairs={{0,2},{1,15},{2,4},{3,1},{4,6},{5,3},{6,8},{7,5},{8,10},{9,7},{10,... | collective-permute-start | bytes 786440 | tf_op jit(solution)/shard_map/ppermute | solution.py:165
  82.9 4.1 %collective-permute-done.9 = bf16[2,64,1024]{2,1,0:T(8,128)(2,1)S(1)} collective-permute-done((bf16[2,64,1024]{2,1,0:T(8,128)(2,1)S(1)}, bf16[2,64,1024]{2,1,0:T(8,128)(2,1)S(1)}, u32[]{:S(2)}, u32[]{:S(2)}) %collective-permute-start.9) | collective-permute-done | bytes 262176 | tf_op jit(solution)/shard_map/ppermute | solution.py:164
  87.0 0.1 fusion.3
  87.0 1.9 %collective-permute-start.11 = (bf16[64,1024]{1,0:T(8,128)(2,1)S(1)}, bf16[64,1024]{1,0:T(8,128)(2,1)S(1)}, u32[]{:S(2)}, u32[]{:S(2)}) collective-permute-start(bf16[64,1024]{1,0:T(8,128)(2,1)S(1)} %get-tuple-element.32), channel_id=1, source_target_pairs={{0,4},{1,13},{2,6},{3,15},{4,8},{5,1},{6,10},{7,3},{8,12},{9,5},{1... | collective-permute-start | bytes 393224 | tf_op jit(solution)/shard_map/ppermute | solution.py:166
  89.0 6.0 %collective-permute-start.10 = (bf16[64,1024]{1,0:T(8,128)(2,1)S(1)}, bf16[64,1024]{1,0:T(8,128)(2,1)S(1)}, u32[]{:S(2)}, u32[]{:S(2)}) collective-permute-start(bf16[64,1024]{1,0:T(8,128)(2,1)S(1)} %get-tuple-element.31), channel_id=1, source_target_pairs={{0,12},{1,5},{2,14},{3,7},{4,0},{5,9},{6,2},{7,11},{8,4},{9,13},{1... | collective-permute-start | bytes 393224 | tf_op jit(solution)/shard_map/ppermute | solution.py:167
  95.0 0.0 collective-permute-done.8
  95.0 3.4 %collective-permute-done.11 = bf16[64,1024]{1,0:T(8,128)(2,1)S(1)} collective-permute-done((bf16[64,1024]{1,0:T(8,128)(2,1)S(1)}, bf16[64,1024]{1,0:T(8,128)(2,1)S(1)}, u32[]{:S(2)}, u32[]{:S(2)}) %collective-permute-start.11) | collective-permute-done | bytes 131104 | tf_op jit(solution)/shard_map/ppermute | solution.py:166
  98.5 0.1 fusion
  98.5 1.9 %collective-permute-start.12 = (bf16[64,1024]{1,0:T(8,128)(2,1)S(1)}, bf16[64,1024]{1,0:T(8,128)(2,1)S(1)}, u32[]{:S(2)}, u32[]{:S(2)}) collective-permute-start(bf16[64,1024]{1,0:T(8,128)(2,1)S(1)} %fusion), channel_id=1, source_target_pairs={{0,4},{1,13},{2,6},{3,15},{4,8},{5,1},{6,10},{7,3},{8,12},{9,5},{1... | collective-permute-start | bytes 393224 | tf_op jit(solution)/shard_map/ppermute | solution.py:168
  100.4 0.1 collective-permute-done.10
  100.5 7.0 %collective-permute-done.12 = bf16[64,1024]{1,0:T(8,128)(2,1)S(1)} collective-permute-done((bf16[64,1024]{1,0:T(8,128)(2,1)S(1)}, bf16[64,1024]{1,0:T(8,128)(2,1)S(1)}, u32[]{:S(2)}, u32[]{:S(2)}) %collective-permute-start.12) | collective-permute-done | bytes 131104 | tf_op jit(solution)/shard_map/ppermute | solution.py:168
  107.5 0.7 fusion.2
Async XLA Ops:
  17.8 21.8 %collective-permute-start = (bf16[8,16,1024]{2,1,0:T(8,128)(2,1)S(1)}, bf16[8,16,1024]{2,1,0:T(8,128)(2,1)S(1)}, u32[]{:S(2)}, u32[]{:S(2)}) collective-permute-start(bf16[8,16,1024]{2,1,0:T(8,128)(2,1)S(1)} %all_to_all.5.refs_0_), channel_id=1, source_target_pairs={{0,128},{1,17},{16,144},{17,33},{32,160},{33,49},{48,176},{49,65},... | collective-permute-start | bytes 786440 | tf_op jit(solution)/shard_map/ppermute | solution.py:155
  23.0 18.5 %collective-permute-start.4 = (bf16[8,16,1024]{2,1,0:T(8,128)(2,1)S(1)}, bf16[8,16,1024]{2,1,0:T(8,128)(2,1)S(1)}, u32[]{:S(2)}, u32[]{:S(2)}) collective-permute-start(bf16[8,16,1024]{2,1,0:T(8,128)(2,1)S(1)} %all_to_all.5.refs_0_), channel_id=1, source_target_pairs={{0,896},{1,113},{16,912},{17,1},{32,928},{33,17},{48,944},{49,33},... | collective-permute-start | bytes 786440 | tf_op jit(solution)/shard_map/ppermute | solution.py:156
  39.6 9.5 %collective-permute-start.1 = (bf16[8,16,1024]{2,1,0:T(8,128)(2,1)S(1)}, bf16[8,16,1024]{2,1,0:T(8,128)(2,1)S(1)}, u32[]{:S(2)}, u32[]{:S(2)}) collective-permute-start(bf16[8,16,1024]{2,1,0:T(8,128)(2,1)S(1)} %collective-permute-done.refs_0_), channel_id=1, source_target_pairs={{0,128},{1,17},{16,144},{17,33},{32,160},{33,49},{48,176},{49,65},... | collective-permute-start | bytes 786440 | tf_op jit(solution)/shard_map/ppermute | solution.py:155
  41.5 9.5 %collective-permute-start.5 = (bf16[8,16,1024]{2,1,0:T(8,128)(2,1)S(1)}, bf16[8,16,1024]{2,1,0:T(8,128)(2,1)S(1)}, u32[]{:S(2)}, u32[]{:S(2)}) collective-permute-start(bf16[8,16,1024]{2,1,0:T(8,128)(2,1)S(1)} %collective-permute-done.4.refs_1_), channel_id=1, source_target_pairs={{0,896},{1,113},{16,912},{17,1},{32,928},{33,17},{48,944},{49,33},... | collective-permute-start | bytes 786440 | tf_op jit(solution)/shard_map/ppermute | solution.py:156
  49.1 10.5 %collective-permute-start.2 = (bf16[8,16,1024]{2,1,0:T(8,128)(2,1)S(1)}, bf16[8,16,1024]{2,1,0:T(8,128)(2,1)S(1)}, u32[]{:S(2)}, u32[]{:S(2)}) collective-permute-start(bf16[8,16,1024]{2,1,0:T(8,128)(2,1)S(1)} %collective-permute-done.1.refs_0_), channel_id=1, source_target_pairs={{0,128},{1,17},{16,144},{17,33},{32,160},{33,49},{48,176},{49,65},... | collective-permute-start | bytes 786440 | tf_op jit(solution)/shard_map/ppermute | solution.py:155
  51.0 17.1 %collective-permute-start.6 = (bf16[8,16,1024]{2,1,0:T(8,128)(2,1)S(1)}, bf16[8,16,1024]{2,1,0:T(8,128)(2,1)S(1)}, u32[]{:S(2)}, u32[]{:S(2)}) collective-permute-start(bf16[8,16,1024]{2,1,0:T(8,128)(2,1)S(1)} %collective-permute-done.5.refs_1_), channel_id=1, source_target_pairs={{0,896},{1,113},{16,912},{17,1},{32,928},{33,17},{48,944},{49,33},... | collective-permute-start | bytes 786440 | tf_op jit(solution)/shard_map/ppermute | solution.py:156
  56.2 1.6 %copy-start = (bf16[1024,1024]{1,0:T(8,128)(2,1)S(1)}, bf16[1024,1024]{1,0:T(8,128)(2,1)}, u32[]{:S(2)}) copy-start(bf16[1024,1024]{1,0:T(8,128)(2,1)} %ints_ref.1) | copy-start | bytes 6291460
  57.7 0.7 copy-start.1
  59.6 10.8 %collective-permute-start.3 = (bf16[8,16,1024]{2,1,0:T(8,128)(2,1)S(1)}, bf16[8,16,1024]{2,1,0:T(8,128)(2,1)S(1)}, u32[]{:S(2)}, u32[]{:S(2)}) collective-permute-start(bf16[8,16,1024]{2,1,0:T(8,128)(2,1)S(1)} %collective-permute-done.2.refs_0_), channel_id=1, source_target_pairs={{0,128},{1,17},{16,144},{17,33},{32,160},{33,49},{48,176},{49,65},... | collective-permute-start | bytes 786440 | tf_op jit(solution)/shard_map/ppermute | solution.py:158
  72.1 4.6 %collective-permute-start.7 = (bf16[8,4,16,1024]{3,2,1,0:T(8,128)(2,1)S(1)}, bf16[8,4,16,1024]{3,2,1,0:T(8,128)(2,1)S(1)}, u32[]{:S(2)}, u32[]{:S(2)}) collective-permute-start(bf16[8,4,16,1024]{3,2,1,0:T(8,128)(2,1)S(1)} %get-tuple-element.27), channel_id=1, source_target_pairs={{0,1},{1,0},{2,3},{3,2},{4,5},{5,4},{6,7},{7,6},{8,9},{9,8},{10,11... | collective-permute-start | bytes 3145736 | tf_op jit(solution)/shard_map/ppermute | solution.py:161
  77.5 9.5 %collective-permute-start.9 = (bf16[2,64,1024]{2,1,0:T(8,128)(2,1)S(1)}, bf16[2,64,1024]{2,1,0:T(8,128)(2,1)S(1)}, u32[]{:S(2)}, u32[]{:S(2)}) collective-permute-start(bf16[2,64,1024]{2,1,0:T(8,128)(2,1)S(1)} %get-tuple-element.30), channel_id=1, source_target_pairs={{0,2},{1,15},{2,4},{3,1},{4,6},{5,3},{6,8},{7,5},{8,10},{9,7},{10,... | collective-permute-start | bytes 786440 | tf_op jit(solution)/shard_map/ppermute | solution.py:164
  80.2 14.8 %collective-permute-start.8 = (bf16[2,64,1024]{2,1,0:T(8,128)(2,1)S(1)}, bf16[2,64,1024]{2,1,0:T(8,128)(2,1)S(1)}, u32[]{:S(2)}, u32[]{:S(2)}) collective-permute-start(bf16[2,64,1024]{2,1,0:T(8,128)(2,1)S(1)} %get-tuple-element.29), channel_id=1, source_target_pairs={{0,2},{1,15},{2,4},{3,1},{4,6},{5,3},{6,8},{7,5},{8,10},{9,7},{10,... | collective-permute-start | bytes 786440 | tf_op jit(solution)/shard_map/ppermute | solution.py:165
  87.0 11.4 %collective-permute-start.11 = (bf16[64,1024]{1,0:T(8,128)(2,1)S(1)}, bf16[64,1024]{1,0:T(8,128)(2,1)S(1)}, u32[]{:S(2)}, u32[]{:S(2)}) collective-permute-start(bf16[64,1024]{1,0:T(8,128)(2,1)S(1)} %get-tuple-element.32), channel_id=1, source_target_pairs={{0,4},{1,13},{2,6},{3,15},{4,8},{5,1},{6,10},{7,3},{8,12},{9,5},{1... | collective-permute-start | bytes 393224 | tf_op jit(solution)/shard_map/ppermute | solution.py:166
  89.0 11.6 %collective-permute-start.10 = (bf16[64,1024]{1,0:T(8,128)(2,1)S(1)}, bf16[64,1024]{1,0:T(8,128)(2,1)S(1)}, u32[]{:S(2)}, u32[]{:S(2)}) collective-permute-start(bf16[64,1024]{1,0:T(8,128)(2,1)S(1)} %get-tuple-element.31), channel_id=1, source_target_pairs={{0,12},{1,5},{2,14},{3,7},{4,0},{5,9},{6,2},{7,11},{8,4},{9,13},{1... | collective-permute-start | bytes 393224 | tf_op jit(solution)/shard_map/ppermute | solution.py:167
  98.5 9.0 %collective-permute-start.12 = (bf16[64,1024]{1,0:T(8,128)(2,1)S(1)}, bf16[64,1024]{1,0:T(8,128)(2,1)S(1)}, u32[]{:S(2)}, u32[]{:S(2)}) collective-permute-start(bf16[64,1024]{1,0:T(8,128)(2,1)S(1)} %fusion), channel_id=1, source_target_pairs={{0,4},{1,13},{2,6},{3,15},{4,8},{5,1},{6,10},{7,3},{8,12},{9,5},{1... | collective-permute-start | bytes 393224 | tf_op jit(solution)/shard_map/ppermute | solution.py:168

commit v3 on v0

v3 whole, which is shorter than its diff:
```python
import functools

import jax
import jax.numpy as jnp
from jax import lax
from jax.experimental import pallas as pl
from jax.experimental.pallas import tpu as pltpu
from jax.sharding import PartitionSpec as P

TILE = 128
SIDE = 8
FAR = 4
CLASSES = 4
ROWS = 16
VMEM = pl.BlockSpec(memory_space=pltpu.VMEM)
SMEM = pl.BlockSpec(memory_space=pltpu.SMEM)
HBM = pl.BlockSpec(memory_space=pltpu.HBM)


def member(z, x, core):
    return (z % SIDE * SIDE + x % SIDE) * 2 + core


def far_groups():
    return [
        [member(pz + 2 * a, px + 2 * b, core) for a in range(FAR) for b in range(FAR)]
        for core in range(2)
        for pz in range(2)
        for px in range(2)
    ]


def near_pairs(dz, dx):
    def partner(place, core):
        return place + 1 if (place + core) % 2 == 0 else place - 1

    return [
        (member(z, x, core), member(partner(z, core) if dz else z, partner(x, core) if dx else x, core))
        for z in range(SIDE)
        for x in range(SIDE)
        for core in range(2)
    ]


def red_step(step):
    return [(y * 2 + c, (y + (step if c == 0 else -step)) % SIDE * 2 + c) for y in range(SIDE) for c in range(2)]


def class_rows(place_ref, rows_ref):
    rep = place_ref[0]
    depth = rows_ref.shape[-1]
    parts = [rows_ref[:, half].reshape(-1, depth) for half in (rep, 1 - rep)]
    return jnp.concatenate(parts, axis=0)


def put(index, here, total, kept_ref, away_ref):
    total = total.astype(kept_ref.dtype).reshape((2,) + kept_ref.shape[1:-1] + (total.shape[-1],))
    kept_ref[index, ..., here] = total[0]
    away_ref[index % away_ref.shape[0], ..., here] = total[1]


def first_kernel(place_ref, bits_hbm, ints_hbm, rows_ref, kept_ref, away_ref, masked_ref, bits_ref, ints_ref, sems):
    cols = ints_ref.shape[1]
    width = 256
    tiles = [slice(start, start + width) for start in range(0, cols, width)]
    bits_copy = pltpu.make_async_copy(bits_hbm, bits_ref, sems.at[len(tiles)])
    bits_copy.start()
    copies = [
        pltpu.make_async_copy(ints_hbm.at[:, here], ints_ref.at[:, here], sems.at[i]) for i, here in enumerate(tiles)
    ]
    for copy in copies:
        copy.start()
    rows = class_rows(place_ref, rows_ref)
    bits_copy.wait()
    for here, copy in zip(tiles, copies):
        copy.wait()
        for q in range(ints_ref.shape[0] // TILE):
            for p in range(here.start // TILE, here.stop // TILE):
                tile = (slice(q * TILE, (q + 1) * TILE), slice(p * TILE, (p + 1) * TILE))
                bit = jnp.broadcast_to(bits_ref[q : q + 1, p : p + 1], (TILE, TILE))
                masked_ref[tile] = ints_ref[tile] * bit.astype(jnp.float32).astype(ints_ref.dtype)
        total = jnp.dot(rows, masked_ref[:, here], preferred_element_type=jnp.float32)
        put(0, here, total, kept_ref, away_ref)


def sums_shape(rows, cols, classes=CLASSES):
    far, _, pairs, _, _ = rows.shape
    return jax.ShapeDtypeStruct((classes, far, pairs, ROWS, cols), jnp.bfloat16)


def first_dot(place, bits, ints, rows):
    depth, cols = ints.shape
    return pl.pallas_call(
        first_kernel,
        in_specs=[SMEM, HBM, HBM, VMEM],
        out_specs=[VMEM, VMEM, VMEM],
        out_shape=[
            sums_shape(rows, cols),
            sums_shape(rows, cols, CLASSES - 1),
            jax.ShapeDtypeStruct(ints.shape, ints.dtype),
        ],
        scratch_shapes=[
            pltpu.VMEM(bits.shape, bits.dtype),
            pltpu.VMEM(ints.shape, ints.dtype),
            pltpu.SemaphoreType.DMA((cols // 256 + 1,)),
        ],
        compiler_params=pltpu.CompilerParams(vmem_limit_bytes=16 * 1024 * 1024),
        cost_estimate=pl.CostEstimate(
            flops=rows.size * cols * 2, bytes_accessed=2 * rows.size + 4 * ints.size, transcendentals=0
        ),
    )(place, bits, ints, rows)


def dot_kernel(index, place_ref, rows_ref, masked_ref, *refs):
    kept_ref, away_ref = refs[-2:]
    width = 256
    rows = class_rows(place_ref, rows_ref)
    for start in range(0, masked_ref.shape[1], width):
        here = slice(start, start + width)
        total = jnp.dot(rows, masked_ref[:, here], preferred_element_type=jnp.float32)
        put(index, here, total, kept_ref, away_ref)


def dot(place, index, rows, masked, *sums):
    cols = masked.shape[1]
    away = sums_shape(rows, cols, CLASSES - 1 if len(sums) == 2 else 1)
    return pl.pallas_call(
        functools.partial(dot_kernel, index),
        in_specs=[SMEM] + [VMEM] * (2 + len(sums)),
        out_specs=[VMEM, VMEM],
        out_shape=[sums_shape(rows, cols), away],
        input_output_aliases={3 + i: i for i in range(len(sums))},
        compiler_params=pltpu.CompilerParams(vmem_limit_bytes=16 * 1024 * 1024),
        cost_estimate=pl.CostEstimate(
            flops=rows.size * cols * 2, bytes_accessed=2 * rows.size + 2 * masked.size, transcendentals=0
        ),
    )(place, rows, masked, *sums)


def share_kernel(steps, place_ref, kept_ref, early_ref, late_ref, *out_refs):
    z, x, y, way = place_ref[1], place_ref[2], place_ref[3], 1 - 2 * place_ref[0]
    flat = [step for group in steps for step in group]
    outs = [(ref, i) for ref, group in zip(out_refs, steps) for i in range(len(group))]
    for step, (out_ref, i) in zip(flat, outs):
        index = (y + way * step + SIDE) & (SIDE - 1)
        dz = (index ^ z) & 1
        a = index >> 1
        for dx in range(2):
            one = kept_ref[2 * dz + dx, a]
            if dx == 0:
                other = early_ref[2 * dz, a]
            else:
                other = jnp.where(dz == 0, early_ref[1, a], late_ref[0, a])
            out_ref[i, :, (x + dx) & 1] = (one.astype(jnp.float32) + other.astype(jnp.float32)).astype(one.dtype)


def share(place, steps, kept, early, late):
    _, _, pairs, rows, cols = kept.shape
    return pl.pallas_call(
        functools.partial(share_kernel, steps),
        in_specs=[SMEM, VMEM, VMEM, VMEM],
        out_specs=[VMEM] * len(steps),
        out_shape=[jax.ShapeDtypeStruct((len(group), pairs, 2, rows, cols), kept.dtype) for group in steps],
        compiler_params=pltpu.CompilerParams(vmem_limit_bytes=16 * 1024 * 1024),
        cost_estimate=pl.CostEstimate(flops=kept.size, bytes_accessed=6 * kept.size, transcendentals=0),
    )(place, kept, early, late)


def added(*terms):
    return sum(t.astype(jnp.float32) for t in terms).astype(jnp.bfloat16)


def per_device(amps, ints, bits):
    owner, y, rep = (lax.axis_index(name).astype(jnp.int32) for name in ("owner", "red", "rep"))
    place = jnp.stack([rep, owner >> 3, owner & (SIDE - 1), y])
    depth = amps.shape[1]
    cols = ints.shape[1]

    copies = jnp.broadcast_to(amps[None], (FAR * FAR,) + amps.shape)
    mine = lax.all_to_all(copies, ("owner", "rep"), 0, 0, axis_index_groups=far_groups(), tiled=True)
    mine = mine.reshape(FAR, 2, 2, ROWS, depth)
    near = [lax.ppermute(mine, ("owner", "rep"), near_pairs(dz, dx)) for dz, dx in ((0, 1), (1, 0), (1, 1))]
    kept, early, masked = first_dot(place, bits, ints, mine)
    kept, early = dot(place, 1, near[0], masked, kept, early)
    kept, early = dot(place, 2, near[1], masked, kept, early)
    swap = [(0, 1), (1, 0)]
    early = lax.ppermute(early, "rep", swap)
    kept, late = dot(place, 3, near[2], masked, kept)
    late = lax.ppermute(late, "rep", swap)

    def along(step, part):
        return lax.ppermute(part, ("red", "rep"), red_step(step))

    groups = ((-1, -4), (1, 3), (-2,), (-3,), (2,), (0,))
    down, up, two_down, three_down, two_up, own = share(place, groups, kept, early, late)
    down, up, two_down = along(-1, down), along(1, up), along(-2, two_down)
    three_down = along(-3, added(three_down[0], down[1]))
    two_up = along(2, added(two_up[0], up[1]))
    return added(own[0], down[0], up[0], two_down[0], three_down, two_up).reshape(-1, cols)


def solution(mesh):
    return jax.shard_map(
        per_device,
        mesh=mesh,
        in_specs=(
            P("owner", ("red", "rep")),
            P(("red", "rep"), "owner"),
            P(("red", "rep"), "owner"),
        ),
        out_specs=P(("red", "rep"), "owner"),
        check_vma=False,
    )
```

time: 191 us -> 98.8 us (0.52)
  waiting for transfers between devices: 168 us -> 9.24 us
  blocking collectives: 0 us -> 39.6 us
  starting transfers between devices: 0.04 us -> 37.4 us
  between operations: 13.4 us -> 0.2 us
  Pallas kernels: 0 us -> 7.78 us
  matrix products: 3.99 us -> 0 us
    all_gather x1 -> x0, waiting for transfers between devices: 103 us -> none  [per_device(): gathered = lax.all_gather(amps, 'owner', axis=0, tiled=True)]
    reduce_scatter x1 -> x0, waiting for transfers between devices: 64.6 us -> none  [per_device(): lax.psum_scatter(partial_sums.astype(jnp.bfloat16), ('red', 'rep'), scatt...]
    all_to_all x0 -> x1, blocking collectives: none -> 39.6 us  [per_device(): lax.all_to_all(copies, ('owner', 'rep'), 0, 0, axis_index_groups=far_grou...]
    ppermute x0 -> x10, starting transfers between devices: none -> 37.4 us  [the longest x5 19.4 us: along(): return lax.ppermute(part, ('red', 'rep'), red_step(step))]
    ppermute x0 -> x10, waiting for transfers between devices: none -> 9.24 us  [the longest x5 7.26 us: along(): return lax.ppermute(part, ('red', 'rep'), red_step(step))]
    pallas_call x0 -> x5, Pallas kernels: none -> 7.78 us  [the longest x3 3.78 us: dot(): pl.pallas_call(functools.partial(dot_kernel, index), in_specs=[SMEM] + [V...]
    dot_general x1 -> x0, matrix products: 3.99 us -> none  [per_device(): partial_sums = jnp.dot(gathered, masked, preferred_element_type=jnp.float32)]
  transfers between devices with their start and end apart: 2 -> 10, of which waited for: 2 -> 4; matrix products, arithmetic and copies ran while one was open for 0% -> 0% of each run, Pallas kernels for 0% -> 7%
where the time goes in v3:
time: 98.8 us; the launch traced here: 98.2 us
  blocking collectives  39.6 us (40%)
  starting transfers between devices  37.4 us (38%)
  waiting for transfers between devices  9.24 us (9%)
  Pallas kernels  7.78 us (8%)
  local copies, waits for them, and re-layouts  3.08 us (3%)
    all_to_all x1, blocking collectives, per_device(): lax.all_to_all(copies, ('owner', 'rep'), 0, 0, axis_index_groups=far_grou...  39.6 us
    ppermute x5, starting transfers between devices, along(): return lax.ppermute(part, ('red', 'rep'), red_step(step))  19.4 us
    ppermute x3, starting transfers between devices, per_device(): lax.ppermute(mine, ('owner', 'rep'), near_pairs(dz, dx))  10.8 us
    ppermute x5, waiting for transfers between devices, along(): return lax.ppermute(part, ('red', 'rep'), red_step(step))  7.26 us
    ppermute x1, starting transfers between devices, per_device(): early = lax.ppermute(early, 'rep', swap)  5.28 us
    pallas_call x3, Pallas kernels, dot(): pl.pallas_call(functools.partial(dot_kernel, index), in_specs=[SMEM] + [V...  3.78 us
    pallas_call x1, Pallas kernels, first_dot(): pl.pallas_call(first_kernel, in_specs=[SMEM, HBM, HBM, VMEM], out_specs=[...  3.18 us
    unnamed x4, local copies, waits for them, and re-layouts  2.27 us
  transfers between devices with their start and end apart: 10, of which 4 were waited for; matrix products, arithmetic and copies ran while one was open for 0% of the time, Pallas kernels for 7%

profile of v3, /device:TPU:1, one launch (start us, length us, event | category | flops | bytes accessed | tf_op | source)
XLA Modules:
  0.0 98.2 jit_solution(7864863001471384836)
XLA Ops:
  0.0 0.8 broadcast_in_dim.2
  0.8 39.6 %all_to_all.5 = bf16[16,16,1024]{2,1,0:T(8,128)(2,1)S(1)} all-to-all(bf16[16,16,1024]{2,1,0:T(8,128)(2,1)S(1)} %broadcast_in_dim.2), channel_id=1, replica_groups={{0,32,64,96,256,288,320,352,512,544,576,608,768,800,832,864},{16,48,80,..., dimensions={0} | all-to-all | bytes 1048576 | tf_op jit(solution)/shard_map/all_to_all | solution.py:180
  40.5 1.9 %collective-permute-start.2 = (bf16[4,2,2,16,1024]{4,3,2,1,0:T(8,128)(2,1)S(1)}, bf16[4,2,2,16,1024]{4,3,2,1,0:T(8,128)(2,1)S(1)}, u32[]{:S(2)}, u32[]{:S(2)}) collective-permute-start(bf16[4,2,2,16,1024]{4,3,2,1,0:T(8,128)(2,1)S(1)} %bitcast.16), channel_id=1, source_target_pairs={{0,16},{1,113},{16,0},{17,33},{32,48},{33,17},{48,32},{49,65},{64,... | collective-permute-start | bytes 1572872 | tf_op jit(solution)/shard_map/ppermute | solution.py:182
  42.4 4.4 %collective-permute-start.1 = (bf16[4,2,2,16,1024]{4,3,2,1,0:T(8,128)(2,1)S(1)}, bf16[4,2,2,16,1024]{4,3,2,1,0:T(8,128)(2,1)S(1)}, u32[]{:S(2)}, u32[]{:S(2)}) collective-permute-start(bf16[4,2,2,16,1024]{4,3,2,1,0:T(8,128)(2,1)S(1)} %bitcast.17), channel_id=1, source_target_pairs={{0,128},{1,897},{16,144},{17,913},{32,160},{33,929},{48,176},{49,9... | collective-permute-start | bytes 1572872 | tf_op jit(solution)/shard_map/ppermute | solution.py:182
  46.8 0.1 pad_add_fusion.place_ref
  46.9 4.4 %collective-permute-start = (bf16[4,2,2,16,1024]{4,3,2,1,0:T(8,128)(2,1)S(1)}, bf16[4,2,2,16,1024]{4,3,2,1,0:T(8,128)(2,1)S(1)}, u32[]{:S(2)}, u32[]{:S(2)}) collective-permute-start(bf16[4,2,2,16,1024]{4,3,2,1,0:T(8,128)(2,1)S(1)} %bitcast.18), channel_id=1, source_target_pairs={{0,144},{1,1009},{16,128},{17,929},{32,176},{33,913},{48,160},{49,... | collective-permute-start | bytes 1572872 | tf_op jit(solution)/shard_map/ppermute | solution.py:182
  51.3 0.0 copy-start
  51.4 1.6 %copy-done = bf16[1024,1024]{1,0:T(8,128)(2,1)S(1)} copy-done((bf16[1024,1024]{1,0:T(8,128)(2,1)S(1)}, bf16[1024,1024]{1,0:T(8,128)(2,1)}, u32[]{:S(2)}) %copy-start) | copy-done | bytes 2097176
  52.9 0.0 copy-start.1
  52.9 0.7 copy-done.1
  53.6 3.2 %shard_map.37 = (bf16[4,4,2,16,1024]{4,3,2,1,0:T(8,128)(2,1)S(1)}, bf16[3,4,2,16,1024]{4,3,2,1,0:T(8,128)(2,1)S(1)}, bf16[1024,1024]{1,0:T(8,128)(2,1)S(1)}) custom-call(s32[4]{0:T(128)S(1)} %pad_add_fusion.place_ref, s32[8,8]{1,0:T(8,128)S(1)} %copy-done.1, bf16[1024,1024]{1,0:T(8,128)(2,1)S(1)} %copy-done, bf16[4,2,2,16,1024]{4,3,2,1,0:T(8,128)(2,1)S(1)} %bitcast.19), custom_call_target="tpu_custom_call" | custom-call | flops 536870912 | bytes 4718592 | tf_op jit(solution)/shard_map/pallas_call | solution.py:93
  56.8 0.0 collective-permute-done.2.rows_ref
  56.8 1.3 %shard_map.38 = (bf16[4,4,2,16,1024]{4,3,2,1,0:T(8,128)(2,1)S(1)}, bf16[3,4,2,16,1024]{4,3,2,1,0:T(8,128)(2,1)S(1)}) custom-call(s32[4]{0:T(128)S(1)} %pad_add_fusion.place_ref, bf16[4,2,2,16,1024]{4,3,2,1,0:T(8,128)(2,1)S(1)} %collective-permute-done.2.rows_ref, ...), custom_call_target="tpu_custom_call", output_to_operand_aliasing={{0}: (3, {}), {1}: (4, {})} | custom-call | flops 536870912 | bytes 2621440 | tf_op jit(solution)/shard_map/pallas_call | solution.py:127
  58.1 0.5 collective-permute-done.1.rows_ref
  58.5 1.2 %shard_map.39 = (bf16[4,4,2,16,1024]{4,3,2,1,0:T(8,128)(2,1)S(1)}, bf16[3,4,2,16,1024]{4,3,2,1,0:T(8,128)(2,1)S(1)}) custom-call(s32[4]{0:T(128)S(1)} %pad_add_fusion.place_ref, bf16[4,2,2,16,1024]{4,3,2,1,0:T(8,128)(2,1)S(1)} %collective-permute-done.1.rows_ref, ...), custom_call_target="tpu_custom_call", output_to_operand_aliasing={{0}: (3, {}), {1}: (4, {})} | custom-call | flops 536870912 | bytes 2621440 | tf_op jit(solution)/shard_map/pallas_call | solution.py:127
  59.8 5.3 %collective-permute-start.3 = (bf16[3,4,2,16,1024]{4,3,2,1,0:T(8,128)(2,1)S(1)}, bf16[3,4,2,16,1024]{4,3,2,1,0:T(8,128)(2,1)S(1)}, u32[]{:S(2)}, u32[]{:S(2)}) collective-permute-start(bf16[3,4,2,16,1024]{4,3,2,1,0:T(8,128)(2,1)S(1)} %get-tuple-element.27), channel_id=1, source_target_pairs={{0,1},{1,0},{2,3},{3,2},{4,5},{5,4},{6,7},{7,6},{8,9},{9,8},{10,11... | collective-permute-start | bytes 2359304 | tf_op jit(solution)/shard_map/ppermute | solution.py:187
  65.1 0.0 collective-permute-done.rows_ref
  65.1 1.3 %shard_map.40 = (bf16[4,4,2,16,1024]{4,3,2,1,0:T(8,128)(2,1)S(1)}, bf16[1,4,2,16,1024]{4,3,2,1,0:T(8,128)(2,1)S(1)}) custom-call(s32[4]{0:T(128)S(1)} %pad_add_fusion.place_ref, bf16[4,2,2,16,1024]{4,3,2,1,0:T(8,128)(2,1)S(1)} %collective-permute-done.rows_ref, bf16[1024,1024]{1,0:T(8,128)(2,1)S(1)} %get-tuple-element.20.masked_ref, ...), custom_call_target="tpu_custom_call", output_to_operand_aliasing={{0}: (3, {})} | custom-call | flops 536870912 | bytes 2621440 | tf_op jit(solution)/shard_map/pallas_call | solution.py:127
  66.4 1.9 %collective-permute-start.4 = (bf16[1,4,2,16,1024]{4,3,2,1,0:T(8,128)(2,1)S(1)}, bf16[1,4,2,16,1024]{4,3,2,1,0:T(8,128)(2,1)S(1)}, u32[]{:S(2)}, u32[]{:S(2)}) collective-permute-start(bf16[1,4,2,16,1024]{4,3,2,1,0:T(8,128)(2,1)S(1)} %get-tuple-element.28), channel_id=1, source_target_pairs={{0,1},{1,0},{2,3},{3,2},{4,5},{5,4},{6,7},{7,6},{8,9},{9,8},{10,11... | collective-permute-start | bytes 786440 | tf_op jit(solution)/shard_map/ppermute | solution.py:189
  68.3 1.5 %collective-permute-done.4.late_ref = bf16[1,4,2,16,1024]{4,3,2,1,0:T(8,128)(2,1)S(1)} collective-permute-done((bf16[1,4,2,16,1024]{4,3,2,1,0:T(8,128)(2,1)S(1)}, bf16[1,4,2,16,1024]{4,3,2,1,0:T(8,128)(2,1)S(1)}, u32[]{:S(2)}, u32[]{:S(2)}) %collective-permute-start.4) | collective-permute-done | bytes 262176 | tf_op jit(solution)/shard_map/ppermute | solution.py:189
  69.8 0.0 collective-permute-done.3.early_ref
  69.8 0.8 shard_map.41
  70.6 3.3 %collective-permute-start.5 = (bf16[2,2,2,16,1024]{4,3,2,1,0:T(8,128)(2,1)S(1)}, bf16[2,2,2,16,1024]{4,3,2,1,0:T(8,128)(2,1)S(1)}, u32[]{:S(2)}, u32[]{:S(2)}) collective-permute-start(bf16[2,2,2,16,1024]{4,3,2,1,0:T(8,128)(2,1)S(1)} %get-tuple-element.30), channel_id=1, source_target_pairs={{0,14},{1,3},{2,0},{3,5},{4,2},{5,7},{6,4},{7,9},{8,6},{9,11},{10,... | collective-permute-start | bytes 786440 | tf_op jit(solution)/shard_map/ppermute | solution.py:192
  74.0 4.5 %collective-permute-start.6 = (bf16[2,2,2,16,1024]{4,3,2,1,0:T(8,128)(2,1)S(1)}, bf16[2,2,2,16,1024]{4,3,2,1,0:T(8,128)(2,1)S(1)}, u32[]{:S(2)}, u32[]{:S(2)}) collective-permute-start(bf16[2,2,2,16,1024]{4,3,2,1,0:T(8,128)(2,1)S(1)} %get-tuple-element.31), channel_id=1, source_target_pairs={{0,2},{1,15},{2,4},{3,1},{4,6},{5,3},{6,8},{7,5},{8,10},{9,7},{10,... | collective-permute-start | bytes 786440 | tf_op jit(solution)/shard_map/ppermute | solution.py:192
  78.5 1.9 %collective-permute-start.7 = (bf16[1,2,2,16,1024]{4,3,2,1,0:T(8,128)(2,1)S(1)}, bf16[1,2,2,16,1024]{4,3,2,1,0:T(8,128)(2,1)S(1)}, u32[]{:S(2)}, u32[]{:S(2)}) collective-permute-start(bf16[1,2,2,16,1024]{4,3,2,1,0:T(8,128)(2,1)S(1)} %get-tuple-element.32), channel_id=1, source_target_pairs={{0,12},{1,5},{2,14},{3,7},{4,0},{5,9},{6,2},{7,11},{8,4},{9,13},{1... | collective-permute-start | bytes 393224 | tf_op jit(solution)/shard_map/ppermute | solution.py:192
  80.4 0.0 collective-permute-done.5
  80.5 5.9 %collective-permute-start.8 = (bf16[2,2,16,1024]{3,2,1,0:T(8,128)(2,1)S(1)}, bf16[2,2,16,1024]{3,2,1,0:T(8,128)(2,1)S(1)}, u32[]{:S(2)}, u32[]{:S(2)}) collective-permute-start(bf16[2,2,16,1024]{3,2,1,0:T(8,128)(2,1)S(1)} %fusion.2), channel_id=1, source_target_pairs={{0,10},{1,7},{2,12},{3,9},{4,14},{5,11},{6,0},{7,13},{8,2},{9,15},... | collective-permute-start | bytes 393224 | tf_op jit(solution)/shard_map/ppermute | solution.py:192
  86.3 0.0 collective-permute-done.6
  86.4 3.8 %collective-permute-start.9 = (bf16[2,2,16,1024]{3,2,1,0:T(8,128)(2,1)S(1)}, bf16[2,2,16,1024]{3,2,1,0:T(8,128)(2,1)S(1)}, u32[]{:S(2)}, u32[]{:S(2)}) collective-permute-start(bf16[2,2,16,1024]{3,2,1,0:T(8,128)(2,1)S(1)} %fusion.3), channel_id=1, source_target_pairs={{0,4},{1,13},{2,6},{3,15},{4,8},{5,1},{6,10},{7,3},{8,12},{9,5},{1... | collective-permute-start | bytes 393224 | tf_op jit(solution)/shard_map/ppermute | solution.py:192
  90.2 0.0 collective-permute-done.7
  90.2 1.8 %collective-permute-done.8 = bf16[2,2,16,1024]{3,2,1,0:T(8,128)(2,1)S(1)} collective-permute-done((bf16[2,2,16,1024]{3,2,1,0:T(8,128)(2,1)S(1)}, bf16[2,2,16,1024]{3,2,1,0:T(8,128)(2,1)S(1)}, u32[]{:S(2)}, u32[]{:S(2)}) %collective-permute-start.8) | collective-permute-done | bytes 131104 | tf_op jit(solution)/shard_map/ppermute | solution.py:192
  92.0 5.5 %collective-permute-done.9 = bf16[2,2,16,1024]{3,2,1,0:T(8,128)(2,1)S(1)} collective-permute-done((bf16[2,2,16,1024]{3,2,1,0:T(8,128)(2,1)S(1)}, bf16[2,2,16,1024]{3,2,1,0:T(8,128)(2,1)S(1)}, u32[]{:S(2)}, u32[]{:S(2)}) %collective-permute-start.9) | collective-permute-done | bytes 131104 | tf_op jit(solution)/shard_map/ppermute | solution.py:192
  97.5 0.8 fusion.1
  (2 shorter events, 0.1 us)
Async XLA Ops:
  40.5 16.4 %collective-permute-start.2 = (bf16[4,2,2,16,1024]{4,3,2,1,0:T(8,128)(2,1)S(1)}, bf16[4,2,2,16,1024]{4,3,2,1,0:T(8,128)(2,1)S(1)}, u32[]{:S(2)}, u32[]{:S(2)}) collective-permute-start(bf16[4,2,2,16,1024]{4,3,2,1,0:T(8,128)(2,1)S(1)} %bitcast.16), channel_id=1, source_target_pairs={{0,16},{1,113},{16,0},{17,33},{32,48},{33,17},{48,32},{49,65},{64,... | collective-permute-start | bytes 1572872 | tf_op jit(solution)/shard_map/ppermute | solution.py:182
  42.4 16.2 %collective-permute-start.1 = (bf16[4,2,2,16,1024]{4,3,2,1,0:T(8,128)(2,1)S(1)}, bf16[4,2,2,16,1024]{4,3,2,1,0:T(8,128)(2,1)S(1)}, u32[]{:S(2)}, u32[]{:S(2)}) collective-permute-start(bf16[4,2,2,16,1024]{4,3,2,1,0:T(8,128)(2,1)S(1)} %bitcast.17), channel_id=1, source_target_pairs={{0,128},{1,897},{16,144},{17,913},{32,160},{33,929},{48,176},{49,9... | collective-permute-start | bytes 1572872 | tf_op jit(solution)/shard_map/ppermute | solution.py:182
  46.9 18.2 %collective-permute-start = (bf16[4,2,2,16,1024]{4,3,2,1,0:T(8,128)(2,1)S(1)}, bf16[4,2,2,16,1024]{4,3,2,1,0:T(8,128)(2,1)S(1)}, u32[]{:S(2)}, u32[]{:S(2)}) collective-permute-start(bf16[4,2,2,16,1024]{4,3,2,1,0:T(8,128)(2,1)S(1)} %bitcast.18), channel_id=1, source_target_pairs={{0,144},{1,1009},{16,128},{17,929},{32,176},{33,913},{48,160},{49,... | collective-permute-start | bytes 1572872 | tf_op jit(solution)/shard_map/ppermute | solution.py:182
  51.3 1.6 %copy-start = (bf16[1024,1024]{1,0:T(8,128)(2,1)S(1)}, bf16[1024,1024]{1,0:T(8,128)(2,1)}, u32[]{:S(2)}) copy-start(bf16[1024,1024]{1,0:T(8,128)(2,1)} %ints_hbm.1) | copy-start | bytes 6291460
  52.9 0.7 copy-start.1
  59.8 10.0 %collective-permute-start.3 = (bf16[3,4,2,16,1024]{4,3,2,1,0:T(8,128)(2,1)S(1)}, bf16[3,4,2,16,1024]{4,3,2,1,0:T(8,128)(2,1)S(1)}, u32[]{:S(2)}, u32[]{:S(2)}) collective-permute-start(bf16[3,4,2,16,1024]{4,3,2,1,0:T(8,128)(2,1)S(1)} %get-tuple-element.27), channel_id=1, source_target_pairs={{0,1},{1,0},{2,3},{3,2},{4,5},{5,4},{6,7},{7,6},{8,9},{9,8},{10,11... | collective-permute-start | bytes 2359304 | tf_op jit(solution)/shard_map/ppermute | solution.py:187
  66.4 3.4 %collective-permute-start.4 = (bf16[1,4,2,16,1024]{4,3,2,1,0:T(8,128)(2,1)S(1)}, bf16[1,4,2,16,1024]{4,3,2,1,0:T(8,128)(2,1)S(1)}, u32[]{:S(2)}, u32[]{:S(2)}) collective-permute-start(bf16[1,4,2,16,1024]{4,3,2,1,0:T(8,128)(2,1)S(1)} %get-tuple-element.28), channel_id=1, source_target_pairs={{0,1},{1,0},{2,3},{3,2},{4,5},{5,4},{6,7},{7,6},{8,9},{9,8},{10,11... | collective-permute-start | bytes 786440 | tf_op jit(solution)/shard_map/ppermute | solution.py:189
  70.6 9.8 %collective-permute-start.5 = (bf16[2,2,2,16,1024]{4,3,2,1,0:T(8,128)(2,1)S(1)}, bf16[2,2,2,16,1024]{4,3,2,1,0:T(8,128)(2,1)S(1)}, u32[]{:S(2)}, u32[]{:S(2)}) collective-permute-start(bf16[2,2,2,16,1024]{4,3,2,1,0:T(8,128)(2,1)S(1)} %get-tuple-element.30), channel_id=1, source_target_pairs={{0,14},{1,3},{2,0},{3,5},{4,2},{5,7},{6,4},{7,9},{8,6},{9,11},{10,... | collective-permute-start | bytes 786440 | tf_op jit(solution)/shard_map/ppermute | solution.py:192
  74.0 12.4 %collective-permute-start.6 = (bf16[2,2,2,16,1024]{4,3,2,1,0:T(8,128)(2,1)S(1)}, bf16[2,2,2,16,1024]{4,3,2,1,0:T(8,128)(2,1)S(1)}, u32[]{:S(2)}, u32[]{:S(2)}) collective-permute-start(bf16[2,2,2,16,1024]{4,3,2,1,0:T(8,128)(2,1)S(1)} %get-tuple-element.31), channel_id=1, source_target_pairs={{0,2},{1,15},{2,4},{3,1},{4,6},{5,3},{6,8},{7,5},{8,10},{9,7},{10,... | collective-permute-start | bytes 786440 | tf_op jit(solution)/shard_map/ppermute | solution.py:192
  78.5 11.7 %collective-permute-start.7 = (bf16[1,2,2,16,1024]{4,3,2,1,0:T(8,128)(2,1)S(1)}, bf16[1,2,2,16,1024]{4,3,2,1,0:T(8,128)(2,1)S(1)}, u32[]{:S(2)}, u32[]{:S(2)}) collective-permute-start(bf16[1,2,2,16,1024]{4,3,2,1,0:T(8,128)(2,1)S(1)} %get-tuple-element.32), channel_id=1, source_target_pairs={{0,12},{1,5},{2,14},{3,7},{4,0},{5,9},{6,2},{7,11},{8,4},{9,13},{1... | collective-permute-start | bytes 393224 | tf_op jit(solution)/shard_map/ppermute | solution.py:192
  80.5 11.5 %collective-permute-start.8 = (bf16[2,2,16,1024]{3,2,1,0:T(8,128)(2,1)S(1)}, bf16[2,2,16,1024]{3,2,1,0:T(8,128)(2,1)S(1)}, u32[]{:S(2)}, u32[]{:S(2)}) collective-permute-start(bf16[2,2,16,1024]{3,2,1,0:T(8,128)(2,1)S(1)} %fusion.2), channel_id=1, source_target_pairs={{0,10},{1,7},{2,12},{3,9},{4,14},{5,11},{6,0},{7,13},{8,2},{9,15},... | collective-permute-start | bytes 393224 | tf_op jit(solution)/shard_map/ppermute | solution.py:192
  86.4 11.1 %collective-permute-start.9 = (bf16[2,2,16,1024]{3,2,1,0:T(8,128)(2,1)S(1)}, bf16[2,2,16,1024]{3,2,1,0:T(8,128)(2,1)S(1)}, u32[]{:S(2)}, u32[]{:S(2)}) collective-permute-start(bf16[2,2,16,1024]{3,2,1,0:T(8,128)(2,1)S(1)} %fusion.3), channel_id=1, source_target_pairs={{0,4},{1,13},{2,6},{3,15},{4,8},{5,1},{6,10},{7,3},{8,12},{9,5},{1... | collective-permute-start | bytes 393224 | tf_op jit(solution)/shard_map/ppermute | solution.py:192

commit v4 on v3

--- a/solution.py
+++ b/solution.py
@@ -10,7 +10,8 @@
 TILE = 128
 SIDE = 8
 FAR = 4
-CLASSES = 4
+PART = 2
+CLASSES = 2 * PART
 ROWS = 16
 VMEM = pl.BlockSpec(memory_space=pltpu.VMEM)
 SMEM = pl.BlockSpec(memory_space=pltpu.SMEM)
@@ -46,23 +47,29 @@
     return [(y * 2 + c, (y + (step if c == 0 else -step)) % SIDE * 2 + c) for y in range(SIDE) for c in range(2)]
 
 
-def class_rows(place_ref, rows_ref):
+def half_rows(half, rows_ref):
+    return rows_ref[:, half].reshape(-1, rows_ref.shape[-1])
+
+
+def put(index, here, total, out_ref):
+    out_ref[index, ..., here] = total.astype(out_ref.dtype).reshape(out_ref.shape[1:-1] + (total.shape[-1],))
+
+
+def class_dot(index, place_ref, rows_ref, masked_ref, tiles, kept_ref, away_ref):
     rep = place_ref[0]
-    depth = rows_ref.shape[-1]
-    parts = [rows_ref[:, half].reshape(-1, depth) for half in (rep, 1 - rep)]
-    return jnp.concatenate(parts, axis=0)
-
-
-def put(index, here, total, kept_ref, away_ref):
-    total = total.astype(kept_ref.dtype).reshape((2,) + kept_ref.shape[1:-1] + (total.shape[-1],))
-    kept_ref[index, ..., here] = total[0]
-    away_ref[index % away_ref.shape[0], ..., here] = total[1]
+    rows = jnp.concatenate([half_rows(half, rows_ref) for half in (rep, 1 - rep)], axis=0)
+    for here in tiles:
+        total = jnp.dot(rows, masked_ref[:, here], preferred_element_type=jnp.float32)
+        put(index, here, total[: rows.shape[0] // 2], kept_ref)
+        put(index, here, total[rows.shape[0] // 2 :], away_ref)
+
+
+def col_tiles(cols, width=256):
+    return [slice(start, start + width) for start in range(0, cols, width)]
 
 
 def first_kernel(place_ref, bits_hbm, ints_hbm, rows_ref, kept_ref, away_ref, masked_ref, bits_ref, ints_ref, sems):
-    cols = ints_ref.shape[1]
-    width = 256
-    tiles = [slice(start, start + width) for start in range(0, cols, width)]
+    tiles = col_tiles(ints_ref.shape[1])
     bits_copy = pltpu.make_async_copy(bits_hbm, bits_ref, sems.at[len(tiles)])
     bits_copy.start()
     copies = [
@@ -70,7 +77,6 @@
     ]
     for copy in copies:
         copy.start()
-    rows = class_rows(place_ref, rows_ref)
     bits_copy.wait()
     for here, copy in zip(tiles, copies):
         copy.wait()
@@ -79,8 +85,7 @@
                 tile = (slice(q * TILE, (q + 1) * TILE), slice(p * TILE, (p + 1) * TILE))
                 bit = jnp.broadcast_to(bits_ref[q : q + 1, p : p + 1], (TILE, TILE))
                 masked_ref[tile] = ints_ref[tile] * bit.astype(jnp.float32).astype(ints_ref.dtype)
-        total = jnp.dot(rows, masked_ref[:, here], preferred_element_type=jnp.float32)
-        put(0, here, total, kept_ref, away_ref)
+        class_dot(0, place_ref, rows_ref, masked_ref, [here], kept_ref, away_ref)
 
 
 def sums_shape(rows, cols, classes=CLASSES):
@@ -96,7 +101,7 @@
         out_specs=[VMEM, VMEM, VMEM],
         out_shape=[
             sums_shape(rows, cols),
-            sums_shape(rows, cols, CLASSES - 1),
+            sums_shape(rows, cols, PART),
             jax.ShapeDtypeStruct(ints.shape, ints.dtype),
         ],
         scratch_shapes=[
@@ -111,30 +116,49 @@
     )(place, bits, ints, rows)
 
 
-def dot_kernel(index, place_ref, rows_ref, masked_ref, *refs):
-    kept_ref, away_ref = refs[-2:]
-    width = 256
-    rows = class_rows(place_ref, rows_ref)
-    for start in range(0, masked_ref.shape[1], width):
-        here = slice(start, start + width)
-        total = jnp.dot(rows, masked_ref[:, here], preferred_element_type=jnp.float32)
-        put(index, here, total, kept_ref, away_ref)
-
-
-def dot(place, index, rows, masked, *sums):
+def second_kernel(place_ref, rows_ref, masked_ref, _, __, kept_ref, away_ref):
+    class_dot(1, place_ref, rows_ref, masked_ref, col_tiles(masked_ref.shape[1]), kept_ref, away_ref)
+
+
+def second_dot(place, rows, masked, kept, away):
     cols = masked.shape[1]
-    away = sums_shape(rows, cols, CLASSES - 1 if len(sums) == 2 else 1)
-    return pl.pallas_call(
-        functools.partial(dot_kernel, index),
-        in_specs=[SMEM] + [VMEM] * (2 + len(sums)),
+    return pl.pallas_call(
+        second_kernel,
+        in_specs=[SMEM] + [VMEM] * 4,
         out_specs=[VMEM, VMEM],
-        out_shape=[sums_shape(rows, cols), away],
-        input_output_aliases={3 + i: i for i in range(len(sums))},
+        out_shape=[sums_shape(rows, cols), sums_shape(rows, cols, PART)],
+        input_output_aliases={3: 0, 4: 1},
         compiler_params=pltpu.CompilerParams(vmem_limit_bytes=16 * 1024 * 1024),
         cost_estimate=pl.CostEstimate(
             flops=rows.size * cols * 2, bytes_accessed=2 * rows.size + 2 * masked.size, transcendentals=0
         ),
-    )(place, rows, masked, *sums)
+    )(place, rows, masked, kept, away)
+
+
+def last_kernel(other, first, place_ref, side_ref, corner_ref, masked_ref, *refs):
+    out_ref = refs[-1]
+    rep = place_ref[0]
+    half = 1 - rep if other else rep
+    rows = jnp.concatenate([half_rows(half, ref) for ref in (side_ref, corner_ref)], axis=0)
+    for here in col_tiles(masked_ref.shape[1]):
+        total = jnp.dot(rows, masked_ref[:, here], preferred_element_type=jnp.float32)
+        for i in range(PART):
+            put(first + i, here, total[i * rows.shape[0] // PART : (i + 1) * rows.shape[0] // PART], out_ref)
+
+
+def last_dot(place, other, side, corner, masked, *kept):
+    cols = masked.shape[1]
+    return pl.pallas_call(
+        functools.partial(last_kernel, other, 0 if other else PART),
+        in_specs=[SMEM] + [VMEM] * (3 + len(kept)),
+        out_specs=VMEM,
+        out_shape=sums_shape(side, cols, PART if other else CLASSES),
+        input_output_aliases={} if other else {4: 0},
+        compiler_params=pltpu.CompilerParams(vmem_limit_bytes=16 * 1024 * 1024),
+        cost_estimate=pl.CostEstimate(
+            flops=side.size * cols * 2, bytes_accessed=2 * side.size + 2 * masked.size, transcendentals=0
+        ),
+    )(place, side, corner, masked, *kept)
 
 
 def share_kernel(steps, place_ref, kept_ref, early_ref, late_ref, *out_refs):
@@ -147,10 +171,7 @@
         a = index >> 1
         for dx in range(2):
             one = kept_ref[2 * dz + dx, a]
-            if dx == 0:
-                other = early_ref[2 * dz, a]
-            else:
-                other = jnp.where(dz == 0, early_ref[1, a], late_ref[0, a])
+            other = jnp.where(dz == 0, early_ref[dx, a], late_ref[dx, a])
             out_ref[i, :, (x + dx) & 1] = (one.astype(jnp.float32) + other.astype(jnp.float32)).astype(one.dtype)
 
 
@@ -180,13 +201,12 @@
     mine = lax.all_to_all(copies, ("owner", "rep"), 0, 0, axis_index_groups=far_groups(), tiled=True)
     mine = mine.reshape(FAR, 2, 2, ROWS, depth)
     near = [lax.ppermute(mine, ("owner", "rep"), near_pairs(dz, dx)) for dz, dx in ((0, 1), (1, 0), (1, 1))]
+    swap = [(0, 1), (1, 0)]
     kept, early, masked = first_dot(place, bits, ints, mine)
-    kept, early = dot(place, 1, near[0], masked, kept, early)
-    kept, early = dot(place, 2, near[1], masked, kept, early)
-    swap = [(0, 1), (1, 0)]
+    kept, early = second_dot(place, near[0], masked, kept, early)
     early = lax.ppermute(early, "rep", swap)
-    kept, late = dot(place, 3, near[2], masked, kept)
-    late = lax.ppermute(late, "rep", swap)
+    late = lax.ppermute(last_dot(place, True, near[1], near[2], masked), "rep", swap)
+    kept = last_dot(place, False, near[1], near[2], masked, kept)
 
     def along(step, part):
         return lax.ppermute(part, ("red", "rep"), red_step(step))

time: 98.8 us -> 96 us (0.972)
  starting transfers between devices: 37.4 us -> 35.9 us
  waiting for transfers between devices: 9.24 us -> 7.97 us
    ppermute x1, starting transfers between devices: 5.28 us -> 3.15 us  [per_device(): early = lax.ppermute(early, 'rep', swap)]
    ppermute x1, waiting for transfers between devices: 1.5 us -> 0.24 us  [per_device(): lax.ppermute(last_dot(place, True, near[1], near[2], masked), 'rep', swap)]
  transfers between devices with their start and end apart: 10 -> 10, of which waited for: 4 -> 3; matrix products, arithmetic and copies ran while one was open for 0% -> 0% of each run, Pallas kernels for 7% -> 7%
where the time goes in v4:
time: 96 us; the launch traced here: 95.5 us
  blocking collectives  39.6 us (41%)
  starting transfers between devices  35.9 us (37%)
  waiting for transfers between devices  7.97 us (8%)
  Pallas kernels  7.76 us (8%)
  local copies, waits for them, and re-layouts  3.08 us (3%)
    all_to_all x1, blocking collectives, per_device(): lax.all_to_all(copies, ('owner', 'rep'), 0, 0, axis_index_groups=far_grou...  39.6 us
    ppermute x5, starting transfers between devices, along(): return lax.ppermute(part, ('red', 'rep'), red_step(step))  19.4 us
    ppermute x3, starting transfers between devices, per_device(): lax.ppermute(mine, ('owner', 'rep'), near_pairs(dz, dx))  10.8 us
    ppermute x5, waiting for transfers between devices, along(): return lax.ppermute(part, ('red', 'rep'), red_step(step))  7.72 us
    pallas_call x1, Pallas kernels, first_dot(): pl.pallas_call(first_kernel, in_specs=[SMEM, HBM, HBM, VMEM], out_specs=[...  3.18 us
    ppermute x1, starting transfers between devices, per_device(): early = lax.ppermute(early, 'rep', swap)  3.15 us
    ppermute x1, starting transfers between devices, per_device(): lax.ppermute(last_dot(place, True, near[1], near[2], masked), 'rep', swap)  2.56 us
    pallas_call x2, Pallas kernels, last_dot(): pl.pallas_call(functools.partial(last_kernel, other, 0 if other else PART...  2.5 us
  transfers between devices with their start and end apart: 10, of which 3 were waited for; matrix products, arithmetic and copies ran while one was open for 0% of the time, Pallas kernels for 7%

profile of v4, /device:TPU:1, one launch (start us, length us, event | category | flops | bytes accessed | tf_op | source)
XLA Modules:
  0.0 95.5 jit_solution(3609082635761632153)
XLA Ops:
  0.0 0.8 broadcast_in_dim.2
  0.8 39.6 %all_to_all.5 = bf16[16,16,1024]{2,1,0:T(8,128)(2,1)S(1)} all-to-all(bf16[16,16,1024]{2,1,0:T(8,128)(2,1)S(1)} %broadcast_in_dim.2), channel_id=1, replica_groups={{0,32,64,96,256,288,320,352,512,544,576,608,768,800,832,864},{16,48,80,..., dimensions={0} | all-to-all | bytes 1048576 | tf_op jit(solution)/shard_map/all_to_all | solution.py:201
  40.5 1.9 %collective-permute-start.2 = (bf16[4,2,2,16,1024]{4,3,2,1,0:T(8,128)(2,1)S(1)}, bf16[4,2,2,16,1024]{4,3,2,1,0:T(8,128)(2,1)S(1)}, u32[]{:S(2)}, u32[]{:S(2)}) collective-permute-start(bf16[4,2,2,16,1024]{4,3,2,1,0:T(8,128)(2,1)S(1)} %bitcast.16), channel_id=1, source_target_pairs={{0,16},{1,113},{16,0},{17,33},{32,48},{33,17},{48,32},{49,65},{64,... | collective-permute-start | bytes 1572872 | tf_op jit(solution)/shard_map/ppermute | solution.py:203
  42.4 4.4 %collective-permute-start = (bf16[4,2,2,16,1024]{4,3,2,1,0:T(8,128)(2,1)S(1)}, bf16[4,2,2,16,1024]{4,3,2,1,0:T(8,128)(2,1)S(1)}, u32[]{:S(2)}, u32[]{:S(2)}) collective-permute-start(bf16[4,2,2,16,1024]{4,3,2,1,0:T(8,128)(2,1)S(1)} %bitcast.17), channel_id=1, source_target_pairs={{0,128},{1,897},{16,144},{17,913},{32,160},{33,929},{48,176},{49,9... | collective-permute-start | bytes 1572872 | tf_op jit(solution)/shard_map/ppermute | solution.py:203
  46.8 4.4 %collective-permute-start.1 = (bf16[4,2,2,16,1024]{4,3,2,1,0:T(8,128)(2,1)S(1)}, bf16[4,2,2,16,1024]{4,3,2,1,0:T(8,128)(2,1)S(1)}, u32[]{:S(2)}, u32[]{:S(2)}) collective-permute-start(bf16[4,2,2,16,1024]{4,3,2,1,0:T(8,128)(2,1)S(1)} %bitcast.18), channel_id=1, source_target_pairs={{0,144},{1,1009},{16,128},{17,929},{32,176},{33,913},{48,160},{49,... | collective-permute-start | bytes 1572872 | tf_op jit(solution)/shard_map/ppermute | solution.py:203
  51.3 0.1 pad_add_fusion.place_ref
  51.4 0.0 copy-start
  51.4 1.6 %copy-done = bf16[1024,1024]{1,0:T(8,128)(2,1)S(1)} copy-done((bf16[1024,1024]{1,0:T(8,128)(2,1)S(1)}, bf16[1024,1024]{1,0:T(8,128)(2,1)}, u32[]{:S(2)}) %copy-start) | copy-done | bytes 2097176
  52.9 0.0 copy-start.1
  52.9 0.7 copy-done.1
  53.6 3.2 %shard_map.37 = (bf16[4,4,2,16,1024]{4,3,2,1,0:T(8,128)(2,1)S(1)}, bf16[2,4,2,16,1024]{4,3,2,1,0:T(8,128)(2,1)S(1)}, bf16[1024,1024]{1,0:T(8,128)(2,1)S(1)}) custom-call(s32[4]{0:T(128)S(1)} %pad_add_fusion.place_ref, s32[8,8]{1,0:T(8,128)S(1)} %copy-done.1, bf16[1024,1024]{1,0:T(8,128)(2,1)S(1)} %copy-done, bf16[4,2,2,16,1024]{4,3,2,1,0:T(8,128)(2,1)S(1)} %bitcast.19), custom_call_target="tpu_custom_call" | custom-call | flops 536870912 | bytes 4718592 | tf_op jit(solution)/shard_map/pallas_call | solution.py:98
  56.8 0.0 collective-permute-done.2.rows_ref
  56.8 1.3 %shard_map.38 = (bf16[4,4,2,16,1024]{4,3,2,1,0:T(8,128)(2,1)S(1)}, bf16[2,4,2,16,1024]{4,3,2,1,0:T(8,128)(2,1)S(1)}) custom-call(s32[4]{0:T(128)S(1)} %pad_add_fusion.place_ref, bf16[4,2,2,16,1024]{4,3,2,1,0:T(8,128)(2,1)S(1)} %collective-permute-done.2.rows_ref, ...), custom_call_target="tpu_custom_call", output_to_operand_aliasing={{0}: (3, {}), {1}: (4, {})} | custom-call | flops 536870912 | bytes 2621440 | tf_op jit(solution)/shard_map/pallas_call | solution.py:125
  58.1 3.1 %collective-permute-start.3 = (bf16[2,4,2,16,1024]{4,3,2,1,0:T(8,128)(2,1)S(1)}, bf16[2,4,2,16,1024]{4,3,2,1,0:T(8,128)(2,1)S(1)}, u32[]{:S(2)}, u32[]{:S(2)}) collective-permute-start(bf16[2,4,2,16,1024]{4,3,2,1,0:T(8,128)(2,1)S(1)} %get-tuple-element.20), channel_id=1, source_target_pairs={{0,1},{1,0},{2,3},{3,2},{4,5},{5,4},{6,7},{7,6},{8,9},{9,8},{10,11... | collective-permute-start | bytes 1572872 | tf_op jit(solution)/shard_map/ppermute | solution.py:207
  61.2 0.0 collective-permute-done.side_ref
  61.3 0.0 collective-permute-done.1.corner_ref
  61.3 1.3 %shard_map.40 = bf16[2,4,2,16,1024]{4,3,2,1,0:T(8,128)(2,1)S(1)} custom-call(s32[4]{0:T(128)S(1)} %pad_add_fusion.place_ref, bf16[4,2,2,16,1024]{4,3,2,1,0:T(8,128)(2,1)S(1)} %collective-permute-done.side_ref, bf16[4,2,2,16,1024]{4,3,2,1,0:T(8,128)(2,1)S(1)} %collective-permute-done.1.corner_ref, bf16[1024,1024]{1,0:T(8,128)(2,1)S(1)} %get-tuple-element.16.masked_ref), custom_call_target="tpu_custom_call" | custom-call | flops 536870912 | bytes 2621440 | tf_op jit(solution)/shard_map/pallas_call | solution.py:151
  62.5 2.6 %collective-permute-start.4 = (bf16[2,4,2,16,1024]{4,3,2,1,0:T(8,128)(2,1)S(1)}, bf16[2,4,2,16,1024]{4,3,2,1,0:T(8,128)(2,1)S(1)}, u32[]{:S(2)}, u32[]{:S(2)}) collective-permute-start(bf16[2,4,2,16,1024]{4,3,2,1,0:T(8,128)(2,1)S(1)} %shard_map.40), channel_id=1, source_target_pairs={{0,1},{1,0},{2,3},{3,2},{4,5},{5,4},{6,7},{7,6},{8,9},{9,8},{10,11... | collective-permute-start | bytes 1572872 | tf_op jit(solution)/shard_map/ppermute | solution.py:208
  65.1 1.3 %shard_map.39.kept_ref = bf16[4,4,2,16,1024]{4,3,2,1,0:T(8,128)(2,1)S(1)} custom-call(s32[4]{0:T(128)S(1)} %pad_add_fusion.place_ref, bf16[4,2,2,16,1024]{4,3,2,1,0:T(8,128)(2,1)S(1)} %collective-permute-done.side_ref, bf16[4,2,2,16,1024]{4,3,2,1,0:T(8,128)(2,1)S(1)} %collective-permute-done.1.corner_ref, ...), custom_call_target="tpu_custom_call", output_to_operand_aliasing={{}: (4, {})} | custom-call | flops 536870912 | bytes 2621440 | tf_op jit(solution)/shard_map/pallas_call | solution.py:151
  66.4 0.0 collective-permute-done.3.early_ref
  66.4 0.2 collective-permute-done.4.late_ref
  66.6 0.8 shard_map.41
  67.4 3.3 %collective-permute-start.5 = (bf16[2,2,2,16,1024]{4,3,2,1,0:T(8,128)(2,1)S(1)}, bf16[2,2,2,16,1024]{4,3,2,1,0:T(8,128)(2,1)S(1)}, u32[]{:S(2)}, u32[]{:S(2)}) collective-permute-start(bf16[2,2,2,16,1024]{4,3,2,1,0:T(8,128)(2,1)S(1)} %get-tuple-element.22), channel_id=1, source_target_pairs={{0,14},{1,3},{2,0},{3,5},{4,2},{5,7},{6,4},{7,9},{8,6},{9,11},{10,... | collective-permute-start | bytes 786440 | tf_op jit(solution)/shard_map/ppermute | solution.py:212
  70.8 4.5 %collective-permute-start.6 = (bf16[2,2,2,16,1024]{4,3,2,1,0:T(8,128)(2,1)S(1)}, bf16[2,2,2,16,1024]{4,3,2,1,0:T(8,128)(2,1)S(1)}, u32[]{:S(2)}, u32[]{:S(2)}) collective-permute-start(bf16[2,2,2,16,1024]{4,3,2,1,0:T(8,128)(2,1)S(1)} %get-tuple-element.23), channel_id=1, source_target_pairs={{0,2},{1,15},{2,4},{3,1},{4,6},{5,3},{6,8},{7,5},{8,10},{9,7},{10,... | collective-permute-start | bytes 786440 | tf_op jit(solution)/shard_map/ppermute | solution.py:212
  75.3 1.9 %collective-permute-start.7 = (bf16[1,2,2,16,1024]{4,3,2,1,0:T(8,128)(2,1)S(1)}, bf16[1,2,2,16,1024]{4,3,2,1,0:T(8,128)(2,1)S(1)}, u32[]{:S(2)}, u32[]{:S(2)}) collective-permute-start(bf16[1,2,2,16,1024]{4,3,2,1,0:T(8,128)(2,1)S(1)} %get-tuple-element.24), channel_id=1, source_target_pairs={{0,12},{1,5},{2,14},{3,7},{4,0},{5,9},{6,2},{7,11},{8,4},{9,13},{1... | collective-permute-start | bytes 393224 | tf_op jit(solution)/shard_map/ppermute | solution.py:212
  77.2 0.0 collective-permute-done.5
  77.3 5.9 %collective-permute-start.8 = (bf16[2,2,16,1024]{3,2,1,0:T(8,128)(2,1)S(1)}, bf16[2,2,16,1024]{3,2,1,0:T(8,128)(2,1)S(1)}, u32[]{:S(2)}, u32[]{:S(2)}) collective-permute-start(bf16[2,2,16,1024]{3,2,1,0:T(8,128)(2,1)S(1)} %fusion.2), channel_id=1, source_target_pairs={{0,10},{1,7},{2,12},{3,9},{4,14},{5,11},{6,0},{7,13},{8,2},{9,15},... | collective-permute-start | bytes 393224 | tf_op jit(solution)/shard_map/ppermute | solution.py:212
  83.1 0.0 collective-permute-done.6
  83.2 3.8 %collective-permute-start.9 = (bf16[2,2,16,1024]{3,2,1,0:T(8,128)(2,1)S(1)}, bf16[2,2,16,1024]{3,2,1,0:T(8,128)(2,1)S(1)}, u32[]{:S(2)}, u32[]{:S(2)}) collective-permute-start(bf16[2,2,16,1024]{3,2,1,0:T(8,128)(2,1)S(1)} %fusion.3), channel_id=1, source_target_pairs={{0,4},{1,13},{2,6},{3,15},{4,8},{5,1},{6,10},{7,3},{8,12},{9,5},{1... | collective-permute-start | bytes 393224 | tf_op jit(solution)/shard_map/ppermute | solution.py:212
  87.0 0.0 collective-permute-done.7
  87.0 1.9 %collective-permute-done.8 = bf16[2,2,16,1024]{3,2,1,0:T(8,128)(2,1)S(1)} collective-permute-done((bf16[2,2,16,1024]{3,2,1,0:T(8,128)(2,1)S(1)}, bf16[2,2,16,1024]{3,2,1,0:T(8,128)(2,1)S(1)}, u32[]{:S(2)}, u32[]{:S(2)}) %collective-permute-start.8) | collective-permute-done | bytes 131104 | tf_op jit(solution)/shard_map/ppermute | solution.py:212
  89.0 5.8 %collective-permute-done.9 = bf16[2,2,16,1024]{3,2,1,0:T(8,128)(2,1)S(1)} collective-permute-done((bf16[2,2,16,1024]{3,2,1,0:T(8,128)(2,1)S(1)}, bf16[2,2,16,1024]{3,2,1,0:T(8,128)(2,1)S(1)}, u32[]{:S(2)}, u32[]{:S(2)}) %collective-permute-start.9) | collective-permute-done | bytes 131104 | tf_op jit(solution)/shard_map/ppermute | solution.py:212
  94.7 0.8 fusion.1
  (2 shorter events, 0.1 us)
Async XLA Ops:
  40.5 16.4 %collective-permute-start.2 = (bf16[4,2,2,16,1024]{4,3,2,1,0:T(8,128)(2,1)S(1)}, bf16[4,2,2,16,1024]{4,3,2,1,0:T(8,128)(2,1)S(1)}, u32[]{:S(2)}, u32[]{:S(2)}) collective-permute-start(bf16[4,2,2,16,1024]{4,3,2,1,0:T(8,128)(2,1)S(1)} %bitcast.16), channel_id=1, source_target_pairs={{0,16},{1,113},{16,0},{17,33},{32,48},{33,17},{48,32},{49,65},{64,... | collective-permute-start | bytes 1572872 | tf_op jit(solution)/shard_map/ppermute | solution.py:203
  42.4 18.9 %collective-permute-start = (bf16[4,2,2,16,1024]{4,3,2,1,0:T(8,128)(2,1)S(1)}, bf16[4,2,2,16,1024]{4,3,2,1,0:T(8,128)(2,1)S(1)}, u32[]{:S(2)}, u32[]{:S(2)}) collective-permute-start(bf16[4,2,2,16,1024]{4,3,2,1,0:T(8,128)(2,1)S(1)} %bitcast.17), channel_id=1, source_target_pairs={{0,128},{1,897},{16,144},{17,913},{32,160},{33,929},{48,176},{49,9... | collective-permute-start | bytes 1572872 | tf_op jit(solution)/shard_map/ppermute | solution.py:203
  46.8 14.4 %collective-permute-start.1 = (bf16[4,2,2,16,1024]{4,3,2,1,0:T(8,128)(2,1)S(1)}, bf16[4,2,2,16,1024]{4,3,2,1,0:T(8,128)(2,1)S(1)}, u32[]{:S(2)}, u32[]{:S(2)}) collective-permute-start(bf16[4,2,2,16,1024]{4,3,2,1,0:T(8,128)(2,1)S(1)} %bitcast.18), channel_id=1, source_target_pairs={{0,144},{1,1009},{16,128},{17,929},{32,176},{33,913},{48,160},{49,... | collective-permute-start | bytes 1572872 | tf_op jit(solution)/shard_map/ppermute | solution.py:203
  51.4 1.6 %copy-start = (bf16[1024,1024]{1,0:T(8,128)(2,1)S(1)}, bf16[1024,1024]{1,0:T(8,128)(2,1)}, u32[]{:S(2)}) copy-start(bf16[1024,1024]{1,0:T(8,128)(2,1)} %ints_hbm.1) | copy-start | bytes 6291460
  52.9 0.7 copy-start.1
  58.1 8.3 %collective-permute-start.3 = (bf16[2,4,2,16,1024]{4,3,2,1,0:T(8,128)(2,1)S(1)}, bf16[2,4,2,16,1024]{4,3,2,1,0:T(8,128)(2,1)S(1)}, u32[]{:S(2)}, u32[]{:S(2)}) collective-permute-start(bf16[2,4,2,16,1024]{4,3,2,1,0:T(8,128)(2,1)S(1)} %get-tuple-element.20), channel_id=1, source_target_pairs={{0,1},{1,0},{2,3},{3,2},{4,5},{5,4},{6,7},{7,6},{8,9},{9,8},{10,11... | collective-permute-start | bytes 1572872 | tf_op jit(solution)/shard_map/ppermute | solution.py:207
  62.5 4.1 %collective-permute-start.4 = (bf16[2,4,2,16,1024]{4,3,2,1,0:T(8,128)(2,1)S(1)}, bf16[2,4,2,16,1024]{4,3,2,1,0:T(8,128)(2,1)S(1)}, u32[]{:S(2)}, u32[]{:S(2)}) collective-permute-start(bf16[2,4,2,16,1024]{4,3,2,1,0:T(8,128)(2,1)S(1)} %shard_map.40), channel_id=1, source_target_pairs={{0,1},{1,0},{2,3},{3,2},{4,5},{5,4},{6,7},{7,6},{8,9},{9,8},{10,11... | collective-permute-start | bytes 1572872 | tf_op jit(solution)/shard_map/ppermute | solution.py:208
  67.4 9.8 %collective-permute-start.5 = (bf16[2,2,2,16,1024]{4,3,2,1,0:T(8,128)(2,1)S(1)}, bf16[2,2,2,16,1024]{4,3,2,1,0:T(8,128)(2,1)S(1)}, u32[]{:S(2)}, u32[]{:S(2)}) collective-permute-start(bf16[2,2,2,16,1024]{4,3,2,1,0:T(8,128)(2,1)S(1)} %get-tuple-element.22), channel_id=1, source_target_pairs={{0,14},{1,3},{2,0},{3,5},{4,2},{5,7},{6,4},{7,9},{8,6},{9,11},{10,... | collective-permute-start | bytes 786440 | tf_op jit(solution)/shard_map/ppermute | solution.py:212
  70.8 12.4 %collective-permute-start.6 = (bf16[2,2,2,16,1024]{4,3,2,1,0:T(8,128)(2,1)S(1)}, bf16[2,2,2,16,1024]{4,3,2,1,0:T(8,128)(2,1)S(1)}, u32[]{:S(2)}, u32[]{:S(2)}) collective-permute-start(bf16[2,2,2,16,1024]{4,3,2,1,0:T(8,128)(2,1)S(1)} %get-tuple-element.23), channel_id=1, source_target_pairs={{0,2},{1,15},{2,4},{3,1},{4,6},{5,3},{6,8},{7,5},{8,10},{9,7},{10,... | collective-permute-start | bytes 786440 | tf_op jit(solution)/shard_map/ppermute | solution.py:212
  75.3 11.7 %collective-permute-start.7 = (bf16[1,2,2,16,1024]{4,3,2,1,0:T(8,128)(2,1)S(1)}, bf16[1,2,2,16,1024]{4,3,2,1,0:T(8,128)(2,1)S(1)}, u32[]{:S(2)}, u32[]{:S(2)}) collective-permute-start(bf16[1,2,2,16,1024]{4,3,2,1,0:T(8,128)(2,1)S(1)} %get-tuple-element.24), channel_id=1, source_target_pairs={{0,12},{1,5},{2,14},{3,7},{4,0},{5,9},{6,2},{7,11},{8,4},{9,13},{1... | collective-permute-start | bytes 393224 | tf_op jit(solution)/shard_map/ppermute | solution.py:212
  77.3 11.7 %collective-permute-start.8 = (bf16[2,2,16,1024]{3,2,1,0:T(8,128)(2,1)S(1)}, bf16[2,2,16,1024]{3,2,1,0:T(8,128)(2,1)S(1)}, u32[]{:S(2)}, u32[]{:S(2)}) collective-permute-start(bf16[2,2,16,1024]{3,2,1,0:T(8,128)(2,1)S(1)} %fusion.2), channel_id=1, source_target_pairs={{0,10},{1,7},{2,12},{3,9},{4,14},{5,11},{6,0},{7,13},{8,2},{9,15},... | collective-permute-start | bytes 393224 | tf_op jit(solution)/shard_map/ppermute | solution.py:212
  83.2 11.5 %collective-permute-start.9 = (bf16[2,2,16,1024]{3,2,1,0:T(8,128)(2,1)S(1)}, bf16[2,2,16,1024]{3,2,1,0:T(8,128)(2,1)S(1)}, u32[]{:S(2)}, u32[]{:S(2)}) collective-permute-start(bf16[2,2,16,1024]{3,2,1,0:T(8,128)(2,1)S(1)} %fusion.3), channel_id=1, source_target_pairs={{0,4},{1,13},{2,6},{3,15},{4,8},{5,1},{6,10},{7,3},{8,12},{9,5},{1... | collective-permute-start | bytes 393224 | tf_op jit(solution)/shard_map/ppermute | solution.py:212

commit v5 on v4

--- a/solution.py
+++ b/solution.py
@@ -15,7 +15,6 @@
 ROWS = 16
 VMEM = pl.BlockSpec(memory_space=pltpu.VMEM)
 SMEM = pl.BlockSpec(memory_space=pltpu.SMEM)
-HBM = pl.BlockSpec(memory_space=pltpu.HBM)
 
 
 def member(z, x, core):
@@ -44,7 +43,7 @@
 
 
 def red_step(step):
-    return [(y * 2 + c, (y + (step if c == 0 else -step)) % SIDE * 2 + c) for y in range(SIDE) for c in range(2)]
+    return [(y * 2 + c, (y + (-step if c == 0 else step)) % SIDE * 2 + c) for y in range(SIDE) for c in range(2)]
 
 
 def half_rows(half, rows_ref):
@@ -68,18 +67,8 @@
     return [slice(start, start + width) for start in range(0, cols, width)]
 
 
-def first_kernel(place_ref, bits_hbm, ints_hbm, rows_ref, kept_ref, away_ref, masked_ref, bits_ref, ints_ref, sems):
-    tiles = col_tiles(ints_ref.shape[1])
-    bits_copy = pltpu.make_async_copy(bits_hbm, bits_ref, sems.at[len(tiles)])
-    bits_copy.start()
-    copies = [
-        pltpu.make_async_copy(ints_hbm.at[:, here], ints_ref.at[:, here], sems.at[i]) for i, here in enumerate(tiles)
-    ]
-    for copy in copies:
-        copy.start()
-    bits_copy.wait()
-    for here, copy in zip(tiles, copies):
-        copy.wait()
+def first_kernel(place_ref, bits_ref, ints_ref, rows_ref, kept_ref, away_ref, masked_ref):
+    for here in col_tiles(ints_ref.shape[1]):
         for q in range(ints_ref.shape[0] // TILE):
             for p in range(here.start // TILE, here.stop // TILE):
                 tile = (slice(q * TILE, (q + 1) * TILE), slice(p * TILE, (p + 1) * TILE))
@@ -94,20 +83,15 @@
 
 
 def first_dot(place, bits, ints, rows):
-    depth, cols = ints.shape
+    cols = ints.shape[1]
     return pl.pallas_call(
         first_kernel,
-        in_specs=[SMEM, HBM, HBM, VMEM],
+        in_specs=[SMEM, VMEM, VMEM, VMEM],
         out_specs=[VMEM, VMEM, VMEM],
         out_shape=[
             sums_shape(rows, cols),
             sums_shape(rows, cols, PART),
             jax.ShapeDtypeStruct(ints.shape, ints.dtype),
-        ],
-        scratch_shapes=[
-            pltpu.VMEM(bits.shape, bits.dtype),
-            pltpu.VMEM(ints.shape, ints.dtype),
-            pltpu.SemaphoreType.DMA((cols // 256 + 1,)),
         ],
         compiler_params=pltpu.CompilerParams(vmem_limit_bytes=16 * 1024 * 1024),
         cost_estimate=pl.CostEstimate(
@@ -162,7 +146,7 @@
 
 
 def share_kernel(steps, place_ref, kept_ref, early_ref, late_ref, *out_refs):
-    z, x, y, way = place_ref[1], place_ref[2], place_ref[3], 1 - 2 * place_ref[0]
+    z, x, y, way = place_ref[1], place_ref[2], place_ref[3], 2 * place_ref[0] - 1
     flat = [step for group in steps for step in group]
     outs = [(ref, i) for ref, group in zip(out_refs, steps) for i in range(len(group))]
     for step, (out_ref, i) in zip(flat, outs):
@@ -170,8 +154,8 @@
         dz = (index ^ z) & 1
         a = index >> 1
         for dx in range(2):
-            one = kept_ref[2 * dz + dx, a]
-            other = jnp.where(dz == 0, early_ref[dx, a], late_ref[dx, a])
+            one = jnp.where(dz == 0, kept_ref[2 * dx, a], kept_ref[3 - 2 * dx, a])
+            other = jnp.where(dz == dx, early_ref[dx, a], late_ref[1 - dx, a])
             out_ref[i, :, (x + dx) & 1] = (one.astype(jnp.float32) + other.astype(jnp.float32)).astype(one.dtype)
 
 
@@ -200,7 +184,7 @@
     copies = jnp.broadcast_to(amps[None], (FAR * FAR,) + amps.shape)
     mine = lax.all_to_all(copies, ("owner", "rep"), 0, 0, axis_index_groups=far_groups(), tiled=True)
     mine = mine.reshape(FAR, 2, 2, ROWS, depth)
-    near = [lax.ppermute(mine, ("owner", "rep"), near_pairs(dz, dx)) for dz, dx in ((0, 1), (1, 0), (1, 1))]
+    near = [lax.ppermute(mine, ("owner", "rep"), near_pairs(dz, dx)) for dz, dx in ((1, 1), (0, 1), (1, 0))]
     swap = [(0, 1), (1, 0)]
     kept, early, masked = first_dot(place, bits, ints, mine)
     kept, early = second_dot(place, near[0], masked, kept, early)

time: 96 us -> 94.5 us (0.984)
  Pallas kernels: 7.76 us -> 6.15 us
    pallas_call x1, Pallas kernels: 3.18 us -> 1.53 us  [first_dot(): pl.pallas_call(first_kernel, in_specs=[SMEM, VMEM, VMEM, VMEM], out_specs...]
  transfers between devices with their start and end apart: 10 -> 10, of which waited for: 3 -> 4; matrix products, arithmetic and copies ran while one was open for 0% -> 0% of each run, Pallas kernels for 7% -> 6%
where the time goes in v5:
time: 94.5 us; the launch traced here: 93.8 us
  blocking collectives  39.6 us (42%)
  starting transfers between devices  35.9 us (38%)
  waiting for transfers between devices  7.95 us (8%)
  Pallas kernels  6.15 us (7%)
  local copies, waits for them, and re-layouts  3.08 us (3%)
    all_to_all x1, blocking collectives, per_device(): lax.all_to_all(copies, ('owner', 'rep'), 0, 0, axis_index_groups=far_grou...  39.6 us
    ppermute x5, starting transfers between devices, along(): return lax.ppermute(part, ('red', 'rep'), red_step(step))  18.7 us
    ppermute x3, starting transfers between devices, per_device(): lax.ppermute(mine, ('owner', 'rep'), near_pairs(dz, dx))  10.8 us
    ppermute x5, waiting for transfers between devices, along(): return lax.ppermute(part, ('red', 'rep'), red_step(step))  6.96 us
    ppermute x1, starting transfers between devices, per_device(): lax.ppermute(last_dot(place, True, near[1], near[2], masked), 'rep', swap)  3.22 us
    ppermute x1, starting transfers between devices, per_device(): early = lax.ppermute(early, 'rep', swap)  3.15 us
    pallas_call x2, Pallas kernels, last_dot(): pl.pallas_call(functools.partial(last_kernel, other, 0 if other else PART...  2.5 us
    unnamed x4, local copies, waits for them, and re-layouts  2.28 us
  transfers between devices with their start and end apart: 10, of which 4 were waited for; matrix products, arithmetic and copies ran while one was open for 0% of the time, Pallas kernels for 6%

profile of v5, /device:TPU:1, one launch (start us, length us, event | category | flops | bytes accessed | tf_op | source)
XLA Modules:
  0.0 93.8 jit_solution(5007932290696176968)
XLA Ops:
  0.0 0.8 broadcast_in_dim.2
  0.8 39.6 %all_to_all.5 = bf16[16,16,1024]{2,1,0:T(8,128)(2,1)S(1)} all-to-all(bf16[16,16,1024]{2,1,0:T(8,128)(2,1)S(1)} %broadcast_in_dim.2), channel_id=1, replica_groups={{0,32,64,96,256,288,320,352,512,544,576,608,768,800,832,864},{16,48,80,..., dimensions={0} | all-to-all | bytes 1048576 | tf_op jit(solution)/shard_map/all_to_all | solution.py:185
  40.5 1.9 %collective-permute-start.2 = (bf16[4,2,2,16,1024]{4,3,2,1,0:T(8,128)(2,1)S(1)}, bf16[4,2,2,16,1024]{4,3,2,1,0:T(8,128)(2,1)S(1)}, u32[]{:S(2)}, u32[]{:S(2)}) collective-permute-start(bf16[4,2,2,16,1024]{4,3,2,1,0:T(8,128)(2,1)S(1)} %bitcast.16), channel_id=1, source_target_pairs={{0,144},{1,1009},{16,128},{17,929},{32,176},{33,913},{48,160},{49,... | collective-permute-start | bytes 1572872 | tf_op jit(solution)/shard_map/ppermute | solution.py:187
  42.4 6.8 %collective-permute-start = (bf16[4,2,2,16,1024]{4,3,2,1,0:T(8,128)(2,1)S(1)}, bf16[4,2,2,16,1024]{4,3,2,1,0:T(8,128)(2,1)S(1)}, u32[]{:S(2)}, u32[]{:S(2)}) collective-permute-start(bf16[4,2,2,16,1024]{4,3,2,1,0:T(8,128)(2,1)S(1)} %bitcast.17), channel_id=1, source_target_pairs={{0,16},{1,113},{16,0},{17,33},{32,48},{33,17},{48,32},{49,65},{64,... | collective-permute-start | bytes 1572872 | tf_op jit(solution)/shard_map/ppermute | solution.py:187
  49.2 2.1 %collective-permute-start.1 = (bf16[4,2,2,16,1024]{4,3,2,1,0:T(8,128)(2,1)S(1)}, bf16[4,2,2,16,1024]{4,3,2,1,0:T(8,128)(2,1)S(1)}, u32[]{:S(2)}, u32[]{:S(2)}) collective-permute-start(bf16[4,2,2,16,1024]{4,3,2,1,0:T(8,128)(2,1)S(1)} %bitcast.18), channel_id=1, source_target_pairs={{0,128},{1,897},{16,144},{17,913},{32,160},{33,929},{48,176},{49,9... | collective-permute-start | bytes 1572872 | tf_op jit(solution)/shard_map/ppermute | solution.py:187
  51.3 0.1 pad_add_fusion.place_ref
  51.4 0.0 copy-start
  51.4 1.6 %copy-done = bf16[1024,1024]{1,0:T(8,128)(2,1)S(1)} copy-done((bf16[1024,1024]{1,0:T(8,128)(2,1)S(1)}, bf16[1024,1024]{1,0:T(8,128)(2,1)}, u32[]{:S(2)}) %copy-start) | copy-done | bytes 2097176
  52.9 0.0 copy-start.1
  52.9 0.7 copy-done.1
  53.6 1.5 %shard_map.37 = (bf16[4,4,2,16,1024]{4,3,2,1,0:T(8,128)(2,1)S(1)}, bf16[2,4,2,16,1024]{4,3,2,1,0:T(8,128)(2,1)S(1)}, bf16[1024,1024]{1,0:T(8,128)(2,1)S(1)}) custom-call(s32[4]{0:T(128)S(1)} %pad_add_fusion.place_ref, s32[8,8]{1,0:T(8,128)S(1)} %copy-done.1, bf16[1024,1024]{1,0:T(8,128)(2,1)S(1)} %copy-done, bf16[4,2,2,16,1024]{4,3,2,1,0:T(8,128)(2,1)S(1)} %bitcast.19), custom_call_target="tpu_custom_call" | custom-call | flops 536870912 | bytes 4718592 | tf_op jit(solution)/shard_map/pallas_call | solution.py:87
  55.2 0.0 collective-permute-done.2.rows_ref
  55.2 1.3 %shard_map.38 = (bf16[4,4,2,16,1024]{4,3,2,1,0:T(8,128)(2,1)S(1)}, bf16[2,4,2,16,1024]{4,3,2,1,0:T(8,128)(2,1)S(1)}) custom-call(s32[4]{0:T(128)S(1)} %pad_add_fusion.place_ref, bf16[4,2,2,16,1024]{4,3,2,1,0:T(8,128)(2,1)S(1)} %collective-permute-done.2.rows_ref, ...), custom_call_target="tpu_custom_call", output_to_operand_aliasing={{0}: (3, {}), {1}: (4, {})} | custom-call | flops 536870912 | bytes 2621440 | tf_op jit(solution)/shard_map/pallas_call | solution.py:109
  56.4 3.2 %collective-permute-start.3 = (bf16[2,4,2,16,1024]{4,3,2,1,0:T(8,128)(2,1)S(1)}, bf16[2,4,2,16,1024]{4,3,2,1,0:T(8,128)(2,1)S(1)}, u32[]{:S(2)}, u32[]{:S(2)}) collective-permute-start(bf16[2,4,2,16,1024]{4,3,2,1,0:T(8,128)(2,1)S(1)} %get-tuple-element.20), channel_id=1, source_target_pairs={{0,1},{1,0},{2,3},{3,2},{4,5},{5,4},{6,7},{7,6},{8,9},{9,8},{10,11... | collective-permute-start | bytes 1572872 | tf_op jit(solution)/shard_map/ppermute | solution.py:191
  59.6 0.0 collective-permute-done.side_ref
  59.6 0.7 collective-permute-done.1.corner_ref
  60.3 1.2 %shard_map.40 = bf16[2,4,2,16,1024]{4,3,2,1,0:T(8,128)(2,1)S(1)} custom-call(s32[4]{0:T(128)S(1)} %pad_add_fusion.place_ref, bf16[4,2,2,16,1024]{4,3,2,1,0:T(8,128)(2,1)S(1)} %collective-permute-done.side_ref, bf16[4,2,2,16,1024]{4,3,2,1,0:T(8,128)(2,1)S(1)} %collective-permute-done.1.corner_ref, bf16[1024,1024]{1,0:T(8,128)(2,1)S(1)} %get-tuple-element.16.masked_ref), custom_call_target="tpu_custom_call" | custom-call | flops 536870912 | bytes 2621440 | tf_op jit(solution)/shard_map/pallas_call | solution.py:135
  61.6 3.2 %collective-permute-start.4 = (bf16[2,4,2,16,1024]{4,3,2,1,0:T(8,128)(2,1)S(1)}, bf16[2,4,2,16,1024]{4,3,2,1,0:T(8,128)(2,1)S(1)}, u32[]{:S(2)}, u32[]{:S(2)}) collective-permute-start(bf16[2,4,2,16,1024]{4,3,2,1,0:T(8,128)(2,1)S(1)} %shard_map.40), channel_id=1, source_target_pairs={{0,1},{1,0},{2,3},{3,2},{4,5},{5,4},{6,7},{7,6},{8,9},{9,8},{10,11... | collective-permute-start | bytes 1572872 | tf_op jit(solution)/shard_map/ppermute | solution.py:192
  64.8 1.3 %shard_map.39.kept_ref = bf16[4,4,2,16,1024]{4,3,2,1,0:T(8,128)(2,1)S(1)} custom-call(s32[4]{0:T(128)S(1)} %pad_add_fusion.place_ref, bf16[4,2,2,16,1024]{4,3,2,1,0:T(8,128)(2,1)S(1)} %collective-permute-done.side_ref, bf16[4,2,2,16,1024]{4,3,2,1,0:T(8,128)(2,1)S(1)} %collective-permute-done.1.corner_ref, ...), custom_call_target="tpu_custom_call", output_to_operand_aliasing={{}: (4, {})} | custom-call | flops 536870912 | bytes 2621440 | tf_op jit(solution)/shard_map/pallas_call | solution.py:135
  66.1 0.0 collective-permute-done.3.early_ref
  66.1 0.2 collective-permute-done.4.late_ref
  66.3 0.9 shard_map.41
  67.2 5.9 %collective-permute-start.5 = (bf16[2,2,2,16,1024]{4,3,2,1,0:T(8,128)(2,1)S(1)}, bf16[2,2,2,16,1024]{4,3,2,1,0:T(8,128)(2,1)S(1)}, u32[]{:S(2)}, u32[]{:S(2)}) collective-permute-start(bf16[2,2,2,16,1024]{4,3,2,1,0:T(8,128)(2,1)S(1)} %get-tuple-element.22), channel_id=1, source_target_pairs={{0,2},{1,15},{2,4},{3,1},{4,6},{5,3},{6,8},{7,5},{8,10},{9,7},{10,... | collective-permute-start | bytes 786440 | tf_op jit(solution)/shard_map/ppermute | solution.py:196
  73.1 1.9 %collective-permute-start.6 = (bf16[2,2,2,16,1024]{4,3,2,1,0:T(8,128)(2,1)S(1)}, bf16[2,2,2,16,1024]{4,3,2,1,0:T(8,128)(2,1)S(1)}, u32[]{:S(2)}, u32[]{:S(2)}) collective-permute-start(bf16[2,2,2,16,1024]{4,3,2,1,0:T(8,128)(2,1)S(1)} %get-tuple-element.23), channel_id=1, source_target_pairs={{0,14},{1,3},{2,0},{3,5},{4,2},{5,7},{6,4},{7,9},{8,6},{9,11},{10,... | collective-permute-start | bytes 786440 | tf_op jit(solution)/shard_map/ppermute | solution.py:196
  75.0 4.0 %collective-permute-start.7 = (bf16[1,2,2,16,1024]{4,3,2,1,0:T(8,128)(2,1)S(1)}, bf16[1,2,2,16,1024]{4,3,2,1,0:T(8,128)(2,1)S(1)}, u32[]{:S(2)}, u32[]{:S(2)}) collective-permute-start(bf16[1,2,2,16,1024]{4,3,2,1,0:T(8,128)(2,1)S(1)} %get-tuple-element.24), channel_id=1, source_target_pairs={{0,4},{1,13},{2,6},{3,15},{4,8},{5,1},{6,10},{7,3},{8,12},{9,5},{1... | collective-permute-start | bytes 393224 | tf_op jit(solution)/shard_map/ppermute | solution.py:196
  79.1 0.0 collective-permute-done.5
  79.1 4.5 %collective-permute-start.8 = (bf16[2,2,16,1024]{3,2,1,0:T(8,128)(2,1)S(1)}, bf16[2,2,16,1024]{3,2,1,0:T(8,128)(2,1)S(1)}, u32[]{:S(2)}, u32[]{:S(2)}) collective-permute-start(bf16[2,2,16,1024]{3,2,1,0:T(8,128)(2,1)S(1)} %fusion.2), channel_id=1, source_target_pairs={{0,6},{1,11},{2,8},{3,13},{4,10},{5,15},{6,12},{7,1},{8,14},{9,3},... | collective-permute-start | bytes 393224 | tf_op jit(solution)/shard_map/ppermute | solution.py:196
  83.7 0.0 collective-permute-done.6
  83.7 2.3 %collective-permute-start.9 = (bf16[2,2,16,1024]{3,2,1,0:T(8,128)(2,1)S(1)}, bf16[2,2,16,1024]{3,2,1,0:T(8,128)(2,1)S(1)}, u32[]{:S(2)}, u32[]{:S(2)}) collective-permute-start(bf16[2,2,16,1024]{3,2,1,0:T(8,128)(2,1)S(1)} %fusion.3), channel_id=1, source_target_pairs={{0,12},{1,5},{2,14},{3,7},{4,0},{5,9},{6,2},{7,11},{8,4},{9,13},{1... | collective-permute-start | bytes 393224 | tf_op jit(solution)/shard_map/ppermute | solution.py:196
  86.1 0.0 collective-permute-done.7
  86.1 0.9 %collective-permute-done.8 = bf16[2,2,16,1024]{3,2,1,0:T(8,128)(2,1)S(1)} collective-permute-done((bf16[2,2,16,1024]{3,2,1,0:T(8,128)(2,1)S(1)}, bf16[2,2,16,1024]{3,2,1,0:T(8,128)(2,1)S(1)}, u32[]{:S(2)}, u32[]{:S(2)}) %collective-permute-start.8) | collective-permute-done | bytes 131104 | tf_op jit(solution)/shard_map/ppermute | solution.py:196
  87.0 6.0 %collective-permute-done.9 = bf16[2,2,16,1024]{3,2,1,0:T(8,128)(2,1)S(1)} collective-permute-done((bf16[2,2,16,1024]{3,2,1,0:T(8,128)(2,1)S(1)}, bf16[2,2,16,1024]{3,2,1,0:T(8,128)(2,1)S(1)}, u32[]{:S(2)}, u32[]{:S(2)}) %collective-permute-start.9) | collective-permute-done | bytes 131104 | tf_op jit(solution)/shard_map/ppermute | solution.py:196
  93.0 0.8 fusion.1
  (2 shorter events, 0.1 us)
Async XLA Ops:
  40.5 14.7 %collective-permute-start.2 = (bf16[4,2,2,16,1024]{4,3,2,1,0:T(8,128)(2,1)S(1)}, bf16[4,2,2,16,1024]{4,3,2,1,0:T(8,128)(2,1)S(1)}, u32[]{:S(2)}, u32[]{:S(2)}) collective-permute-start(bf16[4,2,2,16,1024]{4,3,2,1,0:T(8,128)(2,1)S(1)} %bitcast.16), channel_id=1, source_target_pairs={{0,144},{1,1009},{16,128},{17,929},{32,176},{33,913},{48,160},{49,... | collective-permute-start | bytes 1572872 | tf_op jit(solution)/shard_map/ppermute | solution.py:187
  42.4 17.2 %collective-permute-start = (bf16[4,2,2,16,1024]{4,3,2,1,0:T(8,128)(2,1)S(1)}, bf16[4,2,2,16,1024]{4,3,2,1,0:T(8,128)(2,1)S(1)}, u32[]{:S(2)}, u32[]{:S(2)}) collective-permute-start(bf16[4,2,2,16,1024]{4,3,2,1,0:T(8,128)(2,1)S(1)} %bitcast.17), channel_id=1, source_target_pairs={{0,16},{1,113},{16,0},{17,33},{32,48},{33,17},{48,32},{49,65},{64,... | collective-permute-start | bytes 1572872 | tf_op jit(solution)/shard_map/ppermute | solution.py:187
  49.2 11.1 %collective-permute-start.1 = (bf16[4,2,2,16,1024]{4,3,2,1,0:T(8,128)(2,1)S(1)}, bf16[4,2,2,16,1024]{4,3,2,1,0:T(8,128)(2,1)S(1)}, u32[]{:S(2)}, u32[]{:S(2)}) collective-permute-start(bf16[4,2,2,16,1024]{4,3,2,1,0:T(8,128)(2,1)S(1)} %bitcast.18), channel_id=1, source_target_pairs={{0,128},{1,897},{16,144},{17,913},{32,160},{33,929},{48,176},{49,9... | collective-permute-start | bytes 1572872 | tf_op jit(solution)/shard_map/ppermute | solution.py:187
  51.4 1.6 %copy-start = (bf16[1024,1024]{1,0:T(8,128)(2,1)S(1)}, bf16[1024,1024]{1,0:T(8,128)(2,1)}, u32[]{:S(2)}) copy-start(bf16[1024,1024]{1,0:T(8,128)(2,1)} %ints_ref.1) | copy-start | bytes 6291460
  52.9 0.7 copy-start.1
  56.4 9.7 %collective-permute-start.3 = (bf16[2,4,2,16,1024]{4,3,2,1,0:T(8,128)(2,1)S(1)}, bf16[2,4,2,16,1024]{4,3,2,1,0:T(8,128)(2,1)S(1)}, u32[]{:S(2)}, u32[]{:S(2)}) collective-permute-start(bf16[2,4,2,16,1024]{4,3,2,1,0:T(8,128)(2,1)S(1)} %get-tuple-element.20), channel_id=1, source_target_pairs={{0,1},{1,0},{2,3},{3,2},{4,5},{5,4},{6,7},{7,6},{8,9},{9,8},{10,11... | collective-permute-start | bytes 1572872 | tf_op jit(solution)/shard_map/ppermute | solution.py:191
  61.6 4.7 %collective-permute-start.4 = (bf16[2,4,2,16,1024]{4,3,2,1,0:T(8,128)(2,1)S(1)}, bf16[2,4,2,16,1024]{4,3,2,1,0:T(8,128)(2,1)S(1)}, u32[]{:S(2)}, u32[]{:S(2)}) collective-permute-start(bf16[2,4,2,16,1024]{4,3,2,1,0:T(8,128)(2,1)S(1)} %shard_map.40), channel_id=1, source_target_pairs={{0,1},{1,0},{2,3},{3,2},{4,5},{5,4},{6,7},{7,6},{8,9},{9,8},{10,11... | collective-permute-start | bytes 1572872 | tf_op jit(solution)/shard_map/ppermute | solution.py:192
  67.2 11.9 %collective-permute-start.5 = (bf16[2,2,2,16,1024]{4,3,2,1,0:T(8,128)(2,1)S(1)}, bf16[2,2,2,16,1024]{4,3,2,1,0:T(8,128)(2,1)S(1)}, u32[]{:S(2)}, u32[]{:S(2)}) collective-permute-start(bf16[2,2,2,16,1024]{4,3,2,1,0:T(8,128)(2,1)S(1)} %get-tuple-element.22), channel_id=1, source_target_pairs={{0,2},{1,15},{2,4},{3,1},{4,6},{5,3},{6,8},{7,5},{8,10},{9,7},{10,... | collective-permute-start | bytes 786440 | tf_op jit(solution)/shard_map/ppermute | solution.py:196
  73.1 10.6 %collective-permute-start.6 = (bf16[2,2,2,16,1024]{4,3,2,1,0:T(8,128)(2,1)S(1)}, bf16[2,2,2,16,1024]{4,3,2,1,0:T(8,128)(2,1)S(1)}, u32[]{:S(2)}, u32[]{:S(2)}) collective-permute-start(bf16[2,2,2,16,1024]{4,3,2,1,0:T(8,128)(2,1)S(1)} %get-tuple-element.23), channel_id=1, source_target_pairs={{0,14},{1,3},{2,0},{3,5},{4,2},{5,7},{6,4},{7,9},{8,6},{9,11},{10,... | collective-permute-start | bytes 786440 | tf_op jit(solution)/shard_map/ppermute | solution.py:196
  75.0 11.0 %collective-permute-start.7 = (bf16[1,2,2,16,1024]{4,3,2,1,0:T(8,128)(2,1)S(1)}, bf16[1,2,2,16,1024]{4,3,2,1,0:T(8,128)(2,1)S(1)}, u32[]{:S(2)}, u32[]{:S(2)}) collective-permute-start(bf16[1,2,2,16,1024]{4,3,2,1,0:T(8,128)(2,1)S(1)} %get-tuple-element.24), channel_id=1, source_target_pairs={{0,4},{1,13},{2,6},{3,15},{4,8},{5,1},{6,10},{7,3},{8,12},{9,5},{1... | collective-permute-start | bytes 393224 | tf_op jit(solution)/shard_map/ppermute | solution.py:196
  79.1 7.9 %collective-permute-start.8 = (bf16[2,2,16,1024]{3,2,1,0:T(8,128)(2,1)S(1)}, bf16[2,2,16,1024]{3,2,1,0:T(8,128)(2,1)S(1)}, u32[]{:S(2)}, u32[]{:S(2)}) collective-permute-start(bf16[2,2,16,1024]{3,2,1,0:T(8,128)(2,1)S(1)} %fusion.2), channel_id=1, source_target_pairs={{0,6},{1,11},{2,8},{3,13},{4,10},{5,15},{6,12},{7,1},{8,14},{9,3},... | collective-permute-start | bytes 393224 | tf_op jit(solution)/shard_map/ppermute | solution.py:196
  83.7 9.3 %collective-permute-start.9 = (bf16[2,2,16,1024]{3,2,1,0:T(8,128)(2,1)S(1)}, bf16[2,2,16,1024]{3,2,1,0:T(8,128)(2,1)S(1)}, u32[]{:S(2)}, u32[]{:S(2)}) collective-permute-start(bf16[2,2,16,1024]{3,2,1,0:T(8,128)(2,1)S(1)} %fusion.3), channel_id=1, source_target_pairs={{0,12},{1,5},{2,14},{3,7},{4,0},{5,9},{6,2},{7,11},{8,4},{9,13},{1... | collective-permute-start | bytes 393224 | tf_op jit(solution)/shard_map/ppermute | solution.py:196

commit v6 on v5

--- a/solution.py
+++ b/solution.py
@@ -154,8 +154,8 @@
         dz = (index ^ z) & 1
         a = index >> 1
         for dx in range(2):
-            one = jnp.where(dz == 0, kept_ref[2 * dx, a], kept_ref[3 - 2 * dx, a])
-            other = jnp.where(dz == dx, early_ref[dx, a], late_ref[1 - dx, a])
+            one = jnp.where(dz == 0, kept_ref[3 * dx, a], kept_ref[2 - dx, a])
+            other = jnp.where(dz == dx, early_ref[dx, a], late_ref[dx, a])
             out_ref[i, :, (x + dx) & 1] = (one.astype(jnp.float32) + other.astype(jnp.float32)).astype(one.dtype)
 
 
@@ -184,7 +184,7 @@
     copies = jnp.broadcast_to(amps[None], (FAR * FAR,) + amps.shape)
     mine = lax.all_to_all(copies, ("owner", "rep"), 0, 0, axis_index_groups=far_groups(), tiled=True)
     mine = mine.reshape(FAR, 2, 2, ROWS, depth)
-    near = [lax.ppermute(mine, ("owner", "rep"), near_pairs(dz, dx)) for dz, dx in ((1, 1), (0, 1), (1, 0))]
+    near = [lax.ppermute(mine, ("owner", "rep"), near_pairs(dz, dx)) for dz, dx in ((1, 1), (1, 0), (0, 1))]
     swap = [(0, 1), (1, 0)]
     kept, early, masked = first_dot(place, bits, ints, mine)
     kept, early = second_dot(place, near[0], masked, kept, early)

time: 94.5 us -> 94.3 us (level)
  transfers between devices with their start and end apart: 10 -> 10, of which waited for: 4 -> 3; matrix products, arithmetic and copies ran while one was open for 0% -> 0% of each run, Pallas kernels for 6% -> 6%
where the time goes in v6:
time: 94.3 us; the launch traced here: 93.6 us
  blocking collectives  39.6 us (42%)
  starting transfers between devices  36.4 us (39%)
  waiting for transfers between devices  7.21 us (8%)
  Pallas kernels  6.15 us (7%)
  local copies, waits for them, and re-layouts  3.08 us (3%)
    all_to_all x1, blocking collectives, per_device(): lax.all_to_all(copies, ('owner', 'rep'), 0, 0, axis_index_groups=far_grou...  39.6 us
    ppermute x5, starting transfers between devices, along(): return lax.ppermute(part, ('red', 'rep'), red_step(step))  18.7 us
    ppermute x3, starting transfers between devices, per_device(): lax.ppermute(mine, ('owner', 'rep'), near_pairs(dz, dx))  10.8 us
    ppermute x5, waiting for transfers between devices, along(): return lax.ppermute(part, ('red', 'rep'), red_step(step))  6.96 us
    ppermute x1, starting transfers between devices, per_device(): lax.ppermute(last_dot(place, True, near[1], near[2], masked), 'rep', swap)  3.75 us
    ppermute x1, starting transfers between devices, per_device(): early = lax.ppermute(early, 'rep', swap)  3.15 us
    pallas_call x2, Pallas kernels, last_dot(): pl.pallas_call(functools.partial(last_kernel, other, 0 if other else PART...  2.5 us
    unnamed x4, local copies, waits for them, and re-layouts  2.28 us
  transfers between devices with their start and end apart: 10, of which 3 were waited for; matrix products, arithmetic and copies ran while one was open for 0% of the time, Pallas kernels for 6%

profile of v6, /device:TPU:1, one launch (start us, length us, event | category | flops | bytes accessed | tf_op | source)
XLA Modules:
  0.0 93.6 jit_solution(17378556971545310454)
XLA Ops:
  0.0 0.8 broadcast_in_dim.2
  0.8 39.6 %all_to_all.5 = bf16[16,16,1024]{2,1,0:T(8,128)(2,1)S(1)} all-to-all(bf16[16,16,1024]{2,1,0:T(8,128)(2,1)S(1)} %broadcast_in_dim.2), channel_id=1, replica_groups={{0,32,64,96,256,288,320,352,512,544,576,608,768,800,832,864},{16,48,80,..., dimensions={0} | all-to-all | bytes 1048576 | tf_op jit(solution)/shard_map/all_to_all | solution.py:185
  40.5 1.9 %collective-permute-start.2 = (bf16[4,2,2,16,1024]{4,3,2,1,0:T(8,128)(2,1)S(1)}, bf16[4,2,2,16,1024]{4,3,2,1,0:T(8,128)(2,1)S(1)}, u32[]{:S(2)}, u32[]{:S(2)}) collective-permute-start(bf16[4,2,2,16,1024]{4,3,2,1,0:T(8,128)(2,1)S(1)} %bitcast.16), channel_id=1, source_target_pairs={{0,144},{1,1009},{16,128},{17,929},{32,176},{33,913},{48,160},{49,... | collective-permute-start | bytes 1572872 | tf_op jit(solution)/shard_map/ppermute | solution.py:187
  42.4 4.4 %collective-permute-start = (bf16[4,2,2,16,1024]{4,3,2,1,0:T(8,128)(2,1)S(1)}, bf16[4,2,2,16,1024]{4,3,2,1,0:T(8,128)(2,1)S(1)}, u32[]{:S(2)}, u32[]{:S(2)}) collective-permute-start(bf16[4,2,2,16,1024]{4,3,2,1,0:T(8,128)(2,1)S(1)} %bitcast.17), channel_id=1, source_target_pairs={{0,128},{1,897},{16,144},{17,913},{32,160},{33,929},{48,176},{49,9... | collective-permute-start | bytes 1572872 | tf_op jit(solution)/shard_map/ppermute | solution.py:187
  46.8 4.4 %collective-permute-start.1 = (bf16[4,2,2,16,1024]{4,3,2,1,0:T(8,128)(2,1)S(1)}, bf16[4,2,2,16,1024]{4,3,2,1,0:T(8,128)(2,1)S(1)}, u32[]{:S(2)}, u32[]{:S(2)}) collective-permute-start(bf16[4,2,2,16,1024]{4,3,2,1,0:T(8,128)(2,1)S(1)} %bitcast.18), channel_id=1, source_target_pairs={{0,16},{1,113},{16,0},{17,33},{32,48},{33,17},{48,32},{49,65},{64,... | collective-permute-start | bytes 1572872 | tf_op jit(solution)/shard_map/ppermute | solution.py:187
  51.3 0.1 pad_add_fusion.place_ref
  51.4 0.0 copy-start
  51.4 1.6 %copy-done = bf16[1024,1024]{1,0:T(8,128)(2,1)S(1)} copy-done((bf16[1024,1024]{1,0:T(8,128)(2,1)S(1)}, bf16[1024,1024]{1,0:T(8,128)(2,1)}, u32[]{:S(2)}) %copy-start) | copy-done | bytes 2097176
  52.9 0.0 copy-start.1
  52.9 0.7 copy-done.1
  53.6 1.5 %shard_map.37 = (bf16[4,4,2,16,1024]{4,3,2,1,0:T(8,128)(2,1)S(1)}, bf16[2,4,2,16,1024]{4,3,2,1,0:T(8,128)(2,1)S(1)}, bf16[1024,1024]{1,0:T(8,128)(2,1)S(1)}) custom-call(s32[4]{0:T(128)S(1)} %pad_add_fusion.place_ref, s32[8,8]{1,0:T(8,128)S(1)} %copy-done.1, bf16[1024,1024]{1,0:T(8,128)(2,1)S(1)} %copy-done, bf16[4,2,2,16,1024]{4,3,2,1,0:T(8,128)(2,1)S(1)} %bitcast.19), custom_call_target="tpu_custom_call" | custom-call | flops 536870912 | bytes 4718592 | tf_op jit(solution)/shard_map/pallas_call | solution.py:87
  55.2 0.0 collective-permute-done.2.rows_ref
  55.2 1.3 %shard_map.38 = (bf16[4,4,2,16,1024]{4,3,2,1,0:T(8,128)(2,1)S(1)}, bf16[2,4,2,16,1024]{4,3,2,1,0:T(8,128)(2,1)S(1)}) custom-call(s32[4]{0:T(128)S(1)} %pad_add_fusion.place_ref, bf16[4,2,2,16,1024]{4,3,2,1,0:T(8,128)(2,1)S(1)} %collective-permute-done.2.rows_ref, ...), custom_call_target="tpu_custom_call", output_to_operand_aliasing={{0}: (3, {}), {1}: (4, {})} | custom-call | flops 536870912 | bytes 2621440 | tf_op jit(solution)/shard_map/pallas_call | solution.py:109
  56.4 3.2 %collective-permute-start.3 = (bf16[2,4,2,16,1024]{4,3,2,1,0:T(8,128)(2,1)S(1)}, bf16[2,4,2,16,1024]{4,3,2,1,0:T(8,128)(2,1)S(1)}, u32[]{:S(2)}, u32[]{:S(2)}) collective-permute-start(bf16[2,4,2,16,1024]{4,3,2,1,0:T(8,128)(2,1)S(1)} %get-tuple-element.20), channel_id=1, source_target_pairs={{0,1},{1,0},{2,3},{3,2},{4,5},{5,4},{6,7},{7,6},{8,9},{9,8},{10,11... | collective-permute-start | bytes 1572872 | tf_op jit(solution)/shard_map/ppermute | solution.py:191
  59.6 0.0 collective-permute-done.side_ref
  59.6 0.0 collective-permute-done.1.corner_ref
  59.6 1.3 %shard_map.40 = bf16[2,4,2,16,1024]{4,3,2,1,0:T(8,128)(2,1)S(1)} custom-call(s32[4]{0:T(128)S(1)} %pad_add_fusion.place_ref, bf16[4,2,2,16,1024]{4,3,2,1,0:T(8,128)(2,1)S(1)} %collective-permute-done.side_ref, bf16[4,2,2,16,1024]{4,3,2,1,0:T(8,128)(2,1)S(1)} %collective-permute-done.1.corner_ref, bf16[1024,1024]{1,0:T(8,128)(2,1)S(1)} %get-tuple-element.16.masked_ref), custom_call_target="tpu_custom_call" | custom-call | flops 536870912 | bytes 2621440 | tf_op jit(solution)/shard_map/pallas_call | solution.py:135
  60.9 3.7 %collective-permute-start.4 = (bf16[2,4,2,16,1024]{4,3,2,1,0:T(8,128)(2,1)S(1)}, bf16[2,4,2,16,1024]{4,3,2,1,0:T(8,128)(2,1)S(1)}, u32[]{:S(2)}, u32[]{:S(2)}) collective-permute-start(bf16[2,4,2,16,1024]{4,3,2,1,0:T(8,128)(2,1)S(1)} %shard_map.40), channel_id=1, source_target_pairs={{0,1},{1,0},{2,3},{3,2},{4,5},{5,4},{6,7},{7,6},{8,9},{9,8},{10,11... | collective-permute-start | bytes 1572872 | tf_op jit(solution)/shard_map/ppermute | solution.py:192
  64.6 1.3 %shard_map.39.kept_ref = bf16[4,4,2,16,1024]{4,3,2,1,0:T(8,128)(2,1)S(1)} custom-call(s32[4]{0:T(128)S(1)} %pad_add_fusion.place_ref, bf16[4,2,2,16,1024]{4,3,2,1,0:T(8,128)(2,1)S(1)} %collective-permute-done.side_ref, bf16[4,2,2,16,1024]{4,3,2,1,0:T(8,128)(2,1)S(1)} %collective-permute-done.1.corner_ref, ...), custom_call_target="tpu_custom_call", output_to_operand_aliasing={{}: (4, {})} | custom-call | flops 536870912 | bytes 2621440 | tf_op jit(solution)/shard_map/pallas_call | solution.py:135
  65.9 0.0 collective-permute-done.3.early_ref
  65.9 0.2 collective-permute-done.4.late_ref
  66.1 0.9 shard_map.41
  67.0 5.9 %collective-permute-start.5 = (bf16[2,2,2,16,1024]{4,3,2,1,0:T(8,128)(2,1)S(1)}, bf16[2,2,2,16,1024]{4,3,2,1,0:T(8,128)(2,1)S(1)}, u32[]{:S(2)}, u32[]{:S(2)}) collective-permute-start(bf16[2,2,2,16,1024]{4,3,2,1,0:T(8,128)(2,1)S(1)} %get-tuple-element.22), channel_id=1, source_target_pairs={{0,2},{1,15},{2,4},{3,1},{4,6},{5,3},{6,8},{7,5},{8,10},{9,7},{10,... | collective-permute-start | bytes 786440 | tf_op jit(solution)/shard_map/ppermute | solution.py:196
  72.9 1.9 %collective-permute-start.6 = (bf16[2,2,2,16,1024]{4,3,2,1,0:T(8,128)(2,1)S(1)}, bf16[2,2,2,16,1024]{4,3,2,1,0:T(8,128)(2,1)S(1)}, u32[]{:S(2)}, u32[]{:S(2)}) collective-permute-start(bf16[2,2,2,16,1024]{4,3,2,1,0:T(8,128)(2,1)S(1)} %get-tuple-element.23), channel_id=1, source_target_pairs={{0,14},{1,3},{2,0},{3,5},{4,2},{5,7},{6,4},{7,9},{8,6},{9,11},{10,... | collective-permute-start | bytes 786440 | tf_op jit(solution)/shard_map/ppermute | solution.py:196
  74.8 4.0 %collective-permute-start.7 = (bf16[1,2,2,16,1024]{4,3,2,1,0:T(8,128)(2,1)S(1)}, bf16[1,2,2,16,1024]{4,3,2,1,0:T(8,128)(2,1)S(1)}, u32[]{:S(2)}, u32[]{:S(2)}) collective-permute-start(bf16[1,2,2,16,1024]{4,3,2,1,0:T(8,128)(2,1)S(1)} %get-tuple-element.24), channel_id=1, source_target_pairs={{0,4},{1,13},{2,6},{3,15},{4,8},{5,1},{6,10},{7,3},{8,12},{9,5},{1... | collective-permute-start | bytes 393224 | tf_op jit(solution)/shard_map/ppermute | solution.py:196
  78.9 0.0 collective-permute-done.5
  78.9 4.5 %collective-permute-start.8 = (bf16[2,2,16,1024]{3,2,1,0:T(8,128)(2,1)S(1)}, bf16[2,2,16,1024]{3,2,1,0:T(8,128)(2,1)S(1)}, u32[]{:S(2)}, u32[]{:S(2)}) collective-permute-start(bf16[2,2,16,1024]{3,2,1,0:T(8,128)(2,1)S(1)} %fusion.2), channel_id=1, source_target_pairs={{0,6},{1,11},{2,8},{3,13},{4,10},{5,15},{6,12},{7,1},{8,14},{9,3},... | collective-permute-start | bytes 393224 | tf_op jit(solution)/shard_map/ppermute | solution.py:196
  83.5 0.0 collective-permute-done.6
  83.5 2.3 %collective-permute-start.9 = (bf16[2,2,16,1024]{3,2,1,0:T(8,128)(2,1)S(1)}, bf16[2,2,16,1024]{3,2,1,0:T(8,128)(2,1)S(1)}, u32[]{:S(2)}, u32[]{:S(2)}) collective-permute-start(bf16[2,2,16,1024]{3,2,1,0:T(8,128)(2,1)S(1)} %fusion.3), channel_id=1, source_target_pairs={{0,12},{1,5},{2,14},{3,7},{4,0},{5,9},{6,2},{7,11},{8,4},{9,13},{1... | collective-permute-start | bytes 393224 | tf_op jit(solution)/shard_map/ppermute | solution.py:196
  85.9 0.0 collective-permute-done.7
  85.9 0.9 %collective-permute-done.8 = bf16[2,2,16,1024]{3,2,1,0:T(8,128)(2,1)S(1)} collective-permute-done((bf16[2,2,16,1024]{3,2,1,0:T(8,128)(2,1)S(1)}, bf16[2,2,16,1024]{3,2,1,0:T(8,128)(2,1)S(1)}, u32[]{:S(2)}, u32[]{:S(2)}) %collective-permute-start.8) | collective-permute-done | bytes 131104 | tf_op jit(solution)/shard_map/ppermute | solution.py:196
  86.8 6.0 %collective-permute-done.9 = bf16[2,2,16,1024]{3,2,1,0:T(8,128)(2,1)S(1)} collective-permute-done((bf16[2,2,16,1024]{3,2,1,0:T(8,128)(2,1)S(1)}, bf16[2,2,16,1024]{3,2,1,0:T(8,128)(2,1)S(1)}, u32[]{:S(2)}, u32[]{:S(2)}) %collective-permute-start.9) | collective-permute-done | bytes 131104 | tf_op jit(solution)/shard_map/ppermute | solution.py:196
  92.8 0.8 fusion.1
  (2 shorter events, 0.1 us)
Async XLA Ops:
  40.5 14.7 %collective-permute-start.2 = (bf16[4,2,2,16,1024]{4,3,2,1,0:T(8,128)(2,1)S(1)}, bf16[4,2,2,16,1024]{4,3,2,1,0:T(8,128)(2,1)S(1)}, u32[]{:S(2)}, u32[]{:S(2)}) collective-permute-start(bf16[4,2,2,16,1024]{4,3,2,1,0:T(8,128)(2,1)S(1)} %bitcast.16), channel_id=1, source_target_pairs={{0,144},{1,1009},{16,128},{17,929},{32,176},{33,913},{48,160},{49,... | collective-permute-start | bytes 1572872 | tf_op jit(solution)/shard_map/ppermute | solution.py:187
  42.4 17.2 %collective-permute-start = (bf16[4,2,2,16,1024]{4,3,2,1,0:T(8,128)(2,1)S(1)}, bf16[4,2,2,16,1024]{4,3,2,1,0:T(8,128)(2,1)S(1)}, u32[]{:S(2)}, u32[]{:S(2)}) collective-permute-start(bf16[4,2,2,16,1024]{4,3,2,1,0:T(8,128)(2,1)S(1)} %bitcast.17), channel_id=1, source_target_pairs={{0,128},{1,897},{16,144},{17,913},{32,160},{33,929},{48,176},{49,9... | collective-permute-start | bytes 1572872 | tf_op jit(solution)/shard_map/ppermute | solution.py:187
  46.8 12.8 %collective-permute-start.1 = (bf16[4,2,2,16,1024]{4,3,2,1,0:T(8,128)(2,1)S(1)}, bf16[4,2,2,16,1024]{4,3,2,1,0:T(8,128)(2,1)S(1)}, u32[]{:S(2)}, u32[]{:S(2)}) collective-permute-start(bf16[4,2,2,16,1024]{4,3,2,1,0:T(8,128)(2,1)S(1)} %bitcast.18), channel_id=1, source_target_pairs={{0,16},{1,113},{16,0},{17,33},{32,48},{33,17},{48,32},{49,65},{64,... | collective-permute-start | bytes 1572872 | tf_op jit(solution)/shard_map/ppermute | solution.py:187
  51.4 1.6 %copy-start = (bf16[1024,1024]{1,0:T(8,128)(2,1)S(1)}, bf16[1024,1024]{1,0:T(8,128)(2,1)}, u32[]{:S(2)}) copy-start(bf16[1024,1024]{1,0:T(8,128)(2,1)} %ints_ref.1) | copy-start | bytes 6291460
  52.9 0.7 copy-start.1
  56.4 9.5 %collective-permute-start.3 = (bf16[2,4,2,16,1024]{4,3,2,1,0:T(8,128)(2,1)S(1)}, bf16[2,4,2,16,1024]{4,3,2,1,0:T(8,128)(2,1)S(1)}, u32[]{:S(2)}, u32[]{:S(2)}) collective-permute-start(bf16[2,4,2,16,1024]{4,3,2,1,0:T(8,128)(2,1)S(1)} %get-tuple-element.20), channel_id=1, source_target_pairs={{0,1},{1,0},{2,3},{3,2},{4,5},{5,4},{6,7},{7,6},{8,9},{9,8},{10,11... | collective-permute-start | bytes 1572872 | tf_op jit(solution)/shard_map/ppermute | solution.py:191
  60.9 5.3 %collective-permute-start.4 = (bf16[2,4,2,16,1024]{4,3,2,1,0:T(8,128)(2,1)S(1)}, bf16[2,4,2,16,1024]{4,3,2,1,0:T(8,128)(2,1)S(1)}, u32[]{:S(2)}, u32[]{:S(2)}) collective-permute-start(bf16[2,4,2,16,1024]{4,3,2,1,0:T(8,128)(2,1)S(1)} %shard_map.40), channel_id=1, source_target_pairs={{0,1},{1,0},{2,3},{3,2},{4,5},{5,4},{6,7},{7,6},{8,9},{9,8},{10,11... | collective-permute-start | bytes 1572872 | tf_op jit(solution)/shard_map/ppermute | solution.py:192
  67.0 11.9 %collective-permute-start.5 = (bf16[2,2,2,16,1024]{4,3,2,1,0:T(8,128)(2,1)S(1)}, bf16[2,2,2,16,1024]{4,3,2,1,0:T(8,128)(2,1)S(1)}, u32[]{:S(2)}, u32[]{:S(2)}) collective-permute-start(bf16[2,2,2,16,1024]{4,3,2,1,0:T(8,128)(2,1)S(1)} %get-tuple-element.22), channel_id=1, source_target_pairs={{0,2},{1,15},{2,4},{3,1},{4,6},{5,3},{6,8},{7,5},{8,10},{9,7},{10,... | collective-permute-start | bytes 786440 | tf_op jit(solution)/shard_map/ppermute | solution.py:196
  72.9 10.6 %collective-permute-start.6 = (bf16[2,2,2,16,1024]{4,3,2,1,0:T(8,128)(2,1)S(1)}, bf16[2,2,2,16,1024]{4,3,2,1,0:T(8,128)(2,1)S(1)}, u32[]{:S(2)}, u32[]{:S(2)}) collective-permute-start(bf16[2,2,2,16,1024]{4,3,2,1,0:T(8,128)(2,1)S(1)} %get-tuple-element.23), channel_id=1, source_target_pairs={{0,14},{1,3},{2,0},{3,5},{4,2},{5,7},{6,4},{7,9},{8,6},{9,11},{10,... | collective-permute-start | bytes 786440 | tf_op jit(solution)/shard_map/ppermute | solution.py:196
  74.8 11.0 %collective-permute-start.7 = (bf16[1,2,2,16,1024]{4,3,2,1,0:T(8,128)(2,1)S(1)}, bf16[1,2,2,16,1024]{4,3,2,1,0:T(8,128)(2,1)S(1)}, u32[]{:S(2)}, u32[]{:S(2)}) collective-permute-start(bf16[1,2,2,16,1024]{4,3,2,1,0:T(8,128)(2,1)S(1)} %get-tuple-element.24), channel_id=1, source_target_pairs={{0,4},{1,13},{2,6},{3,15},{4,8},{5,1},{6,10},{7,3},{8,12},{9,5},{1... | collective-permute-start | bytes 393224 | tf_op jit(solution)/shard_map/ppermute | solution.py:196
  78.9 7.9 %collective-permute-start.8 = (bf16[2,2,16,1024]{3,2,1,0:T(8,128)(2,1)S(1)}, bf16[2,2,16,1024]{3,2,1,0:T(8,128)(2,1)S(1)}, u32[]{:S(2)}, u32[]{:S(2)}) collective-permute-start(bf16[2,2,16,1024]{3,2,1,0:T(8,128)(2,1)S(1)} %fusion.2), channel_id=1, source_target_pairs={{0,6},{1,11},{2,8},{3,13},{4,10},{5,15},{6,12},{7,1},{8,14},{9,3},... | collective-permute-start | bytes 393224 | tf_op jit(solution)/shard_map/ppermute | solution.py:196
  83.5 9.3 %collective-permute-start.9 = (bf16[2,2,16,1024]{3,2,1,0:T(8,128)(2,1)S(1)}, bf16[2,2,16,1024]{3,2,1,0:T(8,128)(2,1)S(1)}, u32[]{:S(2)}, u32[]{:S(2)}) collective-permute-start(bf16[2,2,16,1024]{3,2,1,0:T(8,128)(2,1)S(1)} %fusion.3), channel_id=1, source_target_pairs={{0,12},{1,5},{2,14},{3,7},{4,0},{5,9},{6,2},{7,11},{8,4},{9,13},{1... | collective-permute-start | bytes 393224 | tf_op jit(solution)/shard_map/ppermute | solution.py:196

commit v7 on v6

--- a/solution.py
+++ b/solution.py
@@ -11,7 +11,6 @@
 SIDE = 8
 FAR = 4
 PART = 2
-CLASSES = 2 * PART
 ROWS = 16
 VMEM = pl.BlockSpec(memory_space=pltpu.VMEM)
 SMEM = pl.BlockSpec(memory_space=pltpu.SMEM)
@@ -77,9 +76,9 @@
         class_dot(0, place_ref, rows_ref, masked_ref, [here], kept_ref, away_ref)
 
 
-def sums_shape(rows, cols, classes=CLASSES):
+def sums_shape(rows, cols):
     far, _, pairs, _, _ = rows.shape
-    return jax.ShapeDtypeStruct((classes, far, pairs, ROWS, cols), jnp.bfloat16)
+    return jax.ShapeDtypeStruct((PART, far, pairs, ROWS, cols), jnp.bfloat16)
 
 
 def first_dot(place, bits, ints, rows):
@@ -90,7 +89,7 @@
         out_specs=[VMEM, VMEM, VMEM],
         out_shape=[
             sums_shape(rows, cols),
-            sums_shape(rows, cols, PART),
+            sums_shape(rows, cols),
             jax.ShapeDtypeStruct(ints.shape, ints.dtype),
         ],
         compiler_params=pltpu.CompilerParams(vmem_limit_bytes=16 * 1024 * 1024),
@@ -110,7 +109,7 @@
         second_kernel,
         in_specs=[SMEM] + [VMEM] * 4,
         out_specs=[VMEM, VMEM],
-        out_shape=[sums_shape(rows, cols), sums_shape(rows, cols, PART)],
+        out_shape=[sums_shape(rows, cols), sums_shape(rows, cols)],
         input_output_aliases={3: 0, 4: 1},
         compiler_params=pltpu.CompilerParams(vmem_limit_bytes=16 * 1024 * 1024),
         cost_estimate=pl.CostEstimate(
@@ -119,56 +118,79 @@
     )(place, rows, masked, kept, away)
 
 
-def last_kernel(other, first, place_ref, side_ref, corner_ref, masked_ref, *refs):
-    out_ref = refs[-1]
-    rep = place_ref[0]
-    half = 1 - rep if other else rep
+def late_dots(half, side_ref, corner_ref, masked_ref, out_ref):
     rows = jnp.concatenate([half_rows(half, ref) for ref in (side_ref, corner_ref)], axis=0)
     for here in col_tiles(masked_ref.shape[1]):
         total = jnp.dot(rows, masked_ref[:, here], preferred_element_type=jnp.float32)
         for i in range(PART):
-            put(first + i, here, total[i * rows.shape[0] // PART : (i + 1) * rows.shape[0] // PART], out_ref)
-
-
-def last_dot(place, other, side, corner, masked, *kept):
+            put(i, here, total[i * rows.shape[0] // PART : (i + 1) * rows.shape[0] // PART], out_ref)
+
+
+def away_kernel(place_ref, side_ref, corner_ref, masked_ref, out_ref):
+    late_dots(1 - place_ref[0], side_ref, corner_ref, masked_ref, out_ref)
+
+
+def away_dot(place, side, corner, masked):
     cols = masked.shape[1]
     return pl.pallas_call(
-        functools.partial(last_kernel, other, 0 if other else PART),
-        in_specs=[SMEM] + [VMEM] * (3 + len(kept)),
+        away_kernel,
+        in_specs=[SMEM] + [VMEM] * 3,
         out_specs=VMEM,
-        out_shape=sums_shape(side, cols, PART if other else CLASSES),
-        input_output_aliases={} if other else {4: 0},
+        out_shape=sums_shape(side, cols),
         compiler_params=pltpu.CompilerParams(vmem_limit_bytes=16 * 1024 * 1024),
         cost_estimate=pl.CostEstimate(
             flops=side.size * cols * 2, bytes_accessed=2 * side.size + 2 * masked.size, transcendentals=0
         ),
-    )(place, side, corner, masked, *kept)
-
-
-def share_kernel(steps, place_ref, kept_ref, early_ref, late_ref, *out_refs):
+    )(place, side, corner, masked)
+
+
+def share(late, steps, place_ref, kept_ref, arrived_ref, out_refs):
     z, x, y, way = place_ref[1], place_ref[2], place_ref[3], 2 * place_ref[0] - 1
-    flat = [step for group in steps for step in group]
-    outs = [(ref, i) for ref, group in zip(out_refs, steps) for i in range(len(group))]
-    for step, (out_ref, i) in zip(flat, outs):
-        index = (y + way * step + SIDE) & (SIDE - 1)
-        dz = (index ^ z) & 1
-        a = index >> 1
-        for dx in range(2):
-            one = jnp.where(dz == 0, kept_ref[3 * dx, a], kept_ref[2 - dx, a])
-            other = jnp.where(dz == dx, early_ref[dx, a], late_ref[dx, a])
-            out_ref[i, :, (x + dx) & 1] = (one.astype(jnp.float32) + other.astype(jnp.float32)).astype(one.dtype)
-
-
-def share(place, steps, kept, early, late):
-    _, _, pairs, rows, cols = kept.shape
-    return pl.pallas_call(
-        functools.partial(share_kernel, steps),
-        in_specs=[SMEM, VMEM, VMEM, VMEM],
-        out_specs=[VMEM] * len(steps),
-        out_shape=[jax.ShapeDtypeStruct((len(group), pairs, 2, rows, cols), kept.dtype) for group in steps],
+    for group, out_ref in zip(steps, out_refs):
+        for i, step in enumerate(group):
+            index = (y + way * step + SIDE) & (SIDE - 1)
+            dz = (index ^ z) & 1
+            which = 1 - dz if late else dz
+            one, other = kept_ref[which, index >> 1], arrived_ref[which, index >> 1]
+            px = (x + which) & 1
+            out_ref[i, :, px] = (one.astype(jnp.float32) + other.astype(jnp.float32)).astype(one.dtype)
+
+
+def kept_kernel(steps, place_ref, side_ref, corner_ref, masked_ref, early_ref, arrived_ref, kept_ref, *out_refs):
+    late_dots(place_ref[0], side_ref, corner_ref, masked_ref, kept_ref)
+    share(False, steps, place_ref, early_ref, arrived_ref, out_refs)
+
+
+def kept_dot(place, steps, side, corner, masked, early, arrived):
+    cols = masked.shape[1]
+    _, _, pairs, rows, _ = early.shape
+    return pl.pallas_call(
+        functools.partial(kept_kernel, steps),
+        in_specs=[SMEM] + [VMEM] * 5,
+        out_specs=[VMEM] * (1 + len(steps)),
+        out_shape=[sums_shape(side, cols)]
+        + [jax.ShapeDtypeStruct((len(group), pairs, 2, rows, cols), early.dtype) for group in steps],
+        compiler_params=pltpu.CompilerParams(vmem_limit_bytes=16 * 1024 * 1024),
+        cost_estimate=pl.CostEstimate(
+            flops=side.size * cols * 2, bytes_accessed=2 * side.size + 2 * masked.size, transcendentals=0
+        ),
+    )(place, side, corner, masked, early, arrived)
+
+
+def late_kernel(steps, place_ref, kept_ref, arrived_ref, *refs):
+    share(True, steps, place_ref, kept_ref, arrived_ref, refs[len(steps) :])
+
+
+def late_share(place, steps, kept, arrived, parts):
+    return pl.pallas_call(
+        functools.partial(late_kernel, steps),
+        in_specs=[SMEM] + [VMEM] * (2 + len(parts)),
+        out_specs=[VMEM] * len(parts),
+        out_shape=[jax.ShapeDtypeStruct(part.shape, part.dtype) for part in parts],
+        input_output_aliases={3 + i: i for i in range(len(parts))},
         compiler_params=pltpu.CompilerParams(vmem_limit_bytes=16 * 1024 * 1024),
         cost_estimate=pl.CostEstimate(flops=kept.size, bytes_accessed=6 * kept.size, transcendentals=0),
-    )(place, kept, early, late)
+    )(place, kept, arrived, *parts)
 
 
 def added(*terms):
@@ -189,14 +211,14 @@
     kept, early, masked = first_dot(place, bits, ints, mine)
     kept, early = second_dot(place, near[0], masked, kept, early)
     early = lax.ppermute(early, "rep", swap)
-    late = lax.ppermute(last_dot(place, True, near[1], near[2], masked), "rep", swap)
-    kept = last_dot(place, False, near[1], near[2], masked, kept)
+    late = lax.ppermute(away_dot(place, near[1], near[2], masked), "rep", swap)
+    groups = ((-1, -4), (1, 3), (-2,), (-3,), (2,), (0,))
+    late_kept, *parts = kept_dot(place, groups, near[1], near[2], masked, kept, early)
+    down, up, two_down, three_down, two_up, own = late_share(place, groups, late_kept, late, parts)
 
     def along(step, part):
         return lax.ppermute(part, ("red", "rep"), red_step(step))
 
-    groups = ((-1, -4), (1, 3), (-2,), (-3,), (2,), (0,))
-    down, up, two_down, three_down, two_up, own = share(place, groups, kept, early, late)
     down, up, two_down = along(-1, down), along(1, up), along(-2, two_down)
     three_down = along(-3, added(three_down[0], down[1]))
     two_up = along(2, added(two_up[0], up[1]))

time: 94.3 us -> 94.1 us (level)
  no operation moved by 1% of the time
where the time goes in v7:
time: 94.1 us; the launch traced here: 93.4 us
  blocking collectives  39.6 us (42%)
  starting transfers between devices  36.4 us (39%)
  waiting for transfers between devices  7.11 us (8%)
  Pallas kernels  6.1 us (6%)
  local copies, waits for them, and re-layouts  3.08 us (3%)
    all_to_all x1, blocking collectives, per_device(): lax.all_to_all(copies, ('owner', 'rep'), 0, 0, axis_index_groups=far_grou...  39.6 us
    ppermute x5, starting transfers between devices, along(): return lax.ppermute(part, ('red', 'rep'), red_step(step))  18.7 us
    ppermute x3, starting transfers between devices, per_device(): lax.ppermute(mine, ('owner', 'rep'), near_pairs(dz, dx))  10.8 us
    ppermute x5, waiting for transfers between devices, along(): return lax.ppermute(part, ('red', 'rep'), red_step(step))  6.95 us
    ppermute x1, starting transfers between devices, per_device(): late = lax.ppermute(away_dot(place, near[1], near[2], masked), 'rep', swap)  3.71 us
    ppermute x1, starting transfers between devices, per_device(): early = lax.ppermute(early, 'rep', swap)  3.16 us
    unnamed x4, local copies, waits for them, and re-layouts  2.28 us
  transfers between devices with their start and end apart: 10, of which 3 were waited for; matrix products, arithmetic and copies ran while one was open for 0% of the time, Pallas kernels for 6%

profile of v7, /device:TPU:1, one launch (start us, length us, event | category | flops | bytes accessed | tf_op | source)
XLA Modules:
  0.0 93.4 jit_solution(13657334948474368302)
XLA Ops:
  0.0 0.8 broadcast_in_dim.2
  0.8 39.6 %all_to_all.5 = bf16[16,16,1024]{2,1,0:T(8,128)(2,1)S(1)} all-to-all(bf16[16,16,1024]{2,1,0:T(8,128)(2,1)S(1)} %broadcast_in_dim.2), channel_id=1, replica_groups={{0,32,64,96,256,288,320,352,512,544,576,608,768,800,832,864},{16,48,80,..., dimensions={0} | all-to-all | bytes 1048576 | tf_op jit(solution)/shard_map/all_to_all | solution.py:207
  40.5 1.9 %collective-permute-start.2 = (bf16[4,2,2,16,1024]{4,3,2,1,0:T(8,128)(2,1)S(1)}, bf16[4,2,2,16,1024]{4,3,2,1,0:T(8,128)(2,1)S(1)}, u32[]{:S(2)}, u32[]{:S(2)}) collective-permute-start(bf16[4,2,2,16,1024]{4,3,2,1,0:T(8,128)(2,1)S(1)} %bitcast.16), channel_id=1, source_target_pairs={{0,144},{1,1009},{16,128},{17,929},{32,176},{33,913},{48,160},{49,... | collective-permute-start | bytes 1572872 | tf_op jit(solution)/shard_map/ppermute | solution.py:209
  42.4 4.4 %collective-permute-start = (bf16[4,2,2,16,1024]{4,3,2,1,0:T(8,128)(2,1)S(1)}, bf16[4,2,2,16,1024]{4,3,2,1,0:T(8,128)(2,1)S(1)}, u32[]{:S(2)}, u32[]{:S(2)}) collective-permute-start(bf16[4,2,2,16,1024]{4,3,2,1,0:T(8,128)(2,1)S(1)} %bitcast.17), channel_id=1, source_target_pairs={{0,128},{1,897},{16,144},{17,913},{32,160},{33,929},{48,176},{49,9... | collective-permute-start | bytes 1572872 | tf_op jit(solution)/shard_map/ppermute | solution.py:209
  46.8 4.4 %collective-permute-start.1 = (bf16[4,2,2,16,1024]{4,3,2,1,0:T(8,128)(2,1)S(1)}, bf16[4,2,2,16,1024]{4,3,2,1,0:T(8,128)(2,1)S(1)}, u32[]{:S(2)}, u32[]{:S(2)}) collective-permute-start(bf16[4,2,2,16,1024]{4,3,2,1,0:T(8,128)(2,1)S(1)} %bitcast.18), channel_id=1, source_target_pairs={{0,16},{1,113},{16,0},{17,33},{32,48},{33,17},{48,32},{49,65},{64,... | collective-permute-start | bytes 1572872 | tf_op jit(solution)/shard_map/ppermute | solution.py:209
  51.3 0.1 pad_add_fusion.place_ref
  51.4 0.0 copy-start
  51.4 1.6 %copy-done = bf16[1024,1024]{1,0:T(8,128)(2,1)S(1)} copy-done((bf16[1024,1024]{1,0:T(8,128)(2,1)S(1)}, bf16[1024,1024]{1,0:T(8,128)(2,1)}, u32[]{:S(2)}) %copy-start) | copy-done | bytes 2097176
  52.9 0.0 copy-start.1
  52.9 0.7 copy-done.1
  53.6 1.6 %shard_map.37 = (bf16[2,4,2,16,1024]{4,3,2,1,0:T(8,128)(2,1)S(1)}, bf16[2,4,2,16,1024]{4,3,2,1,0:T(8,128)(2,1)S(1)}, bf16[1024,1024]{1,0:T(8,128)(2,1)S(1)}) custom-call(s32[4]{0:T(128)S(1)} %pad_add_fusion.place_ref, s32[8,8]{1,0:T(8,128)S(1)} %copy-done.1, bf16[1024,1024]{1,0:T(8,128)(2,1)S(1)} %copy-done, bf16[4,2,2,16,1024]{4,3,2,1,0:T(8,128)(2,1)S(1)} %bitcast.19), custom_call_target="tpu_custom_call" | custom-call | flops 536870912 | bytes 4718592 | tf_op jit(solution)/shard_map/pallas_call | solution.py:86
  55.2 0.0 collective-permute-done.2.rows_ref
  55.2 1.3 %shard_map.38 = (bf16[2,4,2,16,1024]{4,3,2,1,0:T(8,128)(2,1)S(1)}, bf16[2,4,2,16,1024]{4,3,2,1,0:T(8,128)(2,1)S(1)}) custom-call(s32[4]{0:T(128)S(1)} %pad_add_fusion.place_ref, bf16[4,2,2,16,1024]{4,3,2,1,0:T(8,128)(2,1)S(1)} %collective-permute-done.2.rows_ref, ...), custom_call_target="tpu_custom_call", output_to_operand_aliasing={{0}: (3, {}), {1}: (4, {})} | custom-call | flops 536870912 | bytes 2621440 | tf_op jit(solution)/shard_map/pallas_call | solution.py:108
  56.5 3.2 %collective-permute-start.3 = (bf16[2,4,2,16,1024]{4,3,2,1,0:T(8,128)(2,1)S(1)}, bf16[2,4,2,16,1024]{4,3,2,1,0:T(8,128)(2,1)S(1)}, u32[]{:S(2)}, u32[]{:S(2)}) collective-permute-start(bf16[2,4,2,16,1024]{4,3,2,1,0:T(8,128)(2,1)S(1)} %get-tuple-element.27), channel_id=1, source_target_pairs={{0,1},{1,0},{2,3},{3,2},{4,5},{5,4},{6,7},{7,6},{8,9},{9,8},{10,11... | collective-permute-start | bytes 1572872 | tf_op jit(solution)/shard_map/ppermute | solution.py:213
  59.6 0.0 collective-permute-done.side_ref
  59.7 0.0 collective-permute-done.1.corner_ref
  59.7 1.3 %shard_map.40 = bf16[2,4,2,16,1024]{4,3,2,1,0:T(8,128)(2,1)S(1)} custom-call(s32[4]{0:T(128)S(1)} %pad_add_fusion.place_ref, bf16[4,2,2,16,1024]{4,3,2,1,0:T(8,128)(2,1)S(1)} %collective-permute-done.side_ref, bf16[4,2,2,16,1024]{4,3,2,1,0:T(8,128)(2,1)S(1)} %collective-permute-done.1.corner_ref, bf16[1024,1024]{1,0:T(8,128)(2,1)S(1)} %get-tuple-element.23.masked_ref), custom_call_target="tpu_custom_call" | custom-call | flops 536870912 | bytes 2621440 | tf_op jit(solution)/shard_map/pallas_call | solution.py:135
  60.9 3.7 %collective-permute-start.4 = (bf16[2,4,2,16,1024]{4,3,2,1,0:T(8,128)(2,1)S(1)}, bf16[2,4,2,16,1024]{4,3,2,1,0:T(8,128)(2,1)S(1)}, u32[]{:S(2)}, u32[]{:S(2)}) collective-permute-start(bf16[2,4,2,16,1024]{4,3,2,1,0:T(8,128)(2,1)S(1)} %shard_map.40), channel_id=1, source_target_pairs={{0,1},{1,0},{2,3},{3,2},{4,5},{5,4},{6,7},{7,6},{8,9},{9,8},{10,11... | collective-permute-start | bytes 1572872 | tf_op jit(solution)/shard_map/ppermute | solution.py:214
  64.7 0.0 collective-permute-done.3.arrived_ref
  64.7 1.3 %shard_map.39 = (bf16[2,4,2,16,1024]{4,3,2,1,0:T(8,128)(2,1)S(1)}, bf16[2,2,2,16,1024]{4,3,2,1,0:T(8,128)(2,1)S(1)}, bf16[2,2,2,16,1024]{4,3,2,1,0:T(8,128)(2,1)...) custom-call(s32[4]{0:T(128)S(1)} %pad_add_fusion.place_ref, ...), custom_call_target="tpu_custom_call" | custom-call | flops 536870912 | bytes 2621440 | tf_op jit(solution)/shard_map/pallas_call | solution.py:167
  66.0 0.1 collective-permute-done.4.arrived_ref
  66.2 0.7 shard_map.41
  66.8 5.9 %collective-permute-start.5 = (bf16[2,2,2,16,1024]{4,3,2,1,0:T(8,128)(2,1)S(1)}, bf16[2,2,2,16,1024]{4,3,2,1,0:T(8,128)(2,1)S(1)}, u32[]{:S(2)}, u32[]{:S(2)}) collective-permute-start(bf16[2,2,2,16,1024]{4,3,2,1,0:T(8,128)(2,1)S(1)} %get-tuple-element.36), channel_id=1, source_target_pairs={{0,2},{1,15},{2,4},{3,1},{4,6},{5,3},{6,8},{7,5},{8,10},{9,7},{10,... | collective-permute-start | bytes 786440 | tf_op jit(solution)/shard_map/ppermute | solution.py:220
  72.7 1.9 %collective-permute-start.6 = (bf16[2,2,2,16,1024]{4,3,2,1,0:T(8,128)(2,1)S(1)}, bf16[2,2,2,16,1024]{4,3,2,1,0:T(8,128)(2,1)S(1)}, u32[]{:S(2)}, u32[]{:S(2)}) collective-permute-start(bf16[2,2,2,16,1024]{4,3,2,1,0:T(8,128)(2,1)S(1)} %get-tuple-element.37), channel_id=1, source_target_pairs={{0,14},{1,3},{2,0},{3,5},{4,2},{5,7},{6,4},{7,9},{8,6},{9,11},{10,... | collective-permute-start | bytes 786440 | tf_op jit(solution)/shard_map/ppermute | solution.py:220
  74.7 4.0 %collective-permute-start.7 = (bf16[1,2,2,16,1024]{4,3,2,1,0:T(8,128)(2,1)S(1)}, bf16[1,2,2,16,1024]{4,3,2,1,0:T(8,128)(2,1)S(1)}, u32[]{:S(2)}, u32[]{:S(2)}) collective-permute-start(bf16[1,2,2,16,1024]{4,3,2,1,0:T(8,128)(2,1)S(1)} %get-tuple-element.38), channel_id=1, source_target_pairs={{0,4},{1,13},{2,6},{3,15},{4,8},{5,1},{6,10},{7,3},{8,12},{9,5},{1... | collective-permute-start | bytes 393224 | tf_op jit(solution)/shard_map/ppermute | solution.py:220
  78.7 0.0 collective-permute-done.5
  78.8 4.5 %collective-permute-start.8 = (bf16[2,2,16,1024]{3,2,1,0:T(8,128)(2,1)S(1)}, bf16[2,2,16,1024]{3,2,1,0:T(8,128)(2,1)S(1)}, u32[]{:S(2)}, u32[]{:S(2)}) collective-permute-start(bf16[2,2,16,1024]{3,2,1,0:T(8,128)(2,1)S(1)} %fusion.2), channel_id=1, source_target_pairs={{0,6},{1,11},{2,8},{3,13},{4,10},{5,15},{6,12},{7,1},{8,14},{9,3},... | collective-permute-start | bytes 393224 | tf_op jit(solution)/shard_map/ppermute | solution.py:220
  83.3 0.0 collective-permute-done.6
  83.3 2.3 %collective-permute-start.9 = (bf16[2,2,16,1024]{3,2,1,0:T(8,128)(2,1)S(1)}, bf16[2,2,16,1024]{3,2,1,0:T(8,128)(2,1)S(1)}, u32[]{:S(2)}, u32[]{:S(2)}) collective-permute-start(bf16[2,2,16,1024]{3,2,1,0:T(8,128)(2,1)S(1)} %fusion.3), channel_id=1, source_target_pairs={{0,12},{1,5},{2,14},{3,7},{4,0},{5,9},{6,2},{7,11},{8,4},{9,13},{1... | collective-permute-start | bytes 393224 | tf_op jit(solution)/shard_map/ppermute | solution.py:220
  85.7 0.0 collective-permute-done.7
  85.7 0.9 collective-permute-done.8
  86.6 6.0 %collective-permute-done.9 = bf16[2,2,16,1024]{3,2,1,0:T(8,128)(2,1)S(1)} collective-permute-done((bf16[2,2,16,1024]{3,2,1,0:T(8,128)(2,1)S(1)}, bf16[2,2,16,1024]{3,2,1,0:T(8,128)(2,1)S(1)}, u32[]{:S(2)}, u32[]{:S(2)}) %collective-permute-start.9) | collective-permute-done | bytes 131104 | tf_op jit(solution)/shard_map/ppermute | solution.py:220
  92.6 0.8 fusion.1
  (2 shorter events, 0.1 us)
Async XLA Ops:
  40.5 14.7 %collective-permute-start.2 = (bf16[4,2,2,16,1024]{4,3,2,1,0:T(8,128)(2,1)S(1)}, bf16[4,2,2,16,1024]{4,3,2,1,0:T(8,128)(2,1)S(1)}, u32[]{:S(2)}, u32[]{:S(2)}) collective-permute-start(bf16[4,2,2,16,1024]{4,3,2,1,0:T(8,128)(2,1)S(1)} %bitcast.16), channel_id=1, source_target_pairs={{0,144},{1,1009},{16,128},{17,929},{32,176},{33,913},{48,160},{49,... | collective-permute-start | bytes 1572872 | tf_op jit(solution)/shard_map/ppermute | solution.py:209
  42.4 17.3 %collective-permute-start = (bf16[4,2,2,16,1024]{4,3,2,1,0:T(8,128)(2,1)S(1)}, bf16[4,2,2,16,1024]{4,3,2,1,0:T(8,128)(2,1)S(1)}, u32[]{:S(2)}, u32[]{:S(2)}) collective-permute-start(bf16[4,2,2,16,1024]{4,3,2,1,0:T(8,128)(2,1)S(1)} %bitcast.17), channel_id=1, source_target_pairs={{0,128},{1,897},{16,144},{17,913},{32,160},{33,929},{48,176},{49,9... | collective-permute-start | bytes 1572872 | tf_op jit(solution)/shard_map/ppermute | solution.py:209
  46.8 12.8 %collective-permute-start.1 = (bf16[4,2,2,16,1024]{4,3,2,1,0:T(8,128)(2,1)S(1)}, bf16[4,2,2,16,1024]{4,3,2,1,0:T(8,128)(2,1)S(1)}, u32[]{:S(2)}, u32[]{:S(2)}) collective-permute-start(bf16[4,2,2,16,1024]{4,3,2,1,0:T(8,128)(2,1)S(1)} %bitcast.18), channel_id=1, source_target_pairs={{0,16},{1,113},{16,0},{17,33},{32,48},{33,17},{48,32},{49,65},{64,... | collective-permute-start | bytes 1572872 | tf_op jit(solution)/shard_map/ppermute | solution.py:209
  51.4 1.6 %copy-start = (bf16[1024,1024]{1,0:T(8,128)(2,1)S(1)}, bf16[1024,1024]{1,0:T(8,128)(2,1)}, u32[]{:S(2)}) copy-start(bf16[1024,1024]{1,0:T(8,128)(2,1)} %ints_ref.1) | copy-start | bytes 6291460
  52.9 0.7 copy-start.1
  56.5 8.2 %collective-permute-start.3 = (bf16[2,4,2,16,1024]{4,3,2,1,0:T(8,128)(2,1)S(1)}, bf16[2,4,2,16,1024]{4,3,2,1,0:T(8,128)(2,1)S(1)}, u32[]{:S(2)}, u32[]{:S(2)}) collective-permute-start(bf16[2,4,2,16,1024]{4,3,2,1,0:T(8,128)(2,1)S(1)} %get-tuple-element.27), channel_id=1, source_target_pairs={{0,1},{1,0},{2,3},{3,2},{4,5},{5,4},{6,7},{7,6},{8,9},{9,8},{10,11... | collective-permute-start | bytes 1572872 | tf_op jit(solution)/shard_map/ppermute | solution.py:213
  60.9 5.2 %collective-permute-start.4 = (bf16[2,4,2,16,1024]{4,3,2,1,0:T(8,128)(2,1)S(1)}, bf16[2,4,2,16,1024]{4,3,2,1,0:T(8,128)(2,1)S(1)}, u32[]{:S(2)}, u32[]{:S(2)}) collective-permute-start(bf16[2,4,2,16,1024]{4,3,2,1,0:T(8,128)(2,1)S(1)} %shard_map.40), channel_id=1, source_target_pairs={{0,1},{1,0},{2,3},{3,2},{4,5},{5,4},{6,7},{7,6},{8,9},{9,8},{10,11... | collective-permute-start | bytes 1572872 | tf_op jit(solution)/shard_map/ppermute | solution.py:214
  66.8 11.9 %collective-permute-start.5 = (bf16[2,2,2,16,1024]{4,3,2,1,0:T(8,128)(2,1)S(1)}, bf16[2,2,2,16,1024]{4,3,2,1,0:T(8,128)(2,1)S(1)}, u32[]{:S(2)}, u32[]{:S(2)}) collective-permute-start(bf16[2,2,2,16,1024]{4,3,2,1,0:T(8,128)(2,1)S(1)} %get-tuple-element.36), channel_id=1, source_target_pairs={{0,2},{1,15},{2,4},{3,1},{4,6},{5,3},{6,8},{7,5},{8,10},{9,7},{10,... | collective-permute-start | bytes 786440 | tf_op jit(solution)/shard_map/ppermute | solution.py:220
  72.7 10.6 %collective-permute-start.6 = (bf16[2,2,2,16,1024]{4,3,2,1,0:T(8,128)(2,1)S(1)}, bf16[2,2,2,16,1024]{4,3,2,1,0:T(8,128)(2,1)S(1)}, u32[]{:S(2)}, u32[]{:S(2)}) collective-permute-start(bf16[2,2,2,16,1024]{4,3,2,1,0:T(8,128)(2,1)S(1)} %get-tuple-element.37), channel_id=1, source_target_pairs={{0,14},{1,3},{2,0},{3,5},{4,2},{5,7},{6,4},{7,9},{8,6},{9,11},{10,... | collective-permute-start | bytes 786440 | tf_op jit(solution)/shard_map/ppermute | solution.py:220
  74.7 11.0 %collective-permute-start.7 = (bf16[1,2,2,16,1024]{4,3,2,1,0:T(8,128)(2,1)S(1)}, bf16[1,2,2,16,1024]{4,3,2,1,0:T(8,128)(2,1)S(1)}, u32[]{:S(2)}, u32[]{:S(2)}) collective-permute-start(bf16[1,2,2,16,1024]{4,3,2,1,0:T(8,128)(2,1)S(1)} %get-tuple-element.38), channel_id=1, source_target_pairs={{0,4},{1,13},{2,6},{3,15},{4,8},{5,1},{6,10},{7,3},{8,12},{9,5},{1... | collective-permute-start | bytes 393224 | tf_op jit(solution)/shard_map/ppermute | solution.py:220
  78.8 7.9 %collective-permute-start.8 = (bf16[2,2,16,1024]{3,2,1,0:T(8,128)(2,1)S(1)}, bf16[2,2,16,1024]{3,2,1,0:T(8,128)(2,1)S(1)}, u32[]{:S(2)}, u32[]{:S(2)}) collective-permute-start(bf16[2,2,16,1024]{3,2,1,0:T(8,128)(2,1)S(1)} %fusion.2), channel_id=1, source_target_pairs={{0,6},{1,11},{2,8},{3,13},{4,10},{5,15},{6,12},{7,1},{8,14},{9,3},... | collective-permute-start | bytes 393224 | tf_op jit(solution)/shard_map/ppermute | solution.py:220
  83.3 9.3 %collective-permute-start.9 = (bf16[2,2,16,1024]{3,2,1,0:T(8,128)(2,1)S(1)}, bf16[2,2,16,1024]{3,2,1,0:T(8,128)(2,1)S(1)}, u32[]{:S(2)}, u32[]{:S(2)}) collective-permute-start(bf16[2,2,16,1024]{3,2,1,0:T(8,128)(2,1)S(1)} %fusion.3), channel_id=1, source_target_pairs={{0,12},{1,5},{2,14},{3,7},{4,0},{5,9},{6,2},{7,11},{8,4},{9,13},{1... | collective-permute-start | bytes 393224 | tf_op jit(solution)/shard_map/ppermute | solution.py:220

commit v8 on v7

--- a/solution.py
+++ b/solution.py
@@ -212,16 +212,16 @@
     kept, early = second_dot(place, near[0], masked, kept, early)
     early = lax.ppermute(early, "rep", swap)
     late = lax.ppermute(away_dot(place, near[1], near[2], masked), "rep", swap)
-    groups = ((-1, -4), (1, 3), (-2,), (-3,), (2,), (0,))
+    groups = ((1, 3), (-1, -4), (-2,), (2,), (-3,), (0,))
     late_kept, *parts = kept_dot(place, groups, near[1], near[2], masked, kept, early)
-    down, up, two_down, three_down, two_up, own = late_share(place, groups, late_kept, late, parts)
+    up, down, two_down, two_up, three_down, own = late_share(place, groups, late_kept, late, parts)
 
     def along(step, part):
         return lax.ppermute(part, ("red", "rep"), red_step(step))
 
-    down, up, two_down = along(-1, down), along(1, up), along(-2, two_down)
+    up, down, two_down = along(1, up), along(-1, down), along(-2, two_down)
+    two_up = along(2, added(two_up[0], up[1]))
     three_down = along(-3, added(three_down[0], down[1]))
-    two_up = along(2, added(two_up[0], up[1]))
     return added(own[0], down[0], up[0], two_down[0], three_down, two_up).reshape(-1, cols)
 
 

time: 94.1 us -> 94.1 us (level)
  no operation moved by 1% of the time
where the time goes in v8:
time: 94.1 us; the launch traced here: 93.4 us
  blocking collectives  39.6 us (42%)
  starting transfers between devices  36.4 us (39%)
  waiting for transfers between devices  7.11 us (8%)
  Pallas kernels  6.1 us (6%)
  local copies, waits for them, and re-layouts  3.08 us (3%)
    all_to_all x1, blocking collectives, per_device(): lax.all_to_all(copies, ('owner', 'rep'), 0, 0, axis_index_groups=far_grou...  39.6 us
    ppermute x5, starting transfers between devices, along(): return lax.ppermute(part, ('red', 'rep'), red_step(step))  18.7 us
    ppermute x3, starting transfers between devices, per_device(): lax.ppermute(mine, ('owner', 'rep'), near_pairs(dz, dx))  10.8 us
    ppermute x5, waiting for transfers between devices, along(): return lax.ppermute(part, ('red', 'rep'), red_step(step))  6.95 us
    ppermute x1, starting transfers between devices, per_device(): late = lax.ppermute(away_dot(place, near[1], near[2], masked), 'rep', swap)  3.71 us
    ppermute x1, starting transfers between devices, per_device(): early = lax.ppermute(early, 'rep', swap)  3.16 us
    unnamed x4, local copies, waits for them, and re-layouts  2.28 us
  transfers between devices with their start and end apart: 10, of which 3 were waited for; matrix products, arithmetic and copies ran while one was open for 0% of the time, Pallas kernels for 6%

profile of v8, /device:TPU:1, one launch (start us, length us, event | category | flops | bytes accessed | tf_op | source)
XLA Modules:
  0.0 93.4 jit_solution(6824869214824795118)
XLA Ops:
  0.0 0.8 broadcast_in_dim.2
  0.8 39.6 %all_to_all.5 = bf16[16,16,1024]{2,1,0:T(8,128)(2,1)S(1)} all-to-all(bf16[16,16,1024]{2,1,0:T(8,128)(2,1)S(1)} %broadcast_in_dim.2), channel_id=1, replica_groups={{0,32,64,96,256,288,320,352,512,544,576,608,768,800,832,864},{16,48,80,..., dimensions={0} | all-to-all | bytes 1048576 | tf_op jit(solution)/shard_map/all_to_all | solution.py:207
  40.5 1.9 %collective-permute-start.2 = (bf16[4,2,2,16,1024]{4,3,2,1,0:T(8,128)(2,1)S(1)}, bf16[4,2,2,16,1024]{4,3,2,1,0:T(8,128)(2,1)S(1)}, u32[]{:S(2)}, u32[]{:S(2)}) collective-permute-start(bf16[4,2,2,16,1024]{4,3,2,1,0:T(8,128)(2,1)S(1)} %bitcast.16), channel_id=1, source_target_pairs={{0,144},{1,1009},{16,128},{17,929},{32,176},{33,913},{48,160},{49,... | collective-permute-start | bytes 1572872 | tf_op jit(solution)/shard_map/ppermute | solution.py:209
  42.4 4.4 %collective-permute-start = (bf16[4,2,2,16,1024]{4,3,2,1,0:T(8,128)(2,1)S(1)}, bf16[4,2,2,16,1024]{4,3,2,1,0:T(8,128)(2,1)S(1)}, u32[]{:S(2)}, u32[]{:S(2)}) collective-permute-start(bf16[4,2,2,16,1024]{4,3,2,1,0:T(8,128)(2,1)S(1)} %bitcast.17), channel_id=1, source_target_pairs={{0,128},{1,897},{16,144},{17,913},{32,160},{33,929},{48,176},{49,9... | collective-permute-start | bytes 1572872 | tf_op jit(solution)/shard_map/ppermute | solution.py:209
  46.8 4.4 %collective-permute-start.1 = (bf16[4,2,2,16,1024]{4,3,2,1,0:T(8,128)(2,1)S(1)}, bf16[4,2,2,16,1024]{4,3,2,1,0:T(8,128)(2,1)S(1)}, u32[]{:S(2)}, u32[]{:S(2)}) collective-permute-start(bf16[4,2,2,16,1024]{4,3,2,1,0:T(8,128)(2,1)S(1)} %bitcast.18), channel_id=1, source_target_pairs={{0,16},{1,113},{16,0},{17,33},{32,48},{33,17},{48,32},{49,65},{64,... | collective-permute-start | bytes 1572872 | tf_op jit(solution)/shard_map/ppermute | solution.py:209
  51.3 0.1 pad_add_fusion.place_ref
  51.4 0.0 copy-start
  51.4 1.6 %copy-done = bf16[1024,1024]{1,0:T(8,128)(2,1)S(1)} copy-done((bf16[1024,1024]{1,0:T(8,128)(2,1)S(1)}, bf16[1024,1024]{1,0:T(8,128)(2,1)}, u32[]{:S(2)}) %copy-start) | copy-done | bytes 2097176
  52.9 0.0 copy-start.1
  52.9 0.7 copy-done.1
  53.6 1.6 %shard_map.37 = (bf16[2,4,2,16,1024]{4,3,2,1,0:T(8,128)(2,1)S(1)}, bf16[2,4,2,16,1024]{4,3,2,1,0:T(8,128)(2,1)S(1)}, bf16[1024,1024]{1,0:T(8,128)(2,1)S(1)}) custom-call(s32[4]{0:T(128)S(1)} %pad_add_fusion.place_ref, s32[8,8]{1,0:T(8,128)S(1)} %copy-done.1, bf16[1024,1024]{1,0:T(8,128)(2,1)S(1)} %copy-done, bf16[4,2,2,16,1024]{4,3,2,1,0:T(8,128)(2,1)S(1)} %bitcast.19), custom_call_target="tpu_custom_call" | custom-call | flops 536870912 | bytes 4718592 | tf_op jit(solution)/shard_map/pallas_call | solution.py:86
  55.2 0.0 collective-permute-done.2.rows_ref
  55.2 1.3 %shard_map.38 = (bf16[2,4,2,16,1024]{4,3,2,1,0:T(8,128)(2,1)S(1)}, bf16[2,4,2,16,1024]{4,3,2,1,0:T(8,128)(2,1)S(1)}) custom-call(s32[4]{0:T(128)S(1)} %pad_add_fusion.place_ref, bf16[4,2,2,16,1024]{4,3,2,1,0:T(8,128)(2,1)S(1)} %collective-permute-done.2.rows_ref, ...), custom_call_target="tpu_custom_call", output_to_operand_aliasing={{0}: (3, {}), {1}: (4, {})} | custom-call | flops 536870912 | bytes 2621440 | tf_op jit(solution)/shard_map/pallas_call | solution.py:108
  56.5 3.2 %collective-permute-start.3 = (bf16[2,4,2,16,1024]{4,3,2,1,0:T(8,128)(2,1)S(1)}, bf16[2,4,2,16,1024]{4,3,2,1,0:T(8,128)(2,1)S(1)}, u32[]{:S(2)}, u32[]{:S(2)}) collective-permute-start(bf16[2,4,2,16,1024]{4,3,2,1,0:T(8,128)(2,1)S(1)} %get-tuple-element.27), channel_id=1, source_target_pairs={{0,1},{1,0},{2,3},{3,2},{4,5},{5,4},{6,7},{7,6},{8,9},{9,8},{10,11... | collective-permute-start | bytes 1572872 | tf_op jit(solution)/shard_map/ppermute | solution.py:213
  59.6 0.0 collective-permute-done.side_ref
  59.7 0.0 collective-permute-done.1.corner_ref
  59.7 1.3 %shard_map.40 = bf16[2,4,2,16,1024]{4,3,2,1,0:T(8,128)(2,1)S(1)} custom-call(s32[4]{0:T(128)S(1)} %pad_add_fusion.place_ref, bf16[4,2,2,16,1024]{4,3,2,1,0:T(8,128)(2,1)S(1)} %collective-permute-done.side_ref, bf16[4,2,2,16,1024]{4,3,2,1,0:T(8,128)(2,1)S(1)} %collective-permute-done.1.corner_ref, bf16[1024,1024]{1,0:T(8,128)(2,1)S(1)} %get-tuple-element.23.masked_ref), custom_call_target="tpu_custom_call" | custom-call | flops 536870912 | bytes 2621440 | tf_op jit(solution)/shard_map/pallas_call | solution.py:135
  60.9 3.7 %collective-permute-start.4 = (bf16[2,4,2,16,1024]{4,3,2,1,0:T(8,128)(2,1)S(1)}, bf16[2,4,2,16,1024]{4,3,2,1,0:T(8,128)(2,1)S(1)}, u32[]{:S(2)}, u32[]{:S(2)}) collective-permute-start(bf16[2,4,2,16,1024]{4,3,2,1,0:T(8,128)(2,1)S(1)} %shard_map.40), channel_id=1, source_target_pairs={{0,1},{1,0},{2,3},{3,2},{4,5},{5,4},{6,7},{7,6},{8,9},{9,8},{10,11... | collective-permute-start | bytes 1572872 | tf_op jit(solution)/shard_map/ppermute | solution.py:214
  64.7 0.0 collective-permute-done.3.arrived_ref
  64.7 1.3 %shard_map.39 = (bf16[2,4,2,16,1024]{4,3,2,1,0:T(8,128)(2,1)S(1)}, bf16[2,2,2,16,1024]{4,3,2,1,0:T(8,128)(2,1)S(1)}, bf16[2,2,2,16,1024]{4,3,2,1,0:T(8,128)(2,1)...) custom-call(s32[4]{0:T(128)S(1)} %pad_add_fusion.place_ref, ...), custom_call_target="tpu_custom_call" | custom-call | flops 536870912 | bytes 2621440 | tf_op jit(solution)/shard_map/pallas_call | solution.py:167
  66.0 0.1 collective-permute-done.4.arrived_ref
  66.2 0.7 shard_map.41
  66.8 5.9 %collective-permute-start.5 = (bf16[2,2,2,16,1024]{4,3,2,1,0:T(8,128)(2,1)S(1)}, bf16[2,2,2,16,1024]{4,3,2,1,0:T(8,128)(2,1)S(1)}, u32[]{:S(2)}, u32[]{:S(2)}) collective-permute-start(bf16[2,2,2,16,1024]{4,3,2,1,0:T(8,128)(2,1)S(1)} %get-tuple-element.36), channel_id=1, source_target_pairs={{0,2},{1,15},{2,4},{3,1},{4,6},{5,3},{6,8},{7,5},{8,10},{9,7},{10,... | collective-permute-start | bytes 786440 | tf_op jit(solution)/shard_map/ppermute | solution.py:220
  72.7 1.9 %collective-permute-start.6 = (bf16[2,2,2,16,1024]{4,3,2,1,0:T(8,128)(2,1)S(1)}, bf16[2,2,2,16,1024]{4,3,2,1,0:T(8,128)(2,1)S(1)}, u32[]{:S(2)}, u32[]{:S(2)}) collective-permute-start(bf16[2,2,2,16,1024]{4,3,2,1,0:T(8,128)(2,1)S(1)} %get-tuple-element.37), channel_id=1, source_target_pairs={{0,14},{1,3},{2,0},{3,5},{4,2},{5,7},{6,4},{7,9},{8,6},{9,11},{10,... | collective-permute-start | bytes 786440 | tf_op jit(solution)/shard_map/ppermute | solution.py:220
  74.7 4.0 %collective-permute-start.7 = (bf16[1,2,2,16,1024]{4,3,2,1,0:T(8,128)(2,1)S(1)}, bf16[1,2,2,16,1024]{4,3,2,1,0:T(8,128)(2,1)S(1)}, u32[]{:S(2)}, u32[]{:S(2)}) collective-permute-start(bf16[1,2,2,16,1024]{4,3,2,1,0:T(8,128)(2,1)S(1)} %get-tuple-element.38), channel_id=1, source_target_pairs={{0,4},{1,13},{2,6},{3,15},{4,8},{5,1},{6,10},{7,3},{8,12},{9,5},{1... | collective-permute-start | bytes 393224 | tf_op jit(solution)/shard_map/ppermute | solution.py:220
  78.7 0.0 collective-permute-done.5
  78.8 4.5 %collective-permute-start.8 = (bf16[2,2,16,1024]{3,2,1,0:T(8,128)(2,1)S(1)}, bf16[2,2,16,1024]{3,2,1,0:T(8,128)(2,1)S(1)}, u32[]{:S(2)}, u32[]{:S(2)}) collective-permute-start(bf16[2,2,16,1024]{3,2,1,0:T(8,128)(2,1)S(1)} %fusion.2), channel_id=1, source_target_pairs={{0,6},{1,11},{2,8},{3,13},{4,10},{5,15},{6,12},{7,1},{8,14},{9,3},... | collective-permute-start | bytes 393224 | tf_op jit(solution)/shard_map/ppermute | solution.py:220
  83.3 0.0 collective-permute-done.6
  83.3 2.3 %collective-permute-start.9 = (bf16[2,2,16,1024]{3,2,1,0:T(8,128)(2,1)S(1)}, bf16[2,2,16,1024]{3,2,1,0:T(8,128)(2,1)S(1)}, u32[]{:S(2)}, u32[]{:S(2)}) collective-permute-start(bf16[2,2,16,1024]{3,2,1,0:T(8,128)(2,1)S(1)} %fusion.3), channel_id=1, source_target_pairs={{0,12},{1,5},{2,14},{3,7},{4,0},{5,9},{6,2},{7,11},{8,4},{9,13},{1... | collective-permute-start | bytes 393224 | tf_op jit(solution)/shard_map/ppermute | solution.py:220
  85.7 0.0 collective-permute-done.7
  85.7 0.9 collective-permute-done.8
  86.6 6.0 %collective-permute-done.9 = bf16[2,2,16,1024]{3,2,1,0:T(8,128)(2,1)S(1)} collective-permute-done((bf16[2,2,16,1024]{3,2,1,0:T(8,128)(2,1)S(1)}, bf16[2,2,16,1024]{3,2,1,0:T(8,128)(2,1)S(1)}, u32[]{:S(2)}, u32[]{:S(2)}) %collective-permute-start.9) | collective-permute-done | bytes 131104 | tf_op jit(solution)/shard_map/ppermute | solution.py:220
  92.6 0.8 fusion.1
  (2 shorter events, 0.1 us)
Async XLA Ops:
  40.5 14.7 %collective-permute-start.2 = (bf16[4,2,2,16,1024]{4,3,2,1,0:T(8,128)(2,1)S(1)}, bf16[4,2,2,16,1024]{4,3,2,1,0:T(8,128)(2,1)S(1)}, u32[]{:S(2)}, u32[]{:S(2)}) collective-permute-start(bf16[4,2,2,16,1024]{4,3,2,1,0:T(8,128)(2,1)S(1)} %bitcast.16), channel_id=1, source_target_pairs={{0,144},{1,1009},{16,128},{17,929},{32,176},{33,913},{48,160},{49,... | collective-permute-start | bytes 1572872 | tf_op jit(solution)/shard_map/ppermute | solution.py:209
  42.4 17.3 %collective-permute-start = (bf16[4,2,2,16,1024]{4,3,2,1,0:T(8,128)(2,1)S(1)}, bf16[4,2,2,16,1024]{4,3,2,1,0:T(8,128)(2,1)S(1)}, u32[]{:S(2)}, u32[]{:S(2)}) collective-permute-start(bf16[4,2,2,16,1024]{4,3,2,1,0:T(8,128)(2,1)S(1)} %bitcast.17), channel_id=1, source_target_pairs={{0,128},{1,897},{16,144},{17,913},{32,160},{33,929},{48,176},{49,9... | collective-permute-start | bytes 1572872 | tf_op jit(solution)/shard_map/ppermute | solution.py:209
  46.8 12.8 %collective-permute-start.1 = (bf16[4,2,2,16,1024]{4,3,2,1,0:T(8,128)(2,1)S(1)}, bf16[4,2,2,16,1024]{4,3,2,1,0:T(8,128)(2,1)S(1)}, u32[]{:S(2)}, u32[]{:S(2)}) collective-permute-start(bf16[4,2,2,16,1024]{4,3,2,1,0:T(8,128)(2,1)S(1)} %bitcast.18), channel_id=1, source_target_pairs={{0,16},{1,113},{16,0},{17,33},{32,48},{33,17},{48,32},{49,65},{64,... | collective-permute-start | bytes 1572872 | tf_op jit(solution)/shard_map/ppermute | solution.py:209
  51.4 1.6 %copy-start = (bf16[1024,1024]{1,0:T(8,128)(2,1)S(1)}, bf16[1024,1024]{1,0:T(8,128)(2,1)}, u32[]{:S(2)}) copy-start(bf16[1024,1024]{1,0:T(8,128)(2,1)} %ints_ref.1) | copy-start | bytes 6291460
  52.9 0.7 copy-start.1
  56.5 8.2 %collective-permute-start.3 = (bf16[2,4,2,16,1024]{4,3,2,1,0:T(8,128)(2,1)S(1)}, bf16[2,4,2,16,1024]{4,3,2,1,0:T(8,128)(2,1)S(1)}, u32[]{:S(2)}, u32[]{:S(2)}) collective-permute-start(bf16[2,4,2,16,1024]{4,3,2,1,0:T(8,128)(2,1)S(1)} %get-tuple-element.27), channel_id=1, source_target_pairs={{0,1},{1,0},{2,3},{3,2},{4,5},{5,4},{6,7},{7,6},{8,9},{9,8},{10,11... | collective-permute-start | bytes 1572872 | tf_op jit(solution)/shard_map/ppermute | solution.py:213
  60.9 5.2 %collective-permute-start.4 = (bf16[2,4,2,16,1024]{4,3,2,1,0:T(8,128)(2,1)S(1)}, bf16[2,4,2,16,1024]{4,3,2,1,0:T(8,128)(2,1)S(1)}, u32[]{:S(2)}, u32[]{:S(2)}) collective-permute-start(bf16[2,4,2,16,1024]{4,3,2,1,0:T(8,128)(2,1)S(1)} %shard_map.40), channel_id=1, source_target_pairs={{0,1},{1,0},{2,3},{3,2},{4,5},{5,4},{6,7},{7,6},{8,9},{9,8},{10,11... | collective-permute-start | bytes 1572872 | tf_op jit(solution)/shard_map/ppermute | solution.py:214
  66.8 11.9 %collective-permute-start.5 = (bf16[2,2,2,16,1024]{4,3,2,1,0:T(8,128)(2,1)S(1)}, bf16[2,2,2,16,1024]{4,3,2,1,0:T(8,128)(2,1)S(1)}, u32[]{:S(2)}, u32[]{:S(2)}) collective-permute-start(bf16[2,2,2,16,1024]{4,3,2,1,0:T(8,128)(2,1)S(1)} %get-tuple-element.36), channel_id=1, source_target_pairs={{0,2},{1,15},{2,4},{3,1},{4,6},{5,3},{6,8},{7,5},{8,10},{9,7},{10,... | collective-permute-start | bytes 786440 | tf_op jit(solution)/shard_map/ppermute | solution.py:220
  72.7 10.6 %collective-permute-start.6 = (bf16[2,2,2,16,1024]{4,3,2,1,0:T(8,128)(2,1)S(1)}, bf16[2,2,2,16,1024]{4,3,2,1,0:T(8,128)(2,1)S(1)}, u32[]{:S(2)}, u32[]{:S(2)}) collective-permute-start(bf16[2,2,2,16,1024]{4,3,2,1,0:T(8,128)(2,1)S(1)} %get-tuple-element.37), channel_id=1, source_target_pairs={{0,14},{1,3},{2,0},{3,5},{4,2},{5,7},{6,4},{7,9},{8,6},{9,11},{10,... | collective-permute-start | bytes 786440 | tf_op jit(solution)/shard_map/ppermute | solution.py:220
  74.7 11.0 %collective-permute-start.7 = (bf16[1,2,2,16,1024]{4,3,2,1,0:T(8,128)(2,1)S(1)}, bf16[1,2,2,16,1024]{4,3,2,1,0:T(8,128)(2,1)S(1)}, u32[]{:S(2)}, u32[]{:S(2)}) collective-permute-start(bf16[1,2,2,16,1024]{4,3,2,1,0:T(8,128)(2,1)S(1)} %get-tuple-element.38), channel_id=1, source_target_pairs={{0,4},{1,13},{2,6},{3,15},{4,8},{5,1},{6,10},{7,3},{8,12},{9,5},{1... | collective-permute-start | bytes 393224 | tf_op jit(solution)/shard_map/ppermute | solution.py:220
  78.8 7.9 %collective-permute-start.8 = (bf16[2,2,16,1024]{3,2,1,0:T(8,128)(2,1)S(1)}, bf16[2,2,16,1024]{3,2,1,0:T(8,128)(2,1)S(1)}, u32[]{:S(2)}, u32[]{:S(2)}) collective-permute-start(bf16[2,2,16,1024]{3,2,1,0:T(8,128)(2,1)S(1)} %fusion.2), channel_id=1, source_target_pairs={{0,6},{1,11},{2,8},{3,13},{4,10},{5,15},{6,12},{7,1},{8,14},{9,3},... | collective-permute-start | bytes 393224 | tf_op jit(solution)/shard_map/ppermute | solution.py:220
  83.3 9.3 %collective-permute-start.9 = (bf16[2,2,16,1024]{3,2,1,0:T(8,128)(2,1)S(1)}, bf16[2,2,16,1024]{3,2,1,0:T(8,128)(2,1)S(1)}, u32[]{:S(2)}, u32[]{:S(2)}) collective-permute-start(bf16[2,2,16,1024]{3,2,1,0:T(8,128)(2,1)S(1)} %fusion.3), channel_id=1, source_target_pairs={{0,12},{1,5},{2,14},{3,7},{4,0},{5,9},{6,2},{7,11},{8,4},{9,13},{1... | collective-permute-start | bytes 393224 | tf_op jit(solution)/shard_map/ppermute | solution.py:220
